TPU v7x, 32 devices: a whole 2x2x4 slice. The times are simulated.
32 devices in a mesh: group: 4 (over y, x), shard: 8 (over z, core).
Axes of the slice: x: 2, y: 2, z: 4, core: 2. Of those that a mesh axis runs over, the one named last changes fastest.
Arguments:
- samples: bfloat16 [4096, 1, 4096], P(('group', 'shard')), may hold values from -6 to 6
- fan_taps: float32 [33, 2048], replicated, may hold values from -1 to 1
- pair_blocks: int32 [128, 2], replicated, may hold values from 0 to 31
- pair_valid: int32 [128], P(('group', 'shard')), may hold values 0 or 1
- coil_offsets: int32 [32], replicated, may hold values from 0 to 63
Outputs:
- correlations: float32 [128, 128, 512], P(('group', 'shard'))
Inputs may be any that keep to these rules, and one draw needn't show every extreme that they name: `pair_blocks`: block indices.
All inputs are finite; a program needn't handle non-finite values. No bound on the sum of `pair_valid` on one device may be relied on, other than what follows from the above.
Results may differ from a plain program's by a relative error of at most 0.0076.
Values may be sent and summed in bfloat16 or wider, within the bound.
No kernel may reach another device: no remote copies, remote signals or barrier semaphores. Data moves between devices by JAX's collectives and lax.ppermute only.
A program may use at most 192 MiB of HBM per device.

v0:
```python
import jax
import jax.numpy as jnp
from jax import lax
from jax.sharding import PartitionSpec as P

HALF = 16
SMOOTH = 64
NLAG = 512


EPSILON = 1e-05


def with_halo(cells, sides, width):
    for axis, dim in sides:
        count = lax.axis_size(axis)
        ends = count - 1
        head = lax.slice_in_dim(cells, 0, width, axis=dim)
        tail = lax.slice_in_dim(cells, cells.shape[dim] - width, cells.shape[dim], axis=dim)
        cells = jnp.concatenate(
            [
                lax.ppermute(tail, axis, [(i, (i + 1) % count) for i in range(ends)]),
                cells,
                lax.ppermute(head, axis, [((i + 1) % count, i) for i in range(ends)]),
            ],
            axis=dim,
        )
    return cells


def forward_tables(length, bin_count):
    split = 1 << length.bit_length() // 2
    coarse_n = (jnp.arange(length // split, dtype=jnp.int32) * split)[:, None]
    fine_n = jnp.arange(split, dtype=jnp.int32)[:, None]
    cols_k = jnp.arange(bin_count, dtype=jnp.int32)[None, :]
    coarse_ph = jnp.mod(coarse_n * cols_k, length).astype(jnp.float32) * (2.0 * jnp.pi / length)
    fine_ph = jnp.mod(fine_n * cols_k, length).astype(jnp.float32) * (2.0 * jnp.pi / length)
    cos_a = jnp.cos(coarse_ph)[:, None, :]
    sin_a = jnp.sin(coarse_ph)[:, None, :]
    cos_b = jnp.cos(fine_ph)[None, :, :]
    sin_b = jnp.sin(fine_ph)[None, :, :]
    cosine = (cos_a * cos_b - sin_a * sin_b).reshape(length, bin_count)
    sine_vals = (sin_a * cos_b + cos_a * sin_b).reshape(length, bin_count)
    scaled = 1.0 / jnp.sqrt(jnp.float32(length))
    return (jnp.concatenate([cosine, -sine_vals], axis=1) * scaled).astype(jnp.bfloat16)


def inverse_tables(length, bin_count, lag_count):
    freq_index = jnp.arange(bin_count, dtype=jnp.int32)[:, None]
    lagged = jnp.arange(lag_count, dtype=jnp.int32)[None, :] - lag_count // 2
    phases = jnp.mod(freq_index * lagged, length).astype(jnp.float32) * (2.0 * jnp.pi / length)
    return jnp.stack([jnp.cos(phases), -jnp.sin(phases)]).astype(jnp.bfloat16)


def box_mean(power_sum):
    bin_count = power_sum.shape[1]
    zero_row = jnp.zeros_like(power_sum[:, :1])
    prefix = jnp.concatenate([zero_row, jnp.cumsum(power_sum, axis=1)], axis=1)
    last_row = prefix[:, bin_count : bin_count + 1]
    first_row = prefix[:, 0:1]
    upper_vals = jnp.concatenate(
        [
            prefix[:, SMOOTH + 1 :],
            jnp.broadcast_to(last_row, (prefix.shape[0], SMOOTH) + prefix.shape[2:]),
        ],
        axis=1,
    )
    lower_vals = jnp.concatenate(
        [
            jnp.broadcast_to(first_row, (prefix.shape[0], SMOOTH + 1) + prefix.shape[2:]),
            prefix[:, 1 : bin_count - SMOOTH],
        ],
        axis=1,
    )
    bins_k = jnp.arange(bin_count, dtype=jnp.int32)
    counts = (
        jnp.minimum(bins_k + SMOOTH, bin_count - 1) - jnp.maximum(bins_k - SMOOTH, 0) + 1
    ).astype(jnp.float32)
    return (upper_vals - lower_vals) / counts[None, :, None]


def whiten(padded, fan_taps):
    width = padded.shape[3] - 2 * HALF
    filtered = jnp.zeros(padded.shape[:3] + (width,), jnp.float32)
    for offset in range(2 * HALF + 1):
        filtered = filtered + fan_taps[offset][None, None, :, None] * padded[
            :, :, :, offset : offset + width
        ].astype(jnp.float32)
    power_sum = filtered[:, 0] * filtered[:, 0] + filtered[:, 1] * filtered[:, 1]
    mean_power = box_mean(power_sum)
    return (filtered * lax.rsqrt(mean_power + EPSILON)[:, None]).astype(jnp.bfloat16)


def body(samples, fan_taps, pair_blocks, pair_valid, coil_offsets):
    block_width = samples.shape[0]
    segments = samples.shape[1]
    length = samples.shape[2]
    bin_count = length // 2
    groups = lax.axis_size("group")
    shards = lax.axis_size("shard")
    devices = groups * shards
    bins_device = bin_count // devices
    forward = forward_tables(length, bin_count)
    spectra = jnp.einsum("cst,tk->skc", samples, forward, preferred_element_type=jnp.float32)
    padded = with_halo(
        spectra.astype(jnp.bfloat16).reshape(segments, 2, bin_count, samples.shape[0]),
        ((("group", "shard"), 3),),
        HALF,
    )
    whitened = whiten(padded, fan_taps)
    banded = lax.all_to_all(whitened, ("group", "shard"), split_axis=2, concat_axis=3, tiled=True)
    first_block = pair_blocks[:, 0]
    second_block = pair_blocks[:, 1]
    blocks = banded.reshape(segments, 2, bins_device, devices, block_width)
    rolled = jnp.roll(blocks, -(block_width // 2), axis=4)
    left_side = jnp.take(blocks, first_block, axis=3)
    right_side = jnp.take(rolled, second_block, axis=3)
    form = "skpc,skpc->kpc"
    real_part = jnp.einsum(
        form, left_side[:, 0], right_side[:, 0], preferred_element_type=jnp.float32
    ) + jnp.einsum(form, left_side[:, 1], right_side[:, 1], preferred_element_type=jnp.float32)
    imag_part = jnp.einsum(
        form, left_side[:, 1], right_side[:, 0], preferred_element_type=jnp.float32
    ) - jnp.einsum(form, left_side[:, 0], right_side[:, 1], preferred_element_type=jnp.float32)
    block_ids = jnp.arange(devices, dtype=jnp.int32)[None, :]
    first_offset = jnp.sum(
        jnp.where(first_block[:, None] == block_ids, coil_offsets[None, :], 0), axis=1
    )
    second_offset = jnp.sum(
        jnp.where(second_block[:, None] == block_ids, coil_offsets[None, :], 0), axis=1
    )
    shift_samples = first_offset - second_offset
    bin_index = lax.axis_index(("group", "shard")) * bins_device + jnp.arange(
        bins_device, dtype=jnp.int32
    )
    phases = jnp.mod(bin_index[:, None] * shift_samples[None, :], length).astype(jnp.float32) * (
        2.0 * jnp.pi / length
    )
    cosine = jnp.cos(phases)[:, :, None]
    sine_values = jnp.sin(phases)[:, :, None]
    cross_spec = jnp.stack(
        [real_part * cosine + imag_part * sine_values, imag_part * cosine - real_part * sine_values]
    ).astype(jnp.bfloat16)
    owned_spec = lax.all_to_all(
        cross_spec, ("group", "shard"), split_axis=2, concat_axis=1, tiled=True
    )
    inverse = inverse_tables(length, bin_count, NLAG)
    correlations = jnp.einsum(
        "rkpc,rkl->pcl", owned_spec, inverse, preferred_element_type=jnp.float32
    )
    weights = pair_valid.astype(jnp.float32) / jnp.sqrt(jnp.float32(bin_count * segments))
    return correlations * weights[:, None, None]


def solution(mesh):
    return jax.shard_map(
        body,
        mesh=mesh,
        in_specs=(P(("group", "shard"), None, None), P(), P(), P(("group", "shard")), P()),
        out_specs=P(("group", "shard"), None, None),
        check_vma=False,
    )
```

profile of v0, /device:TPU:0, one launch (start us, length us, event | category | flops | bytes accessed | tf_op | source)
XLA Modules:
  0.0 276.4 jit_solution(8011809217576113419)
XLA Ops:
  0.0 2.0 fusion.74
  2.1 2.1 fusion.77
  4.2 22.0 %multiply_subtract_fusion = (f32[64,64,2048]{2,1,0:T(8,128)}, f32[64,64,2048]{2,1,0:T(8,128)}) fusion(f32[64,2048]{1,0:T(8,128)S(1)} %get-tuple-element.63, f32[64,2048]{1,0:T(8,128)S(1)} %get-tuple-element.62, f32[64,2048]{1,0:T(8,128)S(1)} %get-tuple-element.64, f32[64,2048]{1,0:T(8,128)S(1)} %get-tuple-element.61), kind=kLoop, calls=%fused_computation.5 | loop fusion | flops 58720256 | bytes 69206016 | tf_op jit(solution)/shard_map/sub | solution.py:42
  26.2 22.9 %fusion.3 = bf16[4096,128]{1,0:T(8,128)(2,1)S(1)} fusion(f32[4096,2048]{1,0:T(8,128)} %bitcast.163, f32[4096,2048]{1,0:T(8,128)} %bitcast.162, bf16[128,1,4096]{2,0,1:T(8,128)(2,1)S(1)} %copy-done), kind=kOutput, calls=%fused_computation.76 | convolution fusion | flops 4345823232 | bytes 69206016 | tf_op jit(solution)/shard_map/cst,tk->skc/dot_general | solution.py:104
  49.5 0.6 copy-done.3
  50.4 1.3 collective-permute-start.1
  52.0 3.2 %collective-permute-start = (bf16[1,2,2048,16]{2,3,1,0:T(8,128)(2,1)S(1)}, bf16[1,2,2048,16]{2,3,1,0:T(8,128)(2,1)S(1)}, u32[]{:S(2)}, u32[]{:S(2)}) collective-permute-start(bf16[1,2,2048,16]{2,3,1,0:T(8,128)(2,1)S(1)} %copy.44), channel_id=1, source_target_pairs={{0,1},{1,2},{2,3},{3,4},{4,5},{5,6},{6,7},{7,8},{8,9},{9,10},{10,1... | collective-permute-start | bytes 393224 | tf_op jit(solution)/shard_map/ppermute | solution.py:22
  55.3 0.8 fusion.93
  56.0 0.7 fusion.94
  57.0 1.3 copy.47
  58.3 1.3 copy.45
  59.8 37.3 %multiply_add_fusion = f32[1,2,2048,128]{3,2,1,0:T(8,128)S(1)} fusion(bf16[1,2,2048,128]{3,2,1,0:T(8,128)(2,1)S(1)} %bitcast.165, bf16[1,2,2048,16]{3,2,1,0:T(8,128)(2,1)} %copy.47, bf16[1,2,2048,16]{3,2,1,0:T(8,128)(2,1)} %copy.45, f32[2048]{0:T(1024)S(1)} %bitcast.202, f32[2048]{0:T(1024)S(1)} %bitcast.203, f32[2048]{0:T(1024)S(1)} %bitcast.172, ...), kind=kLoop, calls=%fused_computation.103 | loop fusion | flops 101711872 | bytes 3678208 | tf_op jit(solution)/shard_map/add | solution.py:86
  97.2 0.6 fusion.60
  97.9 1.3 copy.49
  99.2 1.3 bitcast_add_fusion
  101.2 9.5 %copy.50 = bf16[1,2,2048,128]{3,1,0,2:T(2,128)(2,1)} copy(bf16[1,2,2048,128]{3,2,1,0:T(8,128)(2,1)S(1)} %multiply_convert_fusion) | data formatting | bytes 2097152 | tf_op jit(solution)/shard_map/convert_element_type | solution.py:91
  110.7 11.7 %all-to-all-start = ((bf16[1,2,2048,128]{3,1,0,2:T(2,128)(2,1)}), bf16[1,2,2048,128]{3,1,0,2:T(2,128)(2,1)S(1)}, u32[]{:S(2)}, u32[]{:S(2)}) async-start(bf16[1,2,2048,128]{3,1,0,2:T(2,128)(2,1)} %copy.50), calls=%async_computation | async-start | bytes 2097152 | tf_op jit(solution)/shard_map/all_to_all | solution.py:111
  123.0 26.8 %all-to-all-done = bf16[1,2,2048,128]{3,1,0,2:T(2,128)(2,1)S(1)} async-done(((bf16[1,2,2048,128]{3,1,0,2:T(2,128)(2,1)}), bf16[1,2,2048,128]{3,1,0,2:T(2,128)(2,1)S(1)}, u32[]{:S(2)}, u32[]{:S(2)}) %all-to-all-start) | async-done | bytes 1048608 | tf_op jit(solution)/shard_map/all_to_all | solution.py:111
  149.9 0.5 fusion.91
  150.4 0.6 maximum_bitcast_fusion.6
  151.0 3.1 %gather_fusion.1 = bf16[128,2,64,128]{3,2,1,0:T(8,128)(2,1)} fusion(bf16[2,64,32,128]{3,1,2,0:T(8,128)(2,1)S(1)} %maximum_bitcast_fusion.6, s32[1024]{0:T(1024)S(1)} %pad_clamp_fusion), kind=kCustom, calls=%fused_computation.1.clone | custom fusion | bytes 8389120 | tf_op jit(solution)/shard_map/jit(_take)/gather | solution.py:117
  154.1 4.0 %bitcast_select_fusion = bf16[1,2,64,128,128]{4,2,3,1,0:T(8,128)(2,1)} fusion(bf16[128,2,64,128]{3,2,1,0:T(8,128)(2,1)} %gather_fusion.1, pred[128]{0:T(512)(128)(4,1)S(1)} %get-tuple-element.55), kind=kLoop, calls=%fused_computation.90 | loop fusion | flops 2097152 | bytes 8388736 | tf_op jit(solution)/shard_map/jit(_take)/select_n | solution.py:117
  158.1 3.1 %gather_fusion = bf16[128,2,64,128]{3,2,1,0:T(8,128)(2,1)} fusion(bf16[2,64,32,128]{3,1,2,0:T(8,128)(2,1)S(1)} %bitcast.161, s32[1024]{0:T(1024)S(1)} %pad_clamp_fusion.1), kind=kCustom, calls=%fused_computation.clone | custom fusion | bytes 8389120 | tf_op jit(solution)/shard_map/jit(_take)/gather | solution.py:116
  161.2 2.8 %bitcast_select_fusion.1 = bf16[1,2,64,128,128]{4,2,1,3,0:T(8,128)(2,1)S(1)} fusion(bf16[128,2,64,128]{3,2,1,0:T(8,128)(2,1)} %gather_fusion, pred[128]{0:T(512)(128)(4,1)S(1)} %get-tuple-element.8), kind=kLoop, calls=%fused_computation.91 | loop fusion | flops 2097152 | bytes 8388736 | tf_op jit(solution)/shard_map/jit(_take)/select_n | solution.py:116
  164.0 0.7 copy-done.2
  164.6 2.9 %fusion.20 = (bf16[1,64,128,128]{3,1,2,0:T(8,128)(2,1)S(1)}, bf16[1,64,128,128]{3,1,2,0:T(8,128)(2,1)S(1)}) fusion(f32[64,128]{0,1:T(8,128)S(1)} %get-tuple-element.58, f32[64,128]{0,1:T(8,128)S(1)} %get-tuple-element.57, bf16[1,2,64,128,128]{4,2,3,1,0:T(8,128)(2,1)S(1)} %copy-done.2, bf16[1,2,64,128,128]{4,2,1,3,0:T(8,128)(2,1)S(1)} %bitcast_select_fusion.1), kind=kLoop, calls=%fused_computation.99 | loop fusion | flops 18874368 | bytes 12648448 | tf_op jit(solution)/shard_map/stack | solution.py:141
  168.0 3.0 %copy.57 = bf16[2,64,128,128]{3,1,0,2:T(8,128)(2,1)} copy(bf16[2,64,128,128]{3,1,2,0:T(8,128)(2,1)S(1)} %pad_maximum_fusion) | data formatting | bytes 8388608 | tf_op jit(solution)/shard_map/stack | solution.py:141
  171.0 3.7 %all-to-all-start.1 = ((bf16[2,64,128,128]{3,1,0,2:T(8,128)(2,1)}), bf16[2,64,128,128]{3,1,0,2:T(8,128)(2,1)}, u32[]{:S(2)}, u32[]{:S(2)}) async-start(bf16[2,64,128,128]{3,1,0,2:T(8,128)(2,1)} %copy.57), calls=%async_computation.1 | async-start | bytes 8388608 | tf_op jit(solution)/shard_map/all_to_all | solution.py:144
  174.7 18.2 %cosine_convert_fusion = (bf16[1,2048,512]{2,1,0:T(8,128)(2,1)S(1)}, bf16[1,2048,512]{2,1,0:T(8,128)(2,1)}) fusion(s32[512]{0:T(512)S(1)} %iota_add_fusion.2), kind=kLoop, calls=%fused_computation.93 | loop fusion | flops 17825792 | bytes 4196352 | tf_op jit(solution)/shard_map/convert.12
  192.9 76.9 %all-to-all-done.1 = bf16[2,64,128,128]{3,1,0,2:T(8,128)(2,1)} async-done(((bf16[2,64,128,128]{3,1,0,2:T(8,128)(2,1)}), bf16[2,64,128,128]{3,1,0,2:T(8,128)(2,1)}, u32[]{:S(2)}, u32[]{:S(2)}) %all-to-all-start.1) | async-done | bytes 4194336 | tf_op jit(solution)/shard_map/all_to_all | solution.py:144
  269.8 3.3 %copy.59 = bf16[2,32,64,4,128]{4,2,1,3,0:T(8,128)(2,1)S(1)} copy(bf16[2,32,64,4,128]{4,2,0,3,1:T(8,128)(2,1)} %bitcast.67) | data formatting | bytes 8388608 | tf_op jit(solution)/shard_map/all_to_all | solution.py:144
  273.1 3.3 %fusion.23 = f32[4,128,512]{2,1,0:T(8,128)} fusion(bf16[2,2048,4,128]{3,1,2,0:T(8,128)(2,1)S(1)} %bitcast.170, bf16[1,2048,512]{2,1,0:T(8,128)(2,1)S(1)} %copy-done.5, bf16[1,2048,512]{2,1,0:T(8,128)(2,1)S(1)} %get-tuple-element.53, f32[4]{0:T(128)S(1)} %convert_multiply_fusion.4), kind=kOutput, calls=%fused_computation.105 | convolution fusion | flops 2149842944 | bytes 9437200 | tf_op jit(solution)/shard_map/rkpc,rkl->pcl/dot_general | solution.py:148
  (93 shorter events, 3.0 us)
Async XLA Ops:
  0.0 26.2 %copy-start = (bf16[128,1,4096]{2,0,1:T(8,128)(2,1)S(1)}, bf16[128,1,4096]{2,0,1:T(8,128)(2,1)}, u32[]{:S(2)}) copy-start(bf16[128,1,4096]{2,0,1:T(8,128)(2,1)} %param.7) | copy-start | bytes 3145732
  50.1 5.2 %copy-start.6 = (f32[33,2048]{1,0:T(8,128)S(1)}, f32[33,2048]{1,0:T(8,128)}, u32[]{:S(2)}) copy-start(f32[33,2048]{1,0:T(8,128)} %param.8) | copy-start | bytes 811012
  50.4 6.5 %collective-permute-start.1 = (bf16[1,2,2048,16]{2,3,1,0:T(8,128)(2,1)S(1)}, bf16[1,2,2048,16]{2,3,1,0:T(8,128)(2,1)S(1)}, u32[]{:S(2)}, u32[]{:S(2)}) collective-permute-start(bf16[1,2,2048,16]{2,3,1,0:T(8,128)(2,1)S(1)} %copy.46), channel_id=1, source_target_pairs={{1,0},{2,1},{3,2},{4,3},{5,4},{6,5},{7,6},{8,7},{9,8},{10,9},{11,1... | collective-permute-start | bytes 393224 | tf_op jit(solution)/shard_map/ppermute | solution.py:24
  51.7 7.9 %copy-start.4 = (bf16[4096,128]{1,0:T(8,128)(2,1)S(1)}, bf16[4096,128]{1,0:T(8,128)(2,1)}, u32[]{:S(2)}) copy-start(bf16[4096,128]{1,0:T(8,128)(2,1)} %copy-done.3) | copy-start | bytes 3145732
  52.0 6.3 %collective-permute-start = (bf16[1,2,2048,16]{2,3,1,0:T(8,128)(2,1)S(1)}, bf16[1,2,2048,16]{2,3,1,0:T(8,128)(2,1)S(1)}, u32[]{:S(2)}, u32[]{:S(2)}) collective-permute-start(bf16[1,2,2048,16]{2,3,1,0:T(8,128)(2,1)S(1)} %copy.44), channel_id=1, source_target_pairs={{0,1},{1,2},{2,3},{3,4},{4,5},{5,6},{6,7},{7,8},{8,9},{9,10},{10,1... | collective-permute-start | bytes 393224 | tf_op jit(solution)/shard_map/ppermute | solution.py:22
  56.7 2.9 %copy-start.7 = (f32[1,2048]{1,0:T(1,128)S(1)}, f32[1,2048]{1,0:T(1,128)}, u32[]{:S(2)}) copy-start(f32[1,2048]{1,0:T(1,128)} %get-tuple-element.30) | copy-start | bytes 24580
  56.7 2.9 %copy-start.8 = (f32[1,2048]{1,0:T(1,128)S(1)}, f32[1,2048]{1,0:T(1,128)}, u32[]{:S(2)}) copy-start(f32[1,2048]{1,0:T(1,128)} %get-tuple-element.31) | copy-start | bytes 24580
  56.7 2.9 %copy-start.9 = (f32[1,2048]{1,0:T(1,128)S(1)}, f32[1,2048]{1,0:T(1,128)}, u32[]{:S(2)}) copy-start(f32[1,2048]{1,0:T(1,128)} %get-tuple-element.32) | copy-start | bytes 24580
  56.7 2.9 %copy-start.10 = (f32[1,2048]{1,0:T(1,128)S(1)}, f32[1,2048]{1,0:T(1,128)}, u32[]{:S(2)}) copy-start(f32[1,2048]{1,0:T(1,128)} %get-tuple-element.33) | copy-start | bytes 24580
  56.7 2.9 %copy-start.11 = (f32[1,2048]{1,0:T(1,128)S(1)}, f32[1,2048]{1,0:T(1,128)}, u32[]{:S(2)}) copy-start(f32[1,2048]{1,0:T(1,128)} %get-tuple-element.34) | copy-start | bytes 24580
  56.7 2.9 %copy-start.12 = (f32[1,2048]{1,0:T(1,128)S(1)}, f32[1,2048]{1,0:T(1,128)}, u32[]{:S(2)}) copy-start(f32[1,2048]{1,0:T(1,128)} %get-tuple-element.35) | copy-start | bytes 24580
  56.8 2.9 %copy-start.13 = (f32[1,2048]{1,0:T(1,128)S(1)}, f32[1,2048]{1,0:T(1,128)}, u32[]{:S(2)}) copy-start(f32[1,2048]{1,0:T(1,128)} %get-tuple-element.36) | copy-start | bytes 24580
  56.8 2.9 %copy-start.14 = (f32[1,2048]{1,0:T(1,128)S(1)}, f32[1,2048]{1,0:T(1,128)}, u32[]{:S(2)}) copy-start(f32[1,2048]{1,0:T(1,128)} %get-tuple-element.37) | copy-start | bytes 24580
  56.8 2.9 %copy-start.15 = (f32[1,2048]{1,0:T(1,128)S(1)}, f32[1,2048]{1,0:T(1,128)}, u32[]{:S(2)}) copy-start(f32[1,2048]{1,0:T(1,128)} %get-tuple-element.38) | copy-start | bytes 24580
  56.8 2.9 %copy-start.16 = (f32[1,2048]{1,0:T(1,128)S(1)}, f32[1,2048]{1,0:T(1,128)}, u32[]{:S(2)}) copy-start(f32[1,2048]{1,0:T(1,128)} %get-tuple-element.39) | copy-start | bytes 24580
  56.8 2.9 %copy-start.17 = (f32[1,2048]{1,0:T(1,128)S(1)}, f32[1,2048]{1,0:T(1,128)}, u32[]{:S(2)}) copy-start(f32[1,2048]{1,0:T(1,128)} %get-tuple-element.40) | copy-start | bytes 24580
  56.8 2.9 %copy-start.18 = (f32[1,2048]{1,0:T(1,128)S(1)}, f32[1,2048]{1,0:T(1,128)}, u32[]{:S(2)}) copy-start(f32[1,2048]{1,0:T(1,128)} %get-tuple-element.41) | copy-start | bytes 24580
  56.8 2.9 %copy-start.19 = (f32[1,2048]{1,0:T(1,128)S(1)}, f32[1,2048]{1,0:T(1,128)}, u32[]{:S(2)}) copy-start(f32[1,2048]{1,0:T(1,128)} %get-tuple-element.42) | copy-start | bytes 24580
  56.8 2.9 %copy-start.20 = (f32[1,2048]{1,0:T(1,128)S(1)}, f32[1,2048]{1,0:T(1,128)}, u32[]{:S(2)}) copy-start(f32[1,2048]{1,0:T(1,128)} %get-tuple-element.43) | copy-start | bytes 24580
  56.8 2.9 %copy-start.21 = (f32[1,2048]{1,0:T(1,128)S(1)}, f32[1,2048]{1,0:T(1,128)}, u32[]{:S(2)}) copy-start(f32[1,2048]{1,0:T(1,128)} %get-tuple-element.44) | copy-start | bytes 24580
  56.8 2.9 %copy-start.22 = (f32[1,2048]{1,0:T(1,128)S(1)}, f32[1,2048]{1,0:T(1,128)}, u32[]{:S(2)}) copy-start(f32[1,2048]{1,0:T(1,128)} %get-tuple-element.45) | copy-start | bytes 24580
  56.9 2.9 %copy-start.23 = (f32[1,2048]{1,0:T(1,128)S(1)}, f32[1,2048]{1,0:T(1,128)}, u32[]{:S(2)}) copy-start(f32[1,2048]{1,0:T(1,128)} %get-tuple-element.46) | copy-start | bytes 24580
  56.9 2.9 %copy-start.24 = (f32[1,2048]{1,0:T(1,128)S(1)}, f32[1,2048]{1,0:T(1,128)}, u32[]{:S(2)}) copy-start(f32[1,2048]{1,0:T(1,128)} %get-tuple-element.47) | copy-start | bytes 24580
  56.9 2.9 %copy-start.25 = (f32[1,2048]{1,0:T(1,128)S(1)}, f32[1,2048]{1,0:T(1,128)}, u32[]{:S(2)}) copy-start(f32[1,2048]{1,0:T(1,128)} %get-tuple-element.48) | copy-start | bytes 24580
  101.2 21.2 %copy-start.30 = (s32[128,2]{0,1:T(2,128)S(1)}, s32[128,2]{0,1:T(2,128)}, u32[]{:S(2)}) copy-start(s32[128,2]{0,1:T(2,128)} %param.9) | copy-start | bytes 3076
  101.2 21.2 %copy-start.31 = (s32[32]{0:T(128)S(1)}, s32[32]{0:T(128)}, u32[]{:S(2)}) copy-start(s32[32]{0:T(128)} %param.11) | copy-start | bytes 388
  110.7 39.1 %all-to-all-start = ((bf16[1,2,2048,128]{3,1,0,2:T(2,128)(2,1)}), bf16[1,2,2048,128]{3,1,0,2:T(2,128)(2,1)S(1)}, u32[]{:S(2)}, u32[]{:S(2)}) async-start(bf16[1,2,2048,128]{3,1,0,2:T(2,128)(2,1)} %copy.50), calls=%async_computation | async-start | bytes 2097152 | tf_op jit(solution)/shard_map/all_to_all | solution.py:111
  161.2 3.4 %copy-start.2 = (bf16[1,2,64,128,128]{4,2,3,1,0:T(8,128)(2,1)S(1)}, bf16[1,2,64,128,128]{4,2,3,1,0:T(8,128)(2,1)}, u32[]{:S(2)}) copy-start(bf16[1,2,64,128,128]{4,2,3,1,0:T(8,128)(2,1)} %bitcast_select_fusion) | copy-start | bytes 12582916
  171.0 3.7 %copy-start.32 = (s32[4]{0:T(128)S(1)}, s32[4]{0:T(128)}, u32[]{:S(2)}) copy-start(s32[4]{0:T(128)} %param.10) | copy-start | bytes 52
  171.0 98.8 %all-to-all-start.1 = ((bf16[2,64,128,128]{3,1,0,2:T(8,128)(2,1)}), bf16[2,64,128,128]{3,1,0,2:T(8,128)(2,1)}, u32[]{:S(2)}, u32[]{:S(2)}) async-start(bf16[2,64,128,128]{3,1,0,2:T(8,128)(2,1)} %copy.57), calls=%async_computation.1 | async-start | bytes 8388608 | tf_op jit(solution)/shard_map/all_to_all | solution.py:144
  269.8 3.3 %copy-start.5 = (bf16[1,2048,512]{2,1,0:T(8,128)(2,1)S(1)}, bf16[1,2048,512]{2,1,0:T(8,128)(2,1)}, u32[]{:S(2)}) copy-start(bf16[1,2048,512]{2,1,0:T(8,128)(2,1)} %get-tuple-element.54) | copy-start | bytes 6291460
  273.1 3.4 %copy-start.1 = (bf16[128,1,4096]{2,0,1:T(8,128)(2,1)S(1)}, bf16[128,1,4096]{2,0,1:T(8,128)(2,1)}, u32[]{:S(2)}) copy-start(bf16[128,1,4096]{2,0,1:T(8,128)(2,1)} %param.7) | copy-start | bytes 3145732
  (5 other events, 12.5 us)
where the time goes:
time: 277 us; the launch traced here: 276 us
  waiting for transfers between devices  104 us (38%)
  other arithmetic  95.3 us (34%)
  local copies, waits for them, and re-layouts  30.5 us (11%)
  matrix products  26.3 us (9%)
  starting transfers between devices  19.9 us (7%)
    all_to_all x1, waiting for transfers between devices, body(): lax.all_to_all(cross_spec, ('group', 'shard'), split_axis=2, concat_axis=...  76.9 us
    add x1, other arithmetic, whiten(): filtered + fan_taps[offset][None, None, :, None] * padded[:, :, :, offset...  37.3 us
    all_to_all x1, waiting for transfers between devices, body(): lax.all_to_all(whitened, ('group', 'shard'), split_axis=2, concat_axis=3,...  26.8 us
    dot_general x1, matrix products, body(): jnp.einsum('cst,tk->skc', samples, forward, preferred_element_type=jnp.fl...  22.9 us
    sub x1, other arithmetic, forward_tables(): cosine = (cos_a * cos_b - sin_a * sin_b).reshape(length, bin_count)  22 us
    another operation x4, other arithmetic  20.1 us
    all_to_all x1, starting transfers between devices, body(): lax.all_to_all(whitened, ('group', 'shard'), split_axis=2, concat_axis=3,...  11.7 us
    convert_element_type x1, local copies, waits for them, and re-layouts, whiten(): (filtered * lax.rsqrt(mean_power + EPSILON)[:, None]).astype(jnp.bfloat16)  9.46 us
  transfers between devices with their start and end apart: 4, of which 2 were waited for; matrix products, arithmetic and copies ran while one was open for 8% of the time, Pallas kernels for 0%

commit v1 on v0

v1 whole, which is shorter than its diff:
```python
import functools

import jax
import jax.numpy as jnp
import ml_dtypes
import numpy as np
from jax import lax
from jax.experimental import pallas as pl
from jax.experimental.pallas import tpu as pltpu
from jax.sharding import PartitionSpec as P

AXES = ("group", "shard")
HALF = 16
SMOOTH = 64
NLAG = 512
EPSILON = 1e-05
RADIX = 16
VMEM_BYTES = 56 * 1024 * 1024
F32 = jnp.float32
BF16 = jnp.bfloat16


def as_bf16(table):
    return table.astype(ml_dtypes.bfloat16)


def forward_constants(length):
    inner = length // RADIX
    n1 = np.arange(inner)
    turns = (np.arange(RADIX)[:, None] * n1[None, :]) * (2.0 * np.pi / length)
    twiddle = np.concatenate([np.cos(turns), np.sin(turns)]).astype(np.float32)
    angle = np.mod(n1[:, None] * np.arange(inner // 2)[None, :], inner) * (2.0 * np.pi / inner)
    cosine, sine = np.cos(angle), np.sin(angle)
    table = np.concatenate(
        [np.concatenate([cosine, -sine], axis=1), np.concatenate([sine, cosine], axis=1)]
    ) / np.sqrt(length)
    high = as_bf16(table)
    low = as_bf16(table - high.astype(np.float64))
    return twiddle, np.concatenate([high, high, low])


def band_constants(bands, width, length):
    place = np.arange(width)
    diagonal = ((width - 1 - 2 * place) / 2.0) ** 2 * np.cos(np.pi * NLAG / length)
    beside = place[1:] * (width - place[1:]) / 2.0
    matrix = np.diag(diagonal) + np.diag(beside, 1) + np.diag(beside, -1)
    vectors = np.linalg.eigh(matrix)[1][:, ::-1]
    upper = vectors[(width + 1) // 2 :]
    vectors = vectors * np.sign(upper[np.argmax(np.abs(upper), axis=0), np.arange(width)])[None, :]
    lags = np.arange(NLAG) - NLAG // 2
    waves = np.exp(2j * np.pi * np.outer(place - (width - 1) / 2.0, lags) / length)
    rank = width
    for fewer in range(4, width, 4):
        basis = vectors[:, :fewer]
        if np.abs(waves - basis @ (basis.T @ waves)).max() < 1e-7:
            rank = fewer
            break
    basis = vectors[:, :rank]
    partner = basis.T @ waves
    centres = width * np.arange(bands) + (width - 1) / 2.0
    carrier = np.exp(2j * np.pi * np.outer(centres, lags) / length)
    whole = carrier[:, None, :] * partner[None, :, :]
    table = np.concatenate([whole.real, -whole.imag], axis=1).reshape(bands * 2 * rank, NLAG)
    return basis, as_bf16(np.ascontiguousarray(table.T))


def projection_constants(basis, bins_device):
    width, rank = basis.shape
    rows = np.zeros((2, rank, width // RADIX, 2, RADIX))
    split = basis.T.reshape(rank, width // RADIX, RADIX)
    rows[0, :, :, 0, :] = split
    rows[1, :, :, 1, :] = split
    return as_bf16(rows.reshape(2 * rank, 2 * width))


def real_dft(values):
    count = len(values)
    if count == 1:
        return [(values[0], None)]
    even, odd = real_dft(values[0::2]), real_dft(values[1::2])
    out = [None] * (count // 2 + 1)
    out[0] = (even[0][0] + odd[0][0], None)
    out[count // 2] = (even[0][0] - odd[0][0], None)
    for k in range(1, count // 4 + 1):
        er, ei = even[k]
        orr, oi = odd[k]
        if 4 * k == count:
            out[k] = (er, -orr)
            continue
        c, s = float(np.cos(2 * np.pi * k / count)), float(np.sin(2 * np.pi * k / count))
        tr = orr * c + oi * s
        ti = oi * c - orr * s
        out[k] = (er + tr, ei + ti)
        out[count // 2 - k] = (er - tr, ti - ei)
    return out


def transform_rows(x_ref, twiddle_ref, z_ref, rows):
    inner = x_ref.shape[1] // RADIX

    def step(i, carry):
        at = pl.multiple_of(i * 16, 16)
        for half in range(inner // 128):
            lane = 128 * half
            values = [
                x_ref[pl.ds(at, 16), inner * j + lane : inner * j + lane + 128].astype(F32)
                for j in range(RADIX)
            ]
            bins = real_dft(values)
            for q in range(RADIX):
                yr, yi = bins[q] if q <= RADIX // 2 else bins[RADIX - q]
                if q > RADIX // 2:
                    yi = -yi
                if q == 0:
                    zr, zi = yr, jnp.zeros_like(yr)
                else:
                    c = twiddle_ref[q : q + 1, lane : lane + 128]
                    s = twiddle_ref[RADIX + q : RADIX + q + 1, lane : lane + 128]
                    if yi is None:
                        zr, zi = yr * c, -yr * s
                    else:
                        zr, zi = yr * c + yi * s, yi * c - yr * s
                where = pl.ds(pl.multiple_of(q * rows + at, 16), 16)
                for part, z in ((0, zr), (1, zi)):
                    high = z.astype(BF16)
                    z_ref[where, part * inner + lane : part * inner + lane + 128] = high
                    low = (z - high.astype(F32)).astype(BF16)
                    start = (2 + part) * inner + lane
                    z_ref[where, start : start + 128] = low
        return carry

    lax.fori_loop(0, rows // 16, step, 0)


def transform_inner(z, table_ref):
    depth = z.shape[1]
    out = jnp.dot(z, table_ref[0:depth, :], preferred_element_type=F32)
    return out + jnp.dot(
        z[:, : depth // 2], table_ref[depth:, :], preferred_element_type=F32
    )


def own_kernel(x_ref, twiddle_ref, table_ref, out_ref, z_ref):
    rows = x_ref.shape[0]
    transform_rows(x_ref, twiddle_ref, z_ref, rows)
    for q in range(RADIX):
        values = transform_inner(z_ref[q * rows : (q + 1) * rows, :], table_ref)
        out_ref[q, 0] = values[:, :128]
        out_ref[q, 1] = values[:, 128:]


def shifted(values, by):
    count = values.shape[1]
    lane = lax.broadcasted_iota(jnp.int32, values.shape, 1)
    inside = (lane + by >= 0) & (lane + by < count)
    return jnp.where(inside, pltpu.roll(values, (-by) % count, 1), 0.0)


def whiten_kernel(
    length, offset_ref, own_ref, left_ref, right_ref, twiddle_ref, table_ref, taps_ref, count_ref, out_ref,
    x_ref, z_ref, halo_ref, line_ref, filtered_ref, power_ref, base_ref, rows_ref,
):
    width = own_ref.shape[2]
    x_ref[0:HALF, :] = left_ref[...]
    x_ref[HALF:, :] = right_ref[...]
    transform_rows(x_ref, twiddle_ref, z_ref, 2 * HALF)
    halo_ref[...] = transform_inner(z_ref[...], table_ref)

    power_ref[0] = jnp.zeros(power_ref.shape[1:], F32)

    def filter_step(q, carry):
        at = pl.multiple_of(q * 2 * HALF, 2 * HALF)
        total = None
        for r in range(2):
            halo = halo_ref[pl.ds(at, 2 * HALF), 128 * r : 128 * r + 128]
            line_ref[r, 0:HALF, :] = halo[:HALF]
            line_ref[r, HALF : HALF + width, :] = own_ref[q, r]
            line_ref[r, HALF + width :, :] = halo[HALF:]
            result = jnp.zeros((width, 128), F32)
            for t in range(2 * HALF + 1):
                result = result + taps_ref[q, t : t + 1, :] * line_ref[r, t : t + width, :]
            filtered_ref[q, r] = result
            total = result * result if total is None else total + result * result
        power_ref[q + 1] = power_ref[q] + total
        return carry

    lax.fori_loop(0, RADIX, filter_step, 0)

    reach = SMOOTH // RADIX
    whole = power_ref[RADIX]
    base = whole
    for by in range(1, reach):
        base = base + (shifted(whole, by) + shifted(whole, -by))
    base_ref[...] = base

    bins = lax.broadcasted_iota(jnp.int32, (RADIX, 128), 1) * RADIX + lax.broadcasted_iota(
        jnp.int32, (RADIX, 128), 0
    )
    phases = lax.rem(bins * offset_ref[0], length).astype(F32) * (2.0 * np.pi / length)
    cosine, sine = jnp.cos(phases), jnp.sin(phases)
    for q in range(RADIX):
        window = (
            base_ref[...]
            + shifted(power_ref[RADIX] - power_ref[q], -reach)
            + shifted(power_ref[q + 1], reach)
        )
        scale = lax.rsqrt(window * count_ref[q : q + 1, :] + EPSILON)
        fr, fi = filtered_ref[q, 0], filtered_ref[q, 1]
        c, s = cosine[q : q + 1, :], sine[q : q + 1, :]
        wr = (fr * c + fi * s) * scale
        wi = (fi * c - fr * s) * scale
        rows_ref[pl.ds(q, 128, stride=2 * RADIX), :] = wr.T
        rows_ref[pl.ds(RADIX + q, 128, stride=2 * RADIX), :] = wi.T
    out_ref[...] = rows_ref[...].astype(BF16)


def pair_kernel(slots, pairs_ref, band_ref, basis_ref, out_ref, left_ref, right_ref, cross_ref):
    blocks = band_ref.shape[0]
    groups = band_ref.shape[1] // (2 * RADIX)
    deep = basis_ref.shape[0]

    def spread(i, carry):
        values = band_ref[i].astype(F32)
        left_ref[i] = values
        right_ref[i] = pltpu.roll(values, 64, 1)
        return carry

    lax.fori_loop(0, blocks, spread, 0)

    def owner(d, carry):
        for j in range(slots):
            a = pairs_ref[d * slots + j, 0]
            b = pairs_ref[d * slots + j, 1]
            for m in range(groups):
                lo, mid, hi = 2 * RADIX * m, 2 * RADIX * m + RADIX, 2 * RADIX * (m + 1)
                lr, li = left_ref[a, lo:mid, :], left_ref[a, mid:hi, :]
                rr, ri = right_ref[b, lo:mid, :], right_ref[b, mid:hi, :]
                cross_ref[lo:mid, 128 * j : 128 * j + 128] = (lr * rr + li * ri).astype(BF16)
                cross_ref[mid:hi, 128 * j : 128 * j + 128] = (li * rr - lr * ri).astype(BF16)
        result = jnp.dot(basis_ref[...], cross_ref[...], preferred_element_type=F32)
        stacked = jnp.concatenate([result[:, 128 * j : 128 * j + 128] for j in range(slots)], axis=0)
        out_ref[d] = stacked.astype(BF16)
        return carry

    lax.fori_loop(0, blocks, owner, 0)


def lag_kernel(slots, scale, valid_ref, parts_ref, table_ref, out_ref, wide_ref):
    bands = parts_ref.shape[0]
    deep = parts_ref.shape[1] // slots

    def gather(b, carry):
        values = parts_ref[b].astype(F32)
        for j in range(slots):
            at = pl.multiple_of(b * deep, 8)
            wide_ref[pl.ds(at, deep), 128 * j : 128 * j + 128] = values[deep * j : deep * (j + 1)]
        return carry

    lax.fori_loop(0, bands, gather, 0)
    result = jnp.dot(table_ref[...], wide_ref[...].astype(BF16), preferred_element_type=F32)
    for j in range(slots):
        weight = valid_ref[j].astype(F32) * scale
        out_ref[j] = result[:, 128 * j : 128 * j + 128].T * weight


def vmem():
    return pl.BlockSpec(memory_space=pltpu.VMEM)


def smem():
    return pl.BlockSpec(memory_space=pltpu.SMEM)


def params():
    return pltpu.CompilerParams(vmem_limit_bytes=VMEM_BYTES)


def body(samples, fan_taps, pair_blocks, pair_valid, coil_offsets):
    width = samples.shape[0]
    length = samples.shape[2]
    bin_count = length // 2
    devices = lax.axis_size("group") * lax.axis_size("shard")
    bins_device = bin_count // devices
    slots = pair_valid.shape[0]
    inner = length // RADIX
    lanes = bin_count // RADIX

    twiddle, table = forward_constants(length)
    basis, lag_table = band_constants(devices, bins_device, length)
    project = projection_constants(basis, bins_device)
    deep = project.shape[0]
    bins_k = np.arange(bin_count)
    counts = np.minimum(bins_k + SMOOTH, bin_count - 1) - np.maximum(bins_k - SMOOTH, 0) + 1
    inverse_count = (1.0 / counts).reshape(lanes, RADIX).T.astype(np.float32)

    x = samples.reshape(width, length)
    ends = devices - 1
    left = lax.ppermute(x[width - HALF :], AXES, [(i, i + 1) for i in range(ends)])
    right = lax.ppermute(x[:HALF], AXES, [(i + 1, i) for i in range(ends)])
    taps = jnp.transpose(fan_taps.reshape(2 * HALF + 1, lanes, RADIX), (2, 0, 1))
    offset = lax.dynamic_slice(coil_offsets, (lax.axis_index(AXES),), (1,))

    own = pl.pallas_call(
        own_kernel,
        out_shape=jax.ShapeDtypeStruct((RADIX, 2, width, lanes), F32),
        in_specs=[vmem()] * 3,
        out_specs=vmem(),
        scratch_shapes=[pltpu.VMEM((RADIX * width, 4 * inner), BF16)],
        compiler_params=params(),
        name="own_spectra",
    )(x, twiddle, table)

    rows = pl.pallas_call(
        functools.partial(whiten_kernel, length),
        out_shape=jax.ShapeDtypeStruct((2 * bin_count, width), BF16),
        in_specs=[smem()] + [vmem()] * 7,
        out_specs=vmem(),
        scratch_shapes=[
            pltpu.VMEM((2 * HALF, length), BF16),
            pltpu.VMEM((RADIX * 2 * HALF, 4 * inner), BF16),
            pltpu.VMEM((RADIX * 2 * HALF, 2 * lanes), F32),
            pltpu.VMEM((2, width + 2 * HALF, lanes), F32),
            pltpu.VMEM((RADIX, 2, width, lanes), F32),
            pltpu.VMEM((RADIX + 1, width, lanes), F32),
            pltpu.VMEM((width, lanes), F32),
            pltpu.VMEM((2 * bin_count, width), F32),
        ],
        compiler_params=params(),
        name="whiten",
    )(offset, own, left, right, twiddle, table, taps, inverse_count)

    band = lax.all_to_all(
        rows.reshape(devices, 2 * bins_device, width), AXES, split_axis=0, concat_axis=0, tiled=True
    )

    parts = pl.pallas_call(
        functools.partial(pair_kernel, slots),
        out_shape=jax.ShapeDtypeStruct((devices, slots * deep, width), BF16),
        in_specs=[smem(), vmem(), vmem()],
        out_specs=vmem(),
        scratch_shapes=[
            pltpu.VMEM((devices, 2 * bins_device, width), F32),
            pltpu.VMEM((devices, 2 * bins_device, width), F32),
            pltpu.VMEM((2 * bins_device, slots * width), BF16),
        ],
        compiler_params=params(),
        name="pair_products",
    )(pair_blocks, band, project)

    owned = lax.all_to_all(parts, AXES, split_axis=0, concat_axis=0, tiled=True)

    return pl.pallas_call(
        functools.partial(lag_kernel, slots, float(1.0 / np.sqrt(bin_count * samples.shape[1]))),
        out_shape=jax.ShapeDtypeStruct((slots, width, NLAG), F32),
        in_specs=[smem(), vmem(), vmem()],
        out_specs=vmem(),
        scratch_shapes=[pltpu.VMEM((devices * deep, slots * width), F32)],
        compiler_params=params(),
        name="lags",
    )(pair_valid, owned, lag_table)


def solution(mesh):
    return jax.shard_map(
        body,
        mesh=mesh,
        in_specs=(P(AXES, None, None), P(), P(), P(AXES), P()),
        out_specs=P(AXES, None, None),
        check_vma=False,
    )
```

time: 277 us -> 117 us (0.42)
  other arithmetic: 95.3 us -> 0 us
  waiting for transfers between devices: 104 us -> 26.9 us
  blocking collectives: 0 us -> 36.6 us
  Pallas kernels: 0 us -> 33.5 us
  matrix products: 26.3 us -> 0 us
  local copies, waits for them, and re-layouts: 30.5 us -> 6.42 us
  starting transfers between devices: 19.9 us -> 12.9 us
    all_to_all x2 -> x1, waiting for transfers between devices: 104 us -> 26.8 us  [body(): lax.all_to_all(rows.reshape(devices, 2 * bins_device, width), AXES, split...]
    add x3 -> x0, other arithmetic: 37.4 us -> none  [the longest x1 37.3 us: whiten(): filtered + fan_taps[offset][None, None, :, None] * padded[:, :, :, offset...]
    all_to_all x0 -> x1, blocking collectives: none -> 36.6 us  [body(): owned = lax.all_to_all(parts, AXES, split_axis=0, concat_axis=0, tiled=True)]
    pallas_call x0 -> x4, Pallas kernels: none -> 33.5 us  [the longest x1 11.8 us: body(): pl.pallas_call(functools.partial(whiten_kernel, length), out_shape=jax.Sh...]
    dot_general x2 -> x0, matrix products: 26.3 us -> none  [the longest x1 22.9 us: body(): jnp.einsum('cst,tk->skc', samples, forward, preferred_element_type=jnp.fl...]
    another operation x7 -> x0, other arithmetic: 24 us -> none
    sub x3 -> x0, other arithmetic: 22 us -> none  [the longest x1 22 us: forward_tables(): cosine = (cos_a * cos_b - sin_a * sin_b).reshape(length, bin_count)]
    convert_element_type x1 -> x0, local copies, waits for them, and re-layouts: 9.46 us -> none  [whiten(): (filtered * lax.rsqrt(mean_power + EPSILON)[:, None]).astype(jnp.bfloat16)]
  transfers between devices with their start and end apart: 4 -> 3, of which waited for: 2 -> 1; matrix products, arithmetic and copies ran while one was open for 8% -> 3% of each run, Pallas kernels for 0% -> 5%
where the time goes in v1:
time: 117 us; the launch traced here: 116 us
  blocking collectives  36.6 us (31%)
  Pallas kernels  33.5 us (29%)
  waiting for transfers between devices  26.9 us (23%)
  starting transfers between devices  12.9 us (11%)
  local copies, waits for them, and re-layouts  6.42 us (5%)
    all_to_all x1, blocking collectives, body(): owned = lax.all_to_all(parts, AXES, split_axis=0, concat_axis=0, tiled=True)  36.6 us
    all_to_all x1, waiting for transfers between devices, body(): lax.all_to_all(rows.reshape(devices, 2 * bins_device, width), AXES, split...  26.8 us
    pallas_call x1, Pallas kernels, body(): pl.pallas_call(functools.partial(whiten_kernel, length), out_shape=jax.Sh...  11.8 us
    pallas_call x1, Pallas kernels, body(): pl.pallas_call(functools.partial(pair_kernel, slots), out_shape=jax.Shape...  11.3 us
    all_to_all x1, starting transfers between devices, body(): lax.all_to_all(rows.reshape(devices, 2 * bins_device, width), AXES, split...  9.2 us
    pallas_call x1, Pallas kernels, body(): pl.pallas_call(own_kernel, out_shape=jax.ShapeDtypeStruct((RADIX, 2, widt...  6.34 us
    pallas_call x1, Pallas kernels, body(): pl.pallas_call(functools.partial(lag_kernel, slots, float(1.0 / np.sqrt(b...  4.06 us
    unnamed x12, local copies, waits for them, and re-layouts  3.72 us
  transfers between devices with their start and end apart: 3, of which 1 were waited for; matrix products, arithmetic and copies ran while one was open for 3% of the time, Pallas kernels for 5%

profile of v1, /device:TPU:0, one launch (start us, length us, event | category | flops | bytes accessed | tf_op | source)
XLA Modules:
  0.0 116.3 jit_solution(12420062311546862652)
XLA Ops:
  0.0 1.0 slice_bitcast_fusion
  1.0 2.4 %collective-permute-start = (bf16[16,4096]{1,0:T(8,128)(2,1)S(1)}, bf16[16,4096]{1,0:T(8,128)(2,1)S(1)}, u32[]{:S(2)}, u32[]{:S(2)}) collective-permute-start(bf16[16,4096]{1,0:T(8,128)(2,1)S(1)} %get-tuple-element.6), channel_id=1, source_target_pairs={{0,1},{1,2},{2,3},{3,4},{4,5},{5,6},{6,7},{7,8},{8,9},{9,10},{10,1... | collective-permute-start | bytes 393224 | tf_op jit(solution)/shard_map/ppermute | solution.py:298
  3.4 1.3 %collective-permute-start.1 = (bf16[16,4096]{1,0:T(8,128)(2,1)S(1)}, bf16[16,4096]{1,0:T(8,128)(2,1)S(1)}, u32[]{:S(2)}, u32[]{:S(2)}) collective-permute-start(bf16[16,4096]{1,0:T(8,128)(2,1)S(1)} %get-tuple-element.5), channel_id=1, source_target_pairs={{1,0},{2,1},{3,2},{4,3},{5,4},{6,5},{7,6},{8,7},{9,8},{10,9},{11,1... | collective-permute-start | bytes 393224 | tf_op jit(solution)/shard_map/ppermute | solution.py:299
  4.7 0.0 copy-start.4
  4.7 1.3 %copy.12 = f32[33,2048]{0,1:T(8,128)S(1)} copy(f32[33,2048]{1,0:T(8,128)} %param.11) | data formatting | bytes 540672 | tf_op args[1]
  6.0 1.2 %copy.13 = f32[33,128,16]{1,0,2:T(8,128)} copy(f32[33,128,16]{0,2,1:T(8,128)S(1)} %bitcast.9) | data formatting | bytes 540672 | tf_op jit(solution)/shard_map/reshape | solution.py:300
  7.2 0.0 copy-done.4
  7.2 0.5 dynamic_slice.3.offset_ref
  7.7 6.3 %own_spectra.1.own_ref = f32[16,2,128,128]{3,2,1,0:T(8,128)} custom-call(bf16[128,4096]{1,0:T(8,128)(2,1)} %bitcast.10, f32[32,256]{1,0:T(8,128)} %constant.24.clone.twiddle_ref, bf16[1536,256]{1,0:T(8,128)(2,1)} %constant.25.clone.table_ref), custom_call_target="tpu_custom_call" | custom-call | tf_op jit(solution)/shard_map/own_spectra/pallas_call | solution.py:303
  14.1 0.0 collective-permute-done.left_ref
  14.1 0.0 copy-start.1
  14.1 0.0 collective-permute-done.1.right_ref
  14.1 0.0 copy-start.2
  14.1 0.6 copy-done.1
  14.7 0.1 copy-done.2
  14.8 11.8 %whiten.1 = bf16[4096,128]{1,0:T(8,128)(2,1)} custom-call(s32[1]{0:T(128)} %dynamic_slice.3.offset_ref, f32[16,2,128,128]{3,2,1,0:T(8,128)} %own_spectra.1.own_ref, bf16[16,4096]{1,0:T(8,128)(2,1)} %copy-done.1, bf16[16,4096]{1,0:T(8,128)(2,1)} %copy-done.2, f32[32,256]{1,0:T(8,128)} %constant.24.clone.twiddle_ref, ...), custom_call_target="tpu_custom_call" | custom-call | tf_op jit(solution)/shard_map/whiten/pallas_call | solution.py:313
  26.6 0.0 copy-start.3
  26.6 9.2 %all-to-all-start = ((bf16[32,128,128]{2,1,0:T(8,128)(2,1)}), bf16[32,128,128]{2,1,0:T(8,128)(2,1)S(1)}, u32[]{:S(2)}, u32[]{:S(2)}) async-start(bf16[32,128,128]{2,1,0:T(8,128)(2,1)} %bitcast.8), calls=%async_computation | async-start | bytes 2097152 | tf_op jit(solution)/shard_map/all_to_all | solution.py:332
  35.8 0.0 copy-done.3
  35.8 0.7 copy.14.pairs_ref
  36.6 26.8 %all-to-all-done.band_ref = bf16[32,128,128]{2,1,0:T(8,128)(2,1)S(1)} async-done(((bf16[32,128,128]{2,1,0:T(8,128)(2,1)}), bf16[32,128,128]{2,1,0:T(8,128)(2,1)S(1)}, u32[]{:S(2)}, u32[]{:S(2)}) %all-to-all-start) | async-done | bytes 1048608 | tf_op jit(solution)/shard_map/all_to_all | solution.py:332
  63.4 0.0 copy-start
  63.4 1.0 copy-done
  64.4 11.3 %pair_products.1 = bf16[32,160,128]{2,1,0:T(8,128)(2,1)} custom-call(s32[128,2]{1,0:T(8,128)} %copy.14.pairs_ref, bf16[32,128,128]{2,1,0:T(8,128)(2,1)} %copy-done, bf16[40,128]{1,0:T(8,128)(2,1)} %constant.27.clone.basis_ref), custom_call_target="tpu_custom_call" | custom-call | tf_op jit(solution)/shard_map/pair_products/pallas_call | solution.py:336
  75.6 36.6 %all_to_all.10.parts_ref = bf16[32,160,128]{2,1,0:T(8,128)(2,1)} all-to-all(bf16[32,160,128]{2,1,0:T(8,128)(2,1)} %pair_products.1), channel_id=1, replica_groups=mesh['group'=4,'shard'=8] {'group','shard'}, dimensions={0} | all-to-all | bytes 2621440 | tf_op jit(solution)/shard_map/all_to_all | solution.py:350
  112.2 4.1 %lags.1 = f32[4,128,512]{2,1,0:T(8,128)} custom-call(s32[4]{0:T(128)} %valid_ref.1, bf16[32,160,128]{2,1,0:T(8,128)(2,1)} %all_to_all.10.parts_ref, bf16[512,1280]{1,0:T(8,128)(2,1)} %constant.28.clone.table_ref), custom_call_target="tpu_custom_call" | custom-call | tf_op jit(solution)/shard_map/lags/pallas_call | solution.py:352
Async XLA Ops:
  1.0 13.1 %collective-permute-start = (bf16[16,4096]{1,0:T(8,128)(2,1)S(1)}, bf16[16,4096]{1,0:T(8,128)(2,1)S(1)}, u32[]{:S(2)}, u32[]{:S(2)}) collective-permute-start(bf16[16,4096]{1,0:T(8,128)(2,1)S(1)} %get-tuple-element.6), channel_id=1, source_target_pairs={{0,1},{1,2},{2,3},{3,4},{4,5},{5,6},{6,7},{7,8},{8,9},{9,10},{10,1... | collective-permute-start | bytes 393224 | tf_op jit(solution)/shard_map/ppermute | solution.py:298
  3.4 10.7 %collective-permute-start.1 = (bf16[16,4096]{1,0:T(8,128)(2,1)S(1)}, bf16[16,4096]{1,0:T(8,128)(2,1)S(1)}, u32[]{:S(2)}, u32[]{:S(2)}) collective-permute-start(bf16[16,4096]{1,0:T(8,128)(2,1)S(1)} %get-tuple-element.5), channel_id=1, source_target_pairs={{1,0},{2,1},{3,2},{4,3},{5,4},{6,5},{7,6},{8,7},{9,8},{10,9},{11,1... | collective-permute-start | bytes 393224 | tf_op jit(solution)/shard_map/ppermute | solution.py:299
  4.7 2.5 %copy-start.4 = (s32[32]{0:T(128)S(1)}, s32[32]{0:T(128)}, u32[]{:S(2)}) copy-start(s32[32]{0:T(128)} %param.14) | copy-start | bytes 388
  14.1 0.6 copy-start.1
  14.1 0.7 copy-start.2
  26.6 9.2 %copy-start.3 = (s32[128,2]{0,1:T(2,128)S(1)}, s32[128,2]{0,1:T(2,128)}, u32[]{:S(2)}) copy-start(s32[128,2]{0,1:T(2,128)} %param.12) | copy-start | bytes 3076
  26.6 36.8 %all-to-all-start = ((bf16[32,128,128]{2,1,0:T(8,128)(2,1)}), bf16[32,128,128]{2,1,0:T(8,128)(2,1)S(1)}, u32[]{:S(2)}, u32[]{:S(2)}) async-start(bf16[32,128,128]{2,1,0:T(8,128)(2,1)} %bitcast.8), calls=%async_computation | async-start | bytes 2097152 | tf_op jit(solution)/shard_map/all_to_all | solution.py:332
  63.4 1.0 copy-start

commit v2 on v1

--- a/solution.py
+++ b/solution.py
@@ -15,7 +15,7 @@
 NLAG = 512
 EPSILON = 1e-05
 RADIX = 16
-VMEM_BYTES = 56 * 1024 * 1024
+VMEM_BYTES = 32 * 1024 * 1024
 F32 = jnp.float32
 BF16 = jnp.bfloat16
 
@@ -95,15 +95,12 @@
     return out
 
 
-def transform_rows(x_ref, twiddle_ref, z_ref, rows):
+def transform_rows(x_ref, first, rows, twiddle_ref, z_ref):
     inner = x_ref.shape[1] // RADIX
-
-    def step(i, carry):
-        at = pl.multiple_of(i * 16, 16)
-        for half in range(inner // 128):
-            lane = 128 * half
+    for at in range(0, rows, 16):
+        for lane in range(0, inner, 128):
             values = [
-                x_ref[pl.ds(at, 16), inner * j + lane : inner * j + lane + 128].astype(F32)
+                x_ref[first + at : first + at + 16, inner * j + lane : inner * j + lane + 128].astype(F32)
                 for j in range(RADIX)
             ]
             bins = real_dft(values)
@@ -120,16 +117,13 @@
                         zr, zi = yr * c, -yr * s
                     else:
                         zr, zi = yr * c + yi * s, yi * c - yr * s
-                where = pl.ds(pl.multiple_of(q * rows + at, 16), 16)
+                where = slice(q * rows + at, q * rows + at + 16)
                 for part, z in ((0, zr), (1, zi)):
                     high = z.astype(BF16)
                     z_ref[where, part * inner + lane : part * inner + lane + 128] = high
                     low = (z - high.astype(F32)).astype(BF16)
                     start = (2 + part) * inner + lane
                     z_ref[where, start : start + 128] = low
-        return carry
-
-    lax.fori_loop(0, rows // 16, step, 0)
 
 
 def transform_inner(z, table_ref):
@@ -140,13 +134,23 @@
     )
 
 
-def own_kernel(x_ref, twiddle_ref, table_ref, out_ref, z_ref):
-    rows = x_ref.shape[0]
-    transform_rows(x_ref, twiddle_ref, z_ref, rows)
+def own_kernel(x_ref, taps_ref, twiddle_ref, table_ref, out_ref, split_ref, z0_ref, z1_ref, turned_ref):
+    chunk = z0_ref.shape[0] // RADIX
+    steps = x_ref.shape[0] // chunk
+    slots = (z0_ref, z1_ref)
+    transform_rows(x_ref, 0, chunk, twiddle_ref, z0_ref)
+    for i in range(steps):
+        if i + 1 < steps:
+            transform_rows(x_ref, (i + 1) * chunk, chunk, twiddle_ref, slots[(i + 1) % 2])
+        values = transform_inner(slots[i % 2][...], table_ref)
+        for q in range(RADIX):
+            out_ref[q, 0, i * chunk : (i + 1) * chunk, :] = values[q * chunk : (q + 1) * chunk, :128]
+            out_ref[q, 1, i * chunk : (i + 1) * chunk, :] = values[q * chunk : (q + 1) * chunk, 128:]
+    count = taps_ref.shape[0]
+    for at in range(0, taps_ref.shape[1], 128):
+        turned_ref[at : at + 128, 0:count] = taps_ref[:, at : at + 128].T
     for q in range(RADIX):
-        values = transform_inner(z_ref[q * rows : (q + 1) * rows, :], table_ref)
-        out_ref[q, 0] = values[:, :128]
-        out_ref[q, 1] = values[:, 128:]
+        split_ref[q] = turned_ref[pl.ds(q, 128, stride=RADIX), 0:count].T
 
 
 def shifted(values, by):
@@ -163,7 +167,7 @@
     width = own_ref.shape[2]
     x_ref[0:HALF, :] = left_ref[...]
     x_ref[HALF:, :] = right_ref[...]
-    transform_rows(x_ref, twiddle_ref, z_ref, 2 * HALF)
+    transform_rows(x_ref, 0, 2 * HALF, twiddle_ref, z_ref)
     halo_ref[...] = transform_inner(z_ref[...], table_ref)
 
     power_ref[0] = jnp.zeros(power_ref.shape[1:], F32)
@@ -196,7 +200,7 @@
     bins = lax.broadcasted_iota(jnp.int32, (RADIX, 128), 1) * RADIX + lax.broadcasted_iota(
         jnp.int32, (RADIX, 128), 0
     )
-    phases = lax.rem(bins * offset_ref[0], length).astype(F32) * (2.0 * np.pi / length)
+    phases = lax.rem(bins * offset_ref[lax.axis_index(AXES)], length).astype(F32) * (2.0 * np.pi / length)
     cosine, sine = jnp.cos(phases), jnp.sin(phases)
     for q in range(RADIX):
         window = (
@@ -214,53 +218,73 @@
     out_ref[...] = rows_ref[...].astype(BF16)
 
 
-def pair_kernel(slots, pairs_ref, band_ref, basis_ref, out_ref, left_ref, right_ref, cross_ref):
+def pair_kernel(slots, pairs_ref, band_ref, basis_ref, out_ref, left_ref, right_ref, cross0_ref, cross1_ref):
     blocks = band_ref.shape[0]
     groups = band_ref.shape[1] // (2 * RADIX)
-    deep = basis_ref.shape[0]
 
     def spread(i, carry):
-        values = band_ref[i].astype(F32)
-        left_ref[i] = values
-        right_ref[i] = pltpu.roll(values, 64, 1)
+        for n in range(4):
+            values = band_ref[4 * i + n].astype(F32)
+            left_ref[4 * i + n] = values
+            right_ref[4 * i + n] = pltpu.roll(values, 64, 1)
         return carry
 
-    lax.fori_loop(0, blocks, spread, 0)
-
-    def owner(d, carry):
+    lax.fori_loop(0, blocks // 4, spread, 0)
+
+    def products(d, cross_ref):
         for j in range(slots):
-            a = pairs_ref[d * slots + j, 0]
-            b = pairs_ref[d * slots + j, 1]
+            a = pairs_ref[0, d * slots + j]
+            b = pairs_ref[1, d * slots + j]
             for m in range(groups):
                 lo, mid, hi = 2 * RADIX * m, 2 * RADIX * m + RADIX, 2 * RADIX * (m + 1)
                 lr, li = left_ref[a, lo:mid, :], left_ref[a, mid:hi, :]
                 rr, ri = right_ref[b, lo:mid, :], right_ref[b, mid:hi, :]
                 cross_ref[lo:mid, 128 * j : 128 * j + 128] = (lr * rr + li * ri).astype(BF16)
                 cross_ref[mid:hi, 128 * j : 128 * j + 128] = (li * rr - lr * ri).astype(BF16)
+
+    def project(d, cross_ref):
         result = jnp.dot(basis_ref[...], cross_ref[...], preferred_element_type=F32)
         stacked = jnp.concatenate([result[:, 128 * j : 128 * j + 128] for j in range(slots)], axis=0)
         out_ref[d] = stacked.astype(BF16)
+
+    products(0, cross0_ref)
+
+    def owners(i, carry):
+        products(2 * i + 1, cross1_ref)
+        project(2 * i, cross0_ref)
+        products(jnp.minimum(2 * i + 2, blocks - 1), cross0_ref)
+        project(2 * i + 1, cross1_ref)
         return carry
 
-    lax.fori_loop(0, blocks, owner, 0)
-
-
-def lag_kernel(slots, scale, valid_ref, parts_ref, table_ref, out_ref, wide_ref):
+    lax.fori_loop(0, blocks // 2, owners, 0)
+
+
+def lag_kernel(slots, scale, valid_ref, parts_ref, table_ref, out_ref, wide_ref, stage_ref, sem_ref):
     bands = parts_ref.shape[0]
     deep = parts_ref.shape[1] // slots
 
-    def gather(b, carry):
-        values = parts_ref[b].astype(F32)
-        for j in range(slots):
-            at = pl.multiple_of(b * deep, 8)
-            wide_ref[pl.ds(at, deep), 128 * j : 128 * j + 128] = values[deep * j : deep * (j + 1)]
+    def gather(i, carry):
+        for n in range(4):
+            b = 4 * i + n
+            values = parts_ref[b].astype(F32)
+            for j in range(slots):
+                at = pl.multiple_of(b * deep, 8)
+                wide_ref[pl.ds(at, deep), 128 * j : 128 * j + 128] = values[deep * j : deep * (j + 1)]
         return carry
 
-    lax.fori_loop(0, bands, gather, 0)
-    result = jnp.dot(table_ref[...], wide_ref[...].astype(BF16), preferred_element_type=F32)
-    for j in range(slots):
-        weight = valid_ref[j].astype(F32) * scale
-        out_ref[j] = result[:, 128 * j : 128 * j + 128].T * weight
+    lax.fori_loop(0, bands // 4, gather, 0)
+    copies = []
+    for first in range(0, slots, 2):
+        columns = wide_ref[:, 128 * first : 128 * first + 256].astype(BF16)
+        result = jnp.dot(table_ref[...], columns, preferred_element_type=F32)
+        for j in range(2):
+            weight = valid_ref[first + j].astype(F32) * scale
+            stage_ref[first + j] = result[:, 128 * j : 128 * j + 128].T * weight
+            copy = pltpu.make_async_copy(stage_ref.at[first + j], out_ref.at[first + j], sem_ref.at[first + j])
+            copy.start()
+            copies.append(copy)
+    for copy in copies:
+        copy.wait()
 
 
 def vmem():
@@ -273,6 +297,10 @@
 
 def params():
     return pltpu.CompilerParams(vmem_limit_bytes=VMEM_BYTES)
+
+
+def near(array):
+    return pltpu.with_memory_space_constraint(array, pltpu.VMEM)
 
 
 def body(samples, fan_taps, pair_blocks, pair_valid, coil_offsets):
@@ -284,6 +312,7 @@
     slots = pair_valid.shape[0]
     inner = length // RADIX
     lanes = bin_count // RADIX
+    chunk = 32
 
     twiddle, table = forward_constants(length)
     basis, lag_table = band_constants(devices, bins_device, length)
@@ -292,27 +321,33 @@
     bins_k = np.arange(bin_count)
     counts = np.minimum(bins_k + SMOOTH, bin_count - 1) - np.maximum(bins_k - SMOOTH, 0) + 1
     inverse_count = (1.0 / counts).reshape(lanes, RADIX).T.astype(np.float32)
+    twiddle, table = near(jnp.asarray(twiddle)), near(jnp.asarray(table))
 
     x = samples.reshape(width, length)
     ends = devices - 1
     left = lax.ppermute(x[width - HALF :], AXES, [(i, i + 1) for i in range(ends)])
     right = lax.ppermute(x[:HALF], AXES, [(i + 1, i) for i in range(ends)])
-    taps = jnp.transpose(fan_taps.reshape(2 * HALF + 1, lanes, RADIX), (2, 0, 1))
-    offset = lax.dynamic_slice(coil_offsets, (lax.axis_index(AXES),), (1,))
-
-    own = pl.pallas_call(
+
+    own, taps = pl.pallas_call(
         own_kernel,
-        out_shape=jax.ShapeDtypeStruct((RADIX, 2, width, lanes), F32),
-        in_specs=[vmem()] * 3,
-        out_specs=vmem(),
-        scratch_shapes=[pltpu.VMEM((RADIX * width, 4 * inner), BF16)],
+        out_shape=(
+            pltpu.VMEM((RADIX, 2, width, lanes), F32),
+            pltpu.VMEM((RADIX, 2 * HALF + 1, lanes), F32),
+        ),
+        in_specs=[vmem()] * 4,
+        out_specs=(vmem(), vmem()),
+        scratch_shapes=[
+            pltpu.VMEM((RADIX * chunk, 4 * inner), BF16),
+            pltpu.VMEM((RADIX * chunk, 4 * inner), BF16),
+            pltpu.VMEM((bin_count, 128), F32),
+        ],
         compiler_params=params(),
         name="own_spectra",
-    )(x, twiddle, table)
+    )(near(x), near(fan_taps), twiddle, table)
 
     rows = pl.pallas_call(
         functools.partial(whiten_kernel, length),
-        out_shape=jax.ShapeDtypeStruct((2 * bin_count, width), BF16),
+        out_shape=pltpu.VMEM((2 * bin_count, width), BF16),
         in_specs=[smem()] + [vmem()] * 7,
         out_specs=vmem(),
         scratch_shapes=[
@@ -327,7 +362,10 @@
         ],
         compiler_params=params(),
         name="whiten",
-    )(offset, own, left, right, twiddle, table, taps, inverse_count)
+    )(
+        coil_offsets, near(own), near(left), near(right), twiddle, table, near(taps),
+        near(jnp.asarray(inverse_count)),
+    )
 
     band = lax.all_to_all(
         rows.reshape(devices, 2 * bins_device, width), AXES, split_axis=0, concat_axis=0, tiled=True
@@ -335,17 +373,18 @@
 
     parts = pl.pallas_call(
         functools.partial(pair_kernel, slots),
-        out_shape=jax.ShapeDtypeStruct((devices, slots * deep, width), BF16),
+        out_shape=pltpu.VMEM((devices, slots * deep, width), BF16),
         in_specs=[smem(), vmem(), vmem()],
         out_specs=vmem(),
         scratch_shapes=[
             pltpu.VMEM((devices, 2 * bins_device, width), F32),
             pltpu.VMEM((devices, 2 * bins_device, width), F32),
             pltpu.VMEM((2 * bins_device, slots * width), BF16),
+            pltpu.VMEM((2 * bins_device, slots * width), BF16),
         ],
         compiler_params=params(),
         name="pair_products",
-    )(pair_blocks, band, project)
+    )(pair_blocks.T, near(band), near(jnp.asarray(project)))
 
     owned = lax.all_to_all(parts, AXES, split_axis=0, concat_axis=0, tiled=True)
 
@@ -353,11 +392,15 @@
         functools.partial(lag_kernel, slots, float(1.0 / np.sqrt(bin_count * samples.shape[1]))),
         out_shape=jax.ShapeDtypeStruct((slots, width, NLAG), F32),
         in_specs=[smem(), vmem(), vmem()],
-        out_specs=vmem(),
-        scratch_shapes=[pltpu.VMEM((devices * deep, slots * width), F32)],
+        out_specs=pl.BlockSpec(memory_space=pl.ANY),
+        scratch_shapes=[
+            pltpu.VMEM((devices * deep, slots * width), F32),
+            pltpu.VMEM((slots, width, NLAG), F32),
+            pltpu.SemaphoreType.DMA((slots,)),
+        ],
         compiler_params=params(),
         name="lags",
-    )(pair_valid, owned, lag_table)
+    )(pair_valid, near(owned), near(jnp.asarray(lag_table)))
 
 
 def solution(mesh):

time: 117 us -> 103 us (0.88)
  blocking collectives: 36.6 us -> 73.2 us
  waiting for transfers between devices: 26.9 us -> 0.01 us
  Pallas kernels: 33.5 us -> 20 us
  starting transfers between devices: 12.9 us -> 4.33 us
  local copies, waits for them, and re-layouts: 6.42 us -> 5.13 us
    all_to_all x0 -> x1, blocking collectives: none -> 38 us  [body(): lax.all_to_all(rows.reshape(devices, 2 * bins_device, width), AXES, split...]
    all_to_all x1 -> x0, waiting for transfers between devices: 26.8 us -> none  [body(): lax.all_to_all(rows.reshape(devices, 2 * bins_device, width), AXES, split...]
    pallas_call x3, Pallas kernels: 29.4 us -> 17.3 us  [the longest x1 8.64 us: body(): pl.pallas_call(functools.partial(whiten_kernel, length), out_shape=pltpu....]
    all_to_all x1 -> x0, starting transfers between devices: 9.2 us -> none  [body(): lax.all_to_all(rows.reshape(devices, 2 * bins_device, width), AXES, split...]
    all_to_all x1, blocking collectives: 36.6 us -> 35.2 us  [body(): owned = lax.all_to_all(parts, AXES, split_axis=0, concat_axis=0, tiled=True)]
    pallas_call x1, Pallas kernels: 4.06 us -> 2.73 us  [body(): pl.pallas_call(functools.partial(lag_kernel, slots, float(1.0 / np.sqrt(b...]
    unnamed x12 -> x22, local copies, waits for them, and re-layouts: 3.72 us -> 4.12 us
  transfers between devices with their start and end apart: 3 -> 2, of which waited for: 1 -> 0; matrix products, arithmetic and copies ran while one was open for 3% -> 0% of each run, Pallas kernels for 5% -> 3%
where the time goes in v2:
time: 103 us
  blocking collectives  73.2 us (71%)
  Pallas kernels  20 us (19%)
  local copies, waits for them, and re-layouts  5.13 us (5%)
  starting transfers between devices  4.33 us (4%)
    all_to_all x1, blocking collectives, body(): lax.all_to_all(rows.reshape(devices, 2 * bins_device, width), AXES, split...  38 us
    all_to_all x1, blocking collectives, body(): owned = lax.all_to_all(parts, AXES, split_axis=0, concat_axis=0, tiled=True)  35.2 us
    pallas_call x1, Pallas kernels, body(): pl.pallas_call(functools.partial(whiten_kernel, length), out_shape=pltpu....  8.64 us
    pallas_call x1, Pallas kernels, body(): pl.pallas_call(functools.partial(pair_kernel, slots), out_shape=pltpu.VME...  5.22 us
    unnamed x22, local copies, waits for them, and re-layouts  4.12 us
    pallas_call x1, Pallas kernels, body(): pl.pallas_call(own_kernel, out_shape=(pltpu.VMEM((RADIX, 2, width, lanes)...  3.42 us
    ppermute x1, starting transfers between devices, body(): lax.ppermute(x[width - HALF:], AXES, [(i, i + 1) for i in range(ends)])  3.04 us
    pallas_call x1, Pallas kernels, body(): pl.pallas_call(functools.partial(lag_kernel, slots, float(1.0 / np.sqrt(b...  2.73 us
  transfers between devices with their start and end apart: 2, of which 0 were waited for; matrix products, arithmetic and copies ran while one was open for 0% of the time, Pallas kernels for 3%

profile of v2, /device:TPU:0, one launch (start us, length us, event | category | flops | bytes accessed | tf_op | source)
XLA Modules:
  0.0 102.8 jit_solution(5683128939889540536)
XLA Ops:
  0.0 0.0 copy-start.7
  0.0 0.0 copy-start.9
  0.0 1.0 slice_bitcast_fusion
  1.0 1.3 %collective-permute-start.1 = (bf16[16,4096]{1,0:T(8,128)(2,1)S(1)}, bf16[16,4096]{1,0:T(8,128)(2,1)S(1)}, u32[]{:S(2)}, u32[]{:S(2)}) collective-permute-start(bf16[16,4096]{1,0:T(8,128)(2,1)S(1)} %get-tuple-element.9), channel_id=1, source_target_pairs={{1,0},{2,1},{3,2},{4,3},{5,4},{6,5},{7,6},{8,7},{9,8},{10,9},{11,1... | collective-permute-start | bytes 393224 | tf_op jit(solution)/shard_map/ppermute | solution.py:329
  2.3 3.0 %collective-permute-start = (bf16[16,4096]{1,0:T(8,128)(2,1)S(1)}, bf16[16,4096]{1,0:T(8,128)(2,1)S(1)}, u32[]{:S(2)}, u32[]{:S(2)}) collective-permute-start(bf16[16,4096]{1,0:T(8,128)(2,1)S(1)} %get-tuple-element.10), channel_id=1, source_target_pairs={{0,1},{1,2},{2,3},{3,4},{4,5},{5,6},{6,7},{7,8},{8,9},{9,10},{10,1... | collective-permute-start | bytes 393224 | tf_op jit(solution)/shard_map/ppermute | solution.py:328
  5.4 0.0 copy-start
  5.4 1.1 %copy-done = bf16[1536,256]{1,0:T(8,128)(2,1)S(1)} copy-done((bf16[1536,256]{1,0:T(8,128)(2,1)S(1)}, bf16[1536,256]{1,0:T(8,128)(2,1)}, u32[]{:S(2)}) %copy-start) | copy-done | bytes 786456
  6.5 0.0 copy-start.2
  6.5 1.2 %copy-done.2 = bf16[128,1,4096]{2,0,1:T(8,128)(2,1)S(1)} copy-done((bf16[128,1,4096]{2,0,1:T(8,128)(2,1)S(1)}, bf16[128,1,4096]{2,0,1:T(8,128)(2,1)}, u32[]{:S(2)}) %copy-start.2) | copy-done | bytes 1048600
  7.7 0.0 copy-start.4
  7.7 1.0 copy-done.4
  8.7 0.0 copy-start.5
  8.7 0.8 copy-done.5
  9.5 3.4 %own_spectra.1 = (f32[16,2,128,128]{3,2,1,0:T(8,128)S(1)}, f32[16,33,128]{2,1,0:T(8,128)S(1)}) custom-call(bf16[128,4096]{1,0:T(8,128)(2,1)S(1)} %bitcast.8, f32[33,2048]{1,0:T(8,128)S(1)} %copy-done.4, f32[32,256]{1,0:T(8,128)S(1)} %copy-done.5, bf16[1536,256]{1,0:T(8,128)(2,1)S(1)} %copy-done), custom_call_target="tpu_custom_call" | custom-call | tf_op jit(solution)/shard_map/own_spectra/pallas_call | solution.py:331
  12.9 0.0 collective-permute-done.1.right_ref
  12.9 0.0 collective-permute-done.left_ref
  12.9 0.0 copy-done.7
  12.9 0.0 copy-done.9
  12.9 0.0 copy-done.1
  12.9 8.6 %whiten.1 = bf16[4096,128]{1,0:T(8,128)(2,1)S(1)} custom-call(s32[32]{0:T(128)S(1)} %copy-done.9, f32[16,2,128,128]{3,2,1,0:T(8,128)S(1)} %get-tuple-element.7.own_ref, bf16[16,4096]{1,0:T(8,128)(2,1)S(1)} %collective-permute-done.left_ref, bf16[16,4096]{1,0:T(8,128)(2,1)S(1)} %collective-permute-done.1.right_ref, f32[32,256]{1,0:T(8,128)S(1)} %copy-done.5, ...), custom_call_target="tpu_custom_call" | custom-call | tf_op jit(solution)/shard_map/whiten/pallas_call | solution.py:348
  21.6 0.0 copy-start.6
  21.6 0.0 copy-start.8
  21.6 38.0 %all_to_all.10.band_ref = bf16[32,128,128]{2,1,0:T(8,128)(2,1)S(1)} all-to-all(bf16[32,128,128]{2,1,0:T(8,128)(2,1)S(1)} %bitcast.7), channel_id=1, replica_groups=mesh['group'=4,'shard'=8] {'group','shard'}, dimensions={0} | all-to-all | bytes 2097152 | tf_op jit(solution)/shard_map/all_to_all | solution.py:370
  59.6 0.0 copy-done.6
  59.6 0.0 copy-done.8
  59.6 5.2 %pair_products.1 = bf16[32,160,128]{2,1,0:T(8,128)(2,1)S(1)} custom-call(s32[2,128]{1,0:T(2,128)S(1)} %bitcast.9, bf16[32,128,128]{2,1,0:T(8,128)(2,1)S(1)} %all_to_all.10.band_ref, bf16[40,128]{1,0:T(8,128)(2,1)S(1)} %copy-done.6), custom_call_target="tpu_custom_call" | custom-call | tf_op jit(solution)/shard_map/pair_products/pallas_call | solution.py:374
  64.9 0.0 copy-start.3
  64.9 0.0 copy-start.10
  64.9 35.2 %all_to_all.11.parts_ref = bf16[32,160,128]{2,1,0:T(8,128)(2,1)S(1)} all-to-all(bf16[32,160,128]{2,1,0:T(8,128)(2,1)S(1)} %pair_products.1), channel_id=1, replica_groups=mesh['group'=4,'shard'=8] {'group','shard'}, dimensions={0} | all-to-all | bytes 2621440 | tf_op jit(solution)/shard_map/all_to_all | solution.py:389
  100.1 0.0 copy-done.3
  100.1 0.0 copy-done.10
  100.1 2.7 %lags.1 = f32[4,128,512]{2,1,0:T(8,128)} custom-call(s32[4]{0:T(128)S(1)} %copy-done.10, bf16[32,160,128]{2,1,0:T(8,128)(2,1)S(1)} %all_to_all.11.parts_ref, bf16[512,1280]{1,0:T(8,128)(2,1)S(1)} %copy-done.3), custom_call_target="tpu_custom_call" | custom-call | tf_op jit(solution)/shard_map/lags/pallas_call | solution.py:391
  (1 shorter events, 0.0 us)
Async XLA Ops:
  0.0 12.9 %copy-start.7 = (f32[16,128]{1,0:T(8,128)S(1)}, f32[16,128]{1,0:T(8,128)}, u32[]{:S(2)}) copy-start(f32[16,128]{1,0:T(8,128)} %constant.12.clone.count_ref) | copy-start | bytes 24580
  0.0 12.9 %copy-start.9 = (s32[32]{0:T(128)S(1)}, s32[32]{0:T(128)}, u32[]{:S(2)}) copy-start(s32[32]{0:T(128)} %offset_ref.1) | copy-start | bytes 388
  1.0 11.9 %collective-permute-start.1 = (bf16[16,4096]{1,0:T(8,128)(2,1)S(1)}, bf16[16,4096]{1,0:T(8,128)(2,1)S(1)}, u32[]{:S(2)}, u32[]{:S(2)}) collective-permute-start(bf16[16,4096]{1,0:T(8,128)(2,1)S(1)} %get-tuple-element.9), channel_id=1, source_target_pairs={{1,0},{2,1},{3,2},{4,3},{5,4},{6,5},{7,6},{8,7},{9,8},{10,9},{11,1... | collective-permute-start | bytes 393224 | tf_op jit(solution)/shard_map/ppermute | solution.py:329
  2.3 10.6 %collective-permute-start = (bf16[16,4096]{1,0:T(8,128)(2,1)S(1)}, bf16[16,4096]{1,0:T(8,128)(2,1)S(1)}, u32[]{:S(2)}, u32[]{:S(2)}) collective-permute-start(bf16[16,4096]{1,0:T(8,128)(2,1)S(1)} %get-tuple-element.10), channel_id=1, source_target_pairs={{0,1},{1,2},{2,3},{3,4},{4,5},{5,6},{6,7},{7,8},{8,9},{9,10},{10,1... | collective-permute-start | bytes 393224 | tf_op jit(solution)/shard_map/ppermute | solution.py:328
  5.4 1.1 %copy-start = (bf16[1536,256]{1,0:T(8,128)(2,1)S(1)}, bf16[1536,256]{1,0:T(8,128)(2,1)}, u32[]{:S(2)}) copy-start(bf16[1536,256]{1,0:T(8,128)(2,1)} %constant.11.clone.table_ref) | copy-start | bytes 2359300
  6.5 1.2 %copy-start.2 = (bf16[128,1,4096]{2,0,1:T(8,128)(2,1)S(1)}, bf16[128,1,4096]{2,0,1:T(8,128)(2,1)}, u32[]{:S(2)}) copy-start(bf16[128,1,4096]{2,0,1:T(8,128)(2,1)} %param.10) | copy-start | bytes 3145732
  7.7 1.0 copy-start.4
  8.7 0.8 copy-start.5
  9.5 3.5 %copy-start.1 = (bf16[1536,256]{1,0:T(8,128)(2,1)S(1)}, bf16[1536,256]{1,0:T(8,128)(2,1)}, u32[]{:S(2)}) copy-start(bf16[1536,256]{1,0:T(8,128)(2,1)} %constant.11.clone.table_ref) | copy-start | bytes 2359300
  21.6 38.0 %copy-start.6 = (bf16[40,128]{1,0:T(8,128)(2,1)S(1)}, bf16[40,128]{1,0:T(8,128)(2,1)}, u32[]{:S(2)}) copy-start(bf16[40,128]{1,0:T(8,128)(2,1)} %constant.13.clone.basis_ref) | copy-start | bytes 30724
  21.6 38.0 %copy-start.8 = (s32[128,2]{0,1:T(2,128)S(1)}, s32[128,2]{0,1:T(2,128)}, u32[]{:S(2)}) copy-start(s32[128,2]{0,1:T(2,128)} %param.12) | copy-start | bytes 3076
  64.9 35.3 %copy-start.3 = (bf16[512,1280]{1,0:T(8,128)(2,1)S(1)}, bf16[512,1280]{1,0:T(8,128)(2,1)}, u32[]{:S(2)}) copy-start(bf16[512,1280]{1,0:T(8,128)(2,1)} %constant.14.clone.table_ref) | copy-start | bytes 3932164
  64.9 35.2 %copy-start.10 = (s32[4]{0:T(128)S(1)}, s32[4]{0:T(128)}, u32[]{:S(2)}) copy-start(s32[4]{0:T(128)} %valid_ref.1) | copy-start | bytes 52

commit v3 on v2

--- a/solution.py
+++ b/solution.py
@@ -52,7 +52,8 @@
     rank = width
     for fewer in range(4, width, 4):
         basis = vectors[:, :fewer]
-        if np.abs(waves - basis @ (basis.T @ waves)).max() < 1e-7:
+        error = waves - basis @ (basis.T @ waves)
+        if np.sqrt(np.mean(np.abs(error) ** 2)) < 1e-7:
             rank = fewer
             break
     basis = vectors[:, :rank]
@@ -64,13 +65,14 @@
     return basis, as_bf16(np.ascontiguousarray(table.T))
 
 
-def projection_constants(basis, bins_device):
+def projection_constants(basis, halves):
     width, rank = basis.shape
-    rows = np.zeros((2, rank, width // RADIX, 2, RADIX))
-    split = basis.T.reshape(rank, width // RADIX, RADIX)
-    rows[0, :, :, 0, :] = split
-    rows[1, :, :, 1, :] = split
-    return as_bf16(rows.reshape(2 * rank, 2 * width))
+    groups = width // halves // RADIX
+    rows = np.zeros((halves, 2, rank, groups, 2, RADIX))
+    split = basis.T.reshape(rank, halves, groups, RADIX).transpose(1, 0, 2, 3)
+    rows[:, 0, :, :, 0, :] = split
+    rows[:, 1, :, :, 1, :] = split
+    return as_bf16(rows.reshape(halves, 2 * rank, 2 * groups * RADIX))
 
 
 def real_dft(values):
@@ -134,18 +136,36 @@
     )
 
 
-def own_kernel(x_ref, taps_ref, twiddle_ref, table_ref, out_ref, split_ref, z0_ref, z1_ref, turned_ref):
+def own_kernel(
+    x_hbm, taps_hbm, small_hbm, table_hbm, out_ref, split_ref, small_ref, table_ref,
+    x_ref, taps_ref, z0_ref, z1_ref, turned_ref, sem_ref,
+):
     chunk = z0_ref.shape[0] // RADIX
     steps = x_ref.shape[0] // chunk
     slots = (z0_ref, z1_ref)
-    transform_rows(x_ref, 0, chunk, twiddle_ref, z0_ref)
+    copies = [pltpu.make_async_copy(small_hbm, small_ref, sem_ref.at[0])]
+    for i in range(steps):
+        part = pl.ds(i * chunk, chunk)
+        copies.append(pltpu.make_async_copy(x_hbm.at[part], x_ref.at[part], sem_ref.at[1 + i]))
+    copies.append(pltpu.make_async_copy(table_hbm, table_ref, sem_ref.at[1 + steps]))
+    copies.append(pltpu.make_async_copy(taps_hbm, taps_ref, sem_ref.at[2 + steps]))
+    for copy in copies:
+        copy.start()
+    copies[0].wait()
+    copies[1].wait()
+    transform_rows(x_ref, 0, chunk, small_ref, z0_ref)
     for i in range(steps):
         if i + 1 < steps:
-            transform_rows(x_ref, (i + 1) * chunk, chunk, twiddle_ref, slots[(i + 1) % 2])
+            copies[2 + i].wait()
+        if i == 0:
+            copies[1 + steps].wait()
+        if i + 1 < steps:
+            transform_rows(x_ref, (i + 1) * chunk, chunk, small_ref, slots[(i + 1) % 2])
         values = transform_inner(slots[i % 2][...], table_ref)
         for q in range(RADIX):
             out_ref[q, 0, i * chunk : (i + 1) * chunk, :] = values[q * chunk : (q + 1) * chunk, :128]
             out_ref[q, 1, i * chunk : (i + 1) * chunk, :] = values[q * chunk : (q + 1) * chunk, 128:]
+    copies[2 + steps].wait()
     count = taps_ref.shape[0]
     for at in range(0, taps_ref.shape[1], 128):
         turned_ref[at : at + 128, 0:count] = taps_ref[:, at : at + 128].T
@@ -161,13 +181,13 @@
 
 
 def whiten_kernel(
-    length, offset_ref, own_ref, left_ref, right_ref, twiddle_ref, table_ref, taps_ref, count_ref, out_ref,
+    length, offset_ref, own_ref, left_ref, right_ref, small_ref, table_ref, taps_ref, out_ref,
     x_ref, z_ref, halo_ref, line_ref, filtered_ref, power_ref, base_ref, rows_ref,
 ):
     width = own_ref.shape[2]
     x_ref[0:HALF, :] = left_ref[...]
     x_ref[HALF:, :] = right_ref[...]
-    transform_rows(x_ref, 0, 2 * HALF, twiddle_ref, z_ref)
+    transform_rows(x_ref, 0, 2 * HALF, small_ref, z_ref)
     halo_ref[...] = transform_inner(z_ref[...], table_ref)
 
     power_ref[0] = jnp.zeros(power_ref.shape[1:], F32)
@@ -208,7 +228,7 @@
             + shifted(power_ref[RADIX] - power_ref[q], -reach)
             + shifted(power_ref[q + 1], reach)
         )
-        scale = lax.rsqrt(window * count_ref[q : q + 1, :] + EPSILON)
+        scale = lax.rsqrt(window * small_ref[2 * RADIX + q : 2 * RADIX + q + 1, 0:128] + EPSILON)
         fr, fi = filtered_ref[q, 0], filtered_ref[q, 1]
         c, s = cosine[q : q + 1, :], sine[q : q + 1, :]
         wr = (fr * c + fi * s) * scale
@@ -218,9 +238,17 @@
     out_ref[...] = rows_ref[...].astype(BF16)
 
 
-def pair_kernel(slots, pairs_ref, band_ref, basis_ref, out_ref, left_ref, right_ref, cross0_ref, cross1_ref):
+def pair_kernel(slots, mine, pairs_ref, band_ref, basis_ref, *refs):
+    if mine:
+        before_ref, (out_ref, left_ref, right_ref, cross0_ref, cross1_ref) = None, refs
+    else:
+        before_ref, out_ref, left_ref, right_ref, cross0_ref, cross1_ref = refs
     blocks = band_ref.shape[0]
     groups = band_ref.shape[1] // (2 * RADIX)
+    deep = basis_ref.shape[1]
+    half = lax.rem(lax.axis_index("shard"), 2)
+    part = half if mine else 1 - half
+    kept = slots // 2
 
     def spread(i, carry):
         for n in range(4):
@@ -231,45 +259,54 @@
 
     lax.fori_loop(0, blocks // 4, spread, 0)
 
-    def products(d, cross_ref):
-        for j in range(slots):
-            a = pairs_ref[0, d * slots + j]
-            b = pairs_ref[1, d * slots + j]
+    def products(i, cross_ref):
+        for n in range(2 * kept):
+            slot = (2 * i + n // kept) * slots + half * kept + n % kept
+            a, b = pairs_ref[0, slot], pairs_ref[1, slot]
             for m in range(groups):
                 lo, mid, hi = 2 * RADIX * m, 2 * RADIX * m + RADIX, 2 * RADIX * (m + 1)
                 lr, li = left_ref[a, lo:mid, :], left_ref[a, mid:hi, :]
                 rr, ri = right_ref[b, lo:mid, :], right_ref[b, mid:hi, :]
-                cross_ref[lo:mid, 128 * j : 128 * j + 128] = (lr * rr + li * ri).astype(BF16)
-                cross_ref[mid:hi, 128 * j : 128 * j + 128] = (li * rr - lr * ri).astype(BF16)
-
-    def project(d, cross_ref):
-        result = jnp.dot(basis_ref[...], cross_ref[...], preferred_element_type=F32)
-        stacked = jnp.concatenate([result[:, 128 * j : 128 * j + 128] for j in range(slots)], axis=0)
-        out_ref[d] = stacked.astype(BF16)
-
+                cross_ref[lo:mid, 128 * n : 128 * n + 128] = (lr * rr + li * ri).astype(BF16)
+                cross_ref[mid:hi, 128 * n : 128 * n + 128] = (li * rr - lr * ri).astype(BF16)
+
+    def project(i, cross_ref):
+        result = jnp.dot(basis_ref[part], cross_ref[...], preferred_element_type=F32)
+        for u in range(2):
+            lanes = [128 * (kept * u + j) for j in range(kept)]
+            stacked = jnp.concatenate([result[:, at : at + 128] for at in lanes], axis=0)
+            if mine:
+                out_ref[2 * i + u] = stacked
+            else:
+                out_ref[2 * i + u] = (stacked + before_ref[2 * i + u]).astype(BF16)
+
+    last = blocks // 2 - 1
     products(0, cross0_ref)
 
     def owners(i, carry):
         products(2 * i + 1, cross1_ref)
         project(2 * i, cross0_ref)
-        products(jnp.minimum(2 * i + 2, blocks - 1), cross0_ref)
+        products(jnp.minimum(2 * i + 2, last), cross0_ref)
         project(2 * i + 1, cross1_ref)
         return carry
 
-    lax.fori_loop(0, blocks // 2, owners, 0)
+    lax.fori_loop(0, blocks // 4, owners, 0)
 
 
 def lag_kernel(slots, scale, valid_ref, parts_ref, table_ref, out_ref, wide_ref, stage_ref, sem_ref):
-    bands = parts_ref.shape[0]
-    deep = parts_ref.shape[1] // slots
+    bands = parts_ref.shape[0] // 2
+    kept = slots // 2
+    deep = parts_ref.shape[1] // kept
 
     def gather(i, carry):
         for n in range(4):
             b = 4 * i + n
-            values = parts_ref[b].astype(F32)
-            for j in range(slots):
-                at = pl.multiple_of(b * deep, 8)
-                wide_ref[pl.ds(at, deep), 128 * j : 128 * j + 128] = values[deep * j : deep * (j + 1)]
+            at = pl.multiple_of(b * deep, 8)
+            for half in range(2):
+                values = parts_ref[2 * b + half].astype(F32)
+                for j in range(kept):
+                    lane = 128 * (half * kept + j)
+                    wide_ref[pl.ds(at, deep), lane : lane + 128] = values[deep * j : deep * (j + 1)]
         return carry
 
     lax.fori_loop(0, bands // 4, gather, 0)
@@ -303,11 +340,20 @@
     return pltpu.with_memory_space_constraint(array, pltpu.VMEM)
 
 
+def distant(array):
+    return pltpu.with_memory_space_constraint(array, pltpu.HBM)
+
+
+def far():
+    return pl.BlockSpec(memory_space=pltpu.HBM)
+
+
 def body(samples, fan_taps, pair_blocks, pair_valid, coil_offsets):
     width = samples.shape[0]
     length = samples.shape[2]
     bin_count = length // 2
     devices = lax.axis_size("group") * lax.axis_size("shard")
+    shards = lax.axis_size("shard")
     bins_device = bin_count // devices
     slots = pair_valid.shape[0]
     inner = length // RADIX
@@ -315,40 +361,46 @@
     chunk = 32
 
     twiddle, table = forward_constants(length)
-    basis, lag_table = band_constants(devices, bins_device, length)
-    project = projection_constants(basis, bins_device)
-    deep = project.shape[0]
+    basis, lag_table = band_constants(devices // 2, 2 * bins_device, length)
+    project = projection_constants(basis, 2)
+    deep = project.shape[1]
     bins_k = np.arange(bin_count)
     counts = np.minimum(bins_k + SMOOTH, bin_count - 1) - np.maximum(bins_k - SMOOTH, 0) + 1
-    inverse_count = (1.0 / counts).reshape(lanes, RADIX).T.astype(np.float32)
-    twiddle, table = near(jnp.asarray(twiddle)), near(jnp.asarray(table))
+    small = np.zeros((3 * RADIX, inner), np.float32)
+    small[: 2 * RADIX] = twiddle
+    small[2 * RADIX :, :lanes] = (1.0 / counts).reshape(lanes, RADIX).T
 
     x = samples.reshape(width, length)
     ends = devices - 1
     left = lax.ppermute(x[width - HALF :], AXES, [(i, i + 1) for i in range(ends)])
     right = lax.ppermute(x[:HALF], AXES, [(i + 1, i) for i in range(ends)])
 
-    own, taps = pl.pallas_call(
+    own, taps, small, table = pl.pallas_call(
         own_kernel,
         out_shape=(
             pltpu.VMEM((RADIX, 2, width, lanes), F32),
             pltpu.VMEM((RADIX, 2 * HALF + 1, lanes), F32),
+            pltpu.VMEM(small.shape, F32),
+            pltpu.VMEM(table.shape, BF16),
         ),
-        in_specs=[vmem()] * 4,
-        out_specs=(vmem(), vmem()),
+        in_specs=[far()] * 4,
+        out_specs=(vmem(), vmem(), vmem(), vmem()),
         scratch_shapes=[
+            pltpu.VMEM((width, length), BF16),
+            pltpu.VMEM(fan_taps.shape, F32),
             pltpu.VMEM((RADIX * chunk, 4 * inner), BF16),
             pltpu.VMEM((RADIX * chunk, 4 * inner), BF16),
             pltpu.VMEM((bin_count, 128), F32),
+            pltpu.SemaphoreType.DMA((width // chunk + 3,)),
         ],
         compiler_params=params(),
         name="own_spectra",
-    )(near(x), near(fan_taps), twiddle, table)
+    )(distant(x), distant(fan_taps), distant(jnp.asarray(small)), distant(jnp.asarray(table)))
 
     rows = pl.pallas_call(
         functools.partial(whiten_kernel, length),
         out_shape=pltpu.VMEM((2 * bin_count, width), BF16),
-        in_specs=[smem()] + [vmem()] * 7,
+        in_specs=[smem()] + [vmem()] * 6,
         out_specs=vmem(),
         scratch_shapes=[
             pltpu.VMEM((2 * HALF, length), BF16),
@@ -362,29 +414,35 @@
         ],
         compiler_params=params(),
         name="whiten",
-    )(
-        coil_offsets, near(own), near(left), near(right), twiddle, table, near(taps),
-        near(jnp.asarray(inverse_count)),
-    )
+    )(coil_offsets, near(own), near(left), near(right), near(small), near(table), near(taps))
 
     band = lax.all_to_all(
         rows.reshape(devices, 2 * bins_device, width), AXES, split_axis=0, concat_axis=0, tiled=True
     )
-
-    parts = pl.pallas_call(
-        functools.partial(pair_kernel, slots),
-        out_shape=pltpu.VMEM((devices, slots * deep, width), BF16),
-        in_specs=[smem(), vmem(), vmem()],
-        out_specs=vmem(),
-        scratch_shapes=[
-            pltpu.VMEM((devices, 2 * bins_device, width), F32),
-            pltpu.VMEM((devices, 2 * bins_device, width), F32),
-            pltpu.VMEM((2 * bins_device, slots * width), BF16),
-            pltpu.VMEM((2 * bins_device, slots * width), BF16),
-        ],
-        compiler_params=params(),
-        name="pair_products",
-    )(pair_blocks.T, near(band), near(jnp.asarray(project)))
+    other = lax.ppermute(band, "shard", [(i, i ^ 1) for i in range(shards)])
+
+    pairs = pair_blocks.T
+    project = near(jnp.asarray(project))
+    sums = (devices, slots // 2 * deep, width)
+
+    def products(mine, part, before):
+        return pl.pallas_call(
+            functools.partial(pair_kernel, slots, mine),
+            out_shape=pltpu.VMEM(sums, F32 if mine else BF16),
+            in_specs=[smem()] + [vmem()] * (2 + len(before)),
+            out_specs=vmem(),
+            scratch_shapes=[
+                pltpu.VMEM((devices, 2 * bins_device, width), F32),
+                pltpu.VMEM((devices, 2 * bins_device, width), F32),
+                pltpu.VMEM((2 * bins_device, slots * width), BF16),
+                pltpu.VMEM((2 * bins_device, slots * width), BF16),
+            ],
+            compiler_params=params(),
+            name="pairs_own_part" if mine else "pairs_other_part",
+        )(pairs, near(part), project, *before)
+
+    first = products(True, band, ())
+    parts = products(False, other, (near(first),))
 
     owned = lax.all_to_all(parts, AXES, split_axis=0, concat_axis=0, tiled=True)
 
@@ -394,7 +452,7 @@
         in_specs=[smem(), vmem(), vmem()],
         out_specs=pl.BlockSpec(memory_space=pl.ANY),
         scratch_shapes=[
-            pltpu.VMEM((devices * deep, slots * width), F32),
+            pltpu.VMEM((devices // 2 * deep, slots * width), F32),
             pltpu.VMEM((slots, width, NLAG), F32),
             pltpu.SemaphoreType.DMA((slots,)),
         ],

time: 103 us -> 94.6 us (0.918)
  blocking collectives: 73.2 us -> 64.9 us
  local copies, waits for them, and re-layouts: 5.13 us -> 1.03 us
  Pallas kernels: 20 us -> 23.9 us
    all_to_all x1, blocking collectives: 35.2 us -> 26.9 us  [body(): owned = lax.all_to_all(parts, AXES, split_axis=0, concat_axis=0, tiled=True)]
    unnamed x22 -> x10, local copies, waits for them, and re-layouts: 4.12 us -> 0.03 us
    pallas_call x1, Pallas kernels: 3.42 us -> 5.86 us  [body(): pl.pallas_call(own_kernel, out_shape=(pltpu.VMEM((RADIX, 2, width, lanes)...]
    pallas_call x1 -> x2, Pallas kernels: 5.22 us -> 6.89 us  [products(): pl.pallas_call(functools.partial(pair_kernel, slots, mine), out_shape=plt...]
  transfers between devices with their start and end apart: 2 -> 3, of which waited for: 0 -> 0; matrix products, arithmetic and copies ran while one was open for 0% -> 0% of each run, Pallas kernels for 3% -> 10%
where the time goes in v3:
time: 94.6 us; the launch traced here: 94.3 us
  blocking collectives  64.9 us (69%)
  Pallas kernels  23.9 us (25%)
  starting transfers between devices  4.33 us (5%)
  local copies, waits for them, and re-layouts  1.03 us (1%)
    all_to_all x1, blocking collectives, body(): lax.all_to_all(rows.reshape(devices, 2 * bins_device, width), AXES, split...  38 us
    all_to_all x1, blocking collectives, body(): owned = lax.all_to_all(parts, AXES, split_axis=0, concat_axis=0, tiled=True)  26.9 us
    pallas_call x1, Pallas kernels, body(): pl.pallas_call(functools.partial(whiten_kernel, length), out_shape=pltpu....  8.64 us
    pallas_call x2, Pallas kernels, products(): pl.pallas_call(functools.partial(pair_kernel, slots, mine), out_shape=plt...  6.89 us
    pallas_call x1, Pallas kernels, body(): pl.pallas_call(own_kernel, out_shape=(pltpu.VMEM((RADIX, 2, width, lanes)...  5.86 us
    ppermute x1, starting transfers between devices, body(): lax.ppermute(x[width - HALF:], AXES, [(i, i + 1) for i in range(ends)])  3.04 us
    pallas_call x1, Pallas kernels, body(): pl.pallas_call(functools.partial(lag_kernel, slots, float(1.0 / np.sqrt(b...  2.52 us
  transfers between devices with their start and end apart: 3, of which 0 were waited for; matrix products, arithmetic and copies ran while one was open for 0% of the time, Pallas kernels for 10%

profile of v3, /device:TPU:0, one launch (start us, length us, event | category | flops | bytes accessed | tf_op | source)
XLA Modules:
  0.0 94.3 jit_solution(2436445452280593958)
XLA Ops:
  0.0 0.0 copy-start.3
  0.0 1.0 %slice_bitcast_fusion = (bf16[16,4096]{1,0:T(8,128)(2,1)S(1)}, bf16[16,4096]{1,0:T(8,128)(2,1)S(1)}) fusion(bf16[128,1,4096]{2,0,1:T(8,128)(2,1)} %param.9), kind=kLoop, calls=%fused_computation | loop fusion | bytes 524288 | tf_op jit(solution)/shard_map/slice | solution.py:376
  1.0 1.3 %collective-permute-start.1 = (bf16[16,4096]{1,0:T(8,128)(2,1)S(1)}, bf16[16,4096]{1,0:T(8,128)(2,1)S(1)}, u32[]{:S(2)}, u32[]{:S(2)}) collective-permute-start(bf16[16,4096]{1,0:T(8,128)(2,1)S(1)} %get-tuple-element.13), channel_id=1, source_target_pairs={{1,0},{2,1},{3,2},{4,3},{5,4},{6,5},{7,6},{8,7},{9,8},{10,9},{11,1... | collective-permute-start | bytes 393224 | tf_op jit(solution)/shard_map/ppermute | solution.py:376
  2.3 3.0 %collective-permute-start = (bf16[16,4096]{1,0:T(8,128)(2,1)S(1)}, bf16[16,4096]{1,0:T(8,128)(2,1)S(1)}, u32[]{:S(2)}, u32[]{:S(2)}) collective-permute-start(bf16[16,4096]{1,0:T(8,128)(2,1)S(1)} %get-tuple-element.14), channel_id=1, source_target_pairs={{0,1},{1,2},{2,3},{3,4},{4,5},{5,6},{6,7},{7,8},{8,9},{9,10},{10,1... | collective-permute-start | bytes 393224 | tf_op jit(solution)/shard_map/ppermute | solution.py:375
  5.3 5.9 %own_spectra.1 = (f32[16,2,128,128]{3,2,1,0:T(8,128)S(1)}, f32[16,33,128]{2,1,0:T(8,128)S(1)}, f32[48,256]{1,0:T(8,128)S(1)}, bf16[1536,256]{1,0:T(8,128)(2,1)S(1)}) custom-call(bf16[128,4096]{1,0:T(8,128)(2,1)} %bitcast.10, f32[33,2048]{1,0:T(8,128)} %taps_hbm.1, f32[48,256]{1,0:T(8,128)} %constant.8.clone.small_hbm, bf16[1536,256]{1,0:T(8,128)(2,1)} %constant.9.clone.table_hbm), custom_call_target="tpu_custom_call" | custom-call | tf_op jit(solution)/shard_map/own_spectra/pallas_call | solution.py:378
  11.2 0.0 collective-permute-done.1.right_ref
  11.2 0.0 collective-permute-done.left_ref
  11.2 0.0 copy-done.3
  11.2 8.6 %whiten.1 = bf16[4096,128]{1,0:T(8,128)(2,1)S(1)} custom-call(s32[32]{0:T(128)S(1)} %copy-done.3, f32[16,2,128,128]{3,2,1,0:T(8,128)S(1)} %get-tuple-element.9.own_ref, bf16[16,4096]{1,0:T(8,128)(2,1)S(1)} %collective-permute-done.left_ref, bf16[16,4096]{1,0:T(8,128)(2,1)S(1)} %collective-permute-done.1.right_ref, ...), custom_call_target="tpu_custom_call" | custom-call | tf_op jit(solution)/shard_map/whiten/pallas_call | solution.py:400
  19.9 0.0 copy-start.1
  19.9 0.0 copy-start.2
  19.9 38.0 %all_to_all.10.band_ref = bf16[32,128,128]{2,1,0:T(8,128)(2,1)S(1)} all-to-all(bf16[32,128,128]{2,1,0:T(8,128)(2,1)S(1)} %bitcast.7), channel_id=1, replica_groups=mesh['group'=4,'shard'=8] {'group','shard'}, dimensions={0} | all-to-all | bytes 2097152 | tf_op jit(solution)/shard_map/all_to_all | solution.py:419
  57.9 0.0 collective-permute-start.2
  57.9 0.0 copy-done.1
  57.9 0.0 copy-done.2
  57.9 3.4 %pairs_own_part.1.refs_0_ = f32[32,112,128]{2,1,0:T(8,128)S(1)} custom-call(s32[2,128]{1,0:T(2,128)S(1)} %bitcast.8, bf16[32,128,128]{2,1,0:T(8,128)(2,1)S(1)} %all_to_all.10.band_ref, bf16[2,56,128]{2,1,0:T(8,128)(2,1)S(1)} %copy-done.1), custom_call_target="tpu_custom_call" | custom-call | tf_op jit(solution)/shard_map/pairs_own_part/pallas_call | solution.py:429
  61.4 0.0 copy-start
  61.4 0.0 copy-start.4
  61.4 0.0 collective-permute-done.2.band_ref
  61.4 3.4 %pairs_other_part.1 = bf16[32,112,128]{2,1,0:T(8,128)(2,1)S(1)} custom-call(s32[2,128]{1,0:T(2,128)S(1)} %bitcast.9, bf16[32,128,128]{2,1,0:T(8,128)(2,1)S(1)} %collective-permute-done.2.band_ref, bf16[2,56,128]{2,1,0:T(8,128)(2,1)S(1)} %copy-done.1, f32[32,112,128]{2,1,0:T(8,128)S(1)} %pairs_own_part.1.refs_0_), custom_call_target="tpu_custom_call" | custom-call | tf_op jit(solution)/shard_map/pairs_other_part/pallas_call | solution.py:429
  64.9 26.9 %all_to_all.11.parts_ref = bf16[32,112,128]{2,1,0:T(8,128)(2,1)S(1)} all-to-all(bf16[32,112,128]{2,1,0:T(8,128)(2,1)S(1)} %pairs_other_part.1), channel_id=1, replica_groups=mesh['group'=4,'shard'=8] {'group','shard'}, dimensions={0} | all-to-all | bytes 1835008 | tf_op jit(solution)/shard_map/all_to_all | solution.py:447
  91.8 0.0 copy-done
  91.8 0.0 copy-done.4
  91.8 2.5 %lags.1 = f32[4,128,512]{2,1,0:T(8,128)} custom-call(s32[4]{0:T(128)S(1)} %copy-done.4, bf16[32,112,128]{2,1,0:T(8,128)(2,1)S(1)} %all_to_all.11.parts_ref, bf16[512,896]{1,0:T(8,128)(2,1)S(1)} %copy-done), custom_call_target="tpu_custom_call" | custom-call | tf_op jit(solution)/shard_map/lags/pallas_call | solution.py:449
Async XLA Ops:
  0.0 11.2 %copy-start.3 = (s32[32]{0:T(128)S(1)}, s32[32]{0:T(128)}, u32[]{:S(2)}) copy-start(s32[32]{0:T(128)} %offset_ref.1) | copy-start | bytes 388
  1.0 10.2 %collective-permute-start.1 = (bf16[16,4096]{1,0:T(8,128)(2,1)S(1)}, bf16[16,4096]{1,0:T(8,128)(2,1)S(1)}, u32[]{:S(2)}, u32[]{:S(2)}) collective-permute-start(bf16[16,4096]{1,0:T(8,128)(2,1)S(1)} %get-tuple-element.13), channel_id=1, source_target_pairs={{1,0},{2,1},{3,2},{4,3},{5,4},{6,5},{7,6},{8,7},{9,8},{10,9},{11,1... | collective-permute-start | bytes 393224 | tf_op jit(solution)/shard_map/ppermute | solution.py:376
  2.3 8.9 %collective-permute-start = (bf16[16,4096]{1,0:T(8,128)(2,1)S(1)}, bf16[16,4096]{1,0:T(8,128)(2,1)S(1)}, u32[]{:S(2)}, u32[]{:S(2)}) collective-permute-start(bf16[16,4096]{1,0:T(8,128)(2,1)S(1)} %get-tuple-element.14), channel_id=1, source_target_pairs={{0,1},{1,2},{2,3},{3,4},{4,5},{5,6},{6,7},{7,8},{8,9},{9,10},{10,1... | collective-permute-start | bytes 393224 | tf_op jit(solution)/shard_map/ppermute | solution.py:375
  19.9 38.0 %copy-start.1 = (bf16[2,56,128]{2,1,0:T(8,128)(2,1)S(1)}, bf16[2,56,128]{2,1,0:T(8,128)(2,1)}, u32[]{:S(2)}) copy-start(bf16[2,56,128]{2,1,0:T(8,128)(2,1)} %constant.10.clone.basis_ref) | copy-start | bytes 86020
  19.9 38.0 %copy-start.2 = (s32[128,2]{0,1:T(2,128)S(1)}, s32[128,2]{0,1:T(2,128)}, u32[]{:S(2)}) copy-start(s32[128,2]{0,1:T(2,128)} %param.11) | copy-start | bytes 3076
  57.9 3.5 %collective-permute-start.2 = (bf16[32,128,128]{2,1,0:T(8,128)(2,1)S(1)}, bf16[32,128,128]{2,1,0:T(8,128)(2,1)S(1)}, u32[]{:S(2)}, u32[]{:S(2)}) collective-permute-start(bf16[32,128,128]{2,1,0:T(8,128)(2,1)S(1)} %all_to_all.10.band_ref), channel_id=1, source_target_pairs={{0,1},{1,0},{2,3},{3,2},{4,5},{5,4},{6,7},{7,6},{8,9},{9,8},{10,11... | collective-permute-start | bytes 3145736 | tf_op jit(solution)/shard_map/ppermute | solution.py:422
  61.4 30.4 %copy-start = (bf16[512,896]{1,0:T(8,128)(2,1)S(1)}, bf16[512,896]{1,0:T(8,128)(2,1)}, u32[]{:S(2)}) copy-start(bf16[512,896]{1,0:T(8,128)(2,1)} %constant.11.clone.table_ref) | copy-start | bytes 2752516
  61.4 30.4 %copy-start.4 = (s32[4]{0:T(128)S(1)}, s32[4]{0:T(128)}, u32[]{:S(2)}) copy-start(s32[4]{0:T(128)} %valid_ref.1) | copy-start | bytes 52

commit v4 on v3

--- a/solution.py
+++ b/solution.py
@@ -36,7 +36,7 @@
     ) / np.sqrt(length)
     high = as_bf16(table)
     low = as_bf16(table - high.astype(np.float64))
-    return twiddle, np.concatenate([high, high, low])
+    return twiddle, np.concatenate([high, low])
 
 
 def band_constants(bands, width, length):
@@ -129,88 +129,123 @@
 
 
 def transform_inner(z, table_ref):
-    depth = z.shape[1]
-    out = jnp.dot(z, table_ref[0:depth, :], preferred_element_type=F32)
-    return out + jnp.dot(
-        z[:, : depth // 2], table_ref[depth:, :], preferred_element_type=F32
-    )
+    depth = z.shape[1] // 2
+    high, low = table_ref[0:depth, :], table_ref[depth:, :]
+    out = jnp.dot(z[:, :depth], high, preferred_element_type=F32)
+    out = out + jnp.dot(z[:, depth:], high, preferred_element_type=F32)
+    return out + jnp.dot(z[:, :depth], low, preferred_element_type=F32)
 
 
 def own_kernel(
-    x_hbm, taps_hbm, small_hbm, table_hbm, out_ref, split_ref, small_ref, table_ref,
+    x_hbm, taps_hbm, small_hbm, table_hbm, out_ref, split_ref, both_ref, small_ref, table_ref,
     x_ref, taps_ref, z0_ref, z1_ref, turned_ref, sem_ref,
 ):
     chunk = z0_ref.shape[0] // RADIX
     steps = x_ref.shape[0] // chunk
     slots = (z0_ref, z1_ref)
-    copies = [pltpu.make_async_copy(small_hbm, small_ref, sem_ref.at[0])]
+    copies = [pltpu.make_async_copy(taps_hbm, taps_ref, sem_ref.at[0])]
+    copies.append(pltpu.make_async_copy(small_hbm, small_ref, sem_ref.at[1]))
+    copies.append(pltpu.make_async_copy(table_hbm, table_ref, sem_ref.at[2]))
     for i in range(steps):
         part = pl.ds(i * chunk, chunk)
-        copies.append(pltpu.make_async_copy(x_hbm.at[part], x_ref.at[part], sem_ref.at[1 + i]))
-    copies.append(pltpu.make_async_copy(table_hbm, table_ref, sem_ref.at[1 + steps]))
-    copies.append(pltpu.make_async_copy(taps_hbm, taps_ref, sem_ref.at[2 + steps]))
+        copies.append(pltpu.make_async_copy(x_hbm.at[part], x_ref.at[part], sem_ref.at[3 + i]))
     for copy in copies:
         copy.start()
+
     copies[0].wait()
+    count = taps_ref.shape[0]
+    pitch = RADIX + 1
+    for at in range(0, taps_ref.shape[1], 128):
+        turned = taps_ref[:, at : at + 128].T
+        for n in range(128 // RADIX):
+            row = (at // RADIX + n) * pitch
+            turned_ref[row : row + RADIX, 0:count] = turned[RADIX * n : RADIX * (n + 1)]
+    for q in range(RADIX):
+        taps = turned_ref[pl.ds(q, 128, stride=pitch), 0:count].T
+        split_ref[q, 0:count, :] = taps
+        even = split_ref[q, pl.ds(0, HALF, stride=2), :]
+        odd = split_ref[q, pl.ds(1, HALF, stride=2), :]
+        both_ref[q, 0:HALF, :] = even + odd
+        both_ref[q, HALF : HALF + 1, :] = taps[count - 1 :]
+
     copies[1].wait()
+    copies[3].wait()
     transform_rows(x_ref, 0, chunk, small_ref, z0_ref)
+    copies[2].wait()
     for i in range(steps):
         if i + 1 < steps:
-            copies[2 + i].wait()
-        if i == 0:
-            copies[1 + steps].wait()
-        if i + 1 < steps:
+            copies[4 + i].wait()
             transform_rows(x_ref, (i + 1) * chunk, chunk, small_ref, slots[(i + 1) % 2])
         values = transform_inner(slots[i % 2][...], table_ref)
         for q in range(RADIX):
             out_ref[q, 0, i * chunk : (i + 1) * chunk, :] = values[q * chunk : (q + 1) * chunk, :128]
             out_ref[q, 1, i * chunk : (i + 1) * chunk, :] = values[q * chunk : (q + 1) * chunk, 128:]
-    copies[2 + steps].wait()
-    count = taps_ref.shape[0]
-    for at in range(0, taps_ref.shape[1], 128):
-        turned_ref[at : at + 128, 0:count] = taps_ref[:, at : at + 128].T
-    for q in range(RADIX):
-        split_ref[q] = turned_ref[pl.ds(q, 128, stride=RADIX), 0:count].T
-
-
-def shifted(values, by):
-    count = values.shape[1]
-    lane = lax.broadcasted_iota(jnp.int32, values.shape, 1)
-    inside = (lane + by >= 0) & (lane + by < count)
-    return jnp.where(inside, pltpu.roll(values, (-by) % count, 1), 0.0)
 
 
 def whiten_kernel(
-    length, offset_ref, own_ref, left_ref, right_ref, small_ref, table_ref, taps_ref, out_ref,
-    x_ref, z_ref, halo_ref, line_ref, filtered_ref, power_ref, base_ref, rows_ref,
+    length, offset_ref, own_ref, left_ref, right_ref, small_ref, table_ref, taps_ref, both_ref, out_ref,
+    x_ref, z_ref, halo_ref, even_ref, odd_ref, pair_ref, part_ref, filtered_ref, power_ref, base_ref, rows_ref,
 ):
     width = own_ref.shape[2]
     x_ref[0:HALF, :] = left_ref[...]
     x_ref[HALF:, :] = right_ref[...]
     transform_rows(x_ref, 0, 2 * HALF, small_ref, z_ref)
-    halo_ref[...] = transform_inner(z_ref[...], table_ref)
+    values = transform_inner(z_ref[...], table_ref)
+    halo_ref[0] = values[:, :128]
+    halo_ref[1] = values[:, 128:]
 
     power_ref[0] = jnp.zeros(power_ref.shape[1:], F32)
+
+    half = width // 2
+    count = half + HALF
+    edge = HALF // 2
+    even_ref[:, count:, :] = jnp.zeros((2, even_ref.shape[1] - count, 128), F32)
+
+    def placed(values, parity):
+        quarter = half // 2
+        for high in range(2):
+            first = half * high + quarter * parity
+            yield slice(first, first + quarter), values[quarter * high : quarter * (high + 1)]
 
     def filter_step(q, carry):
         at = pl.multiple_of(q * 2 * HALF, 2 * HALF)
-        total = None
+        total = [None, None]
         for r in range(2):
-            halo = halo_ref[pl.ds(at, 2 * HALF), 128 * r : 128 * r + 128]
-            line_ref[r, 0:HALF, :] = halo[:HALF]
-            line_ref[r, HALF : HALF + width, :] = own_ref[q, r]
-            line_ref[r, HALF + width :, :] = halo[HALF:]
-            result = jnp.zeros((width, 128), F32)
-            for t in range(2 * HALF + 1):
-                result = result + taps_ref[q, t : t + 1, :] * line_ref[r, t : t + width, :]
-            filtered_ref[q, r] = result
-            total = result * result if total is None else total + result * result
-        power_ref[q + 1] = power_ref[q] + total
+            for first, ref in ((0, even_ref), (1, odd_ref)):
+                ref[r, 0:edge, :] = halo_ref[r, pl.ds(at + first, edge, stride=2), :]
+                ref[r, edge : edge + half, :] = own_ref[q, r, pl.ds(first, half, stride=2), :]
+                ref[r, edge + half : count, :] = halo_ref[r, pl.ds(at + HALF + first, edge, stride=2), :]
+            pair_ref[r] = odd_ref[r] + even_ref[r, 1 : count + 1, :]
+            evens = jnp.zeros((half + 8, 128), F32)
+            odds = jnp.zeros((half, 128), F32)
+            pairs = jnp.zeros((half, 128), F32)
+            for u in range(HALF + 1):
+                evens = evens + taps_ref[q, 2 * u : 2 * u + 1, :] * even_ref[r, u : u + half + 8, :]
+            part_ref[r] = evens
+            for u in range(HALF):
+                odds = odds + taps_ref[q, 2 * u + 1 : 2 * u + 2, :] * odd_ref[r, u : u + half, :]
+            for u in range(HALF + 1):
+                pairs = pairs + both_ref[q, u : u + 1, :] * pair_ref[r, u : u + half, :]
+            result = (evens[:half] + odds, pairs - (part_ref[r, 1 : half + 1, :] + odds))
+            for n in range(2):
+                for rows, values in placed(result[n], n):
+                    filtered_ref[q, r, rows, :] = values
+                square = result[n] * result[n]
+                total[n] = square if r == 0 else total[n] + square
+        for n in range(2):
+            for rows, values in placed(total[n], n):
+                power_ref[q + 1, rows, :] = power_ref[q, rows, :] + values
         return carry
 
     lax.fori_loop(0, RADIX, filter_step, 0)
 
     reach = SMOOTH // RADIX
+    lane = lax.broadcasted_iota(jnp.int32, (1, 128), 1)
+
+    def shifted(values, by):
+        inside = jnp.where((lane + by >= 0) & (lane + by < 128), 1.0, 0.0)
+        return pltpu.roll(values, (-by) % 128, 1) * inside
+
     whole = power_ref[RADIX]
     base = whole
     for by in range(1, reach):
@@ -222,6 +257,7 @@
     )
     phases = lax.rem(bins * offset_ref[lax.axis_index(AXES)], length).astype(F32) * (2.0 * np.pi / length)
     cosine, sine = jnp.cos(phases), jnp.sin(phases)
+    pitch = 2 * RADIX + 1
     for q in range(RADIX):
         window = (
             base_ref[...]
@@ -233,9 +269,11 @@
         c, s = cosine[q : q + 1, :], sine[q : q + 1, :]
         wr = (fr * c + fi * s) * scale
         wi = (fi * c - fr * s) * scale
-        rows_ref[pl.ds(q, 128, stride=2 * RADIX), :] = wr.T
-        rows_ref[pl.ds(RADIX + q, 128, stride=2 * RADIX), :] = wi.T
-    out_ref[...] = rows_ref[...].astype(BF16)
+        rows_ref[pl.ds(q, 128, stride=pitch), :] = wr.T
+        rows_ref[pl.ds(RADIX + q, 128, stride=pitch), :] = wi.T
+    for m in range(128):
+        rows = rows_ref[m * pitch : m * pitch + 2 * RADIX, :]
+        out_ref[2 * RADIX * m : 2 * RADIX * (m + 1), :] = rows.astype(BF16)
 
 
 def pair_kernel(slots, mine, pairs_ref, band_ref, basis_ref, *refs):
@@ -249,19 +287,20 @@
     half = lax.rem(lax.axis_index("shard"), 2)
     part = half if mine else 1 - half
     kept = slots // 2
+    step = cross0_ref.shape[1] // (128 * kept)
 
     def spread(i, carry):
-        for n in range(4):
-            values = band_ref[4 * i + n].astype(F32)
-            left_ref[4 * i + n] = values
-            right_ref[4 * i + n] = pltpu.roll(values, 64, 1)
+        for n in range(8):
+            values = band_ref[8 * i + n].astype(F32)
+            left_ref[8 * i + n] = values
+            right_ref[8 * i + n] = pltpu.roll(values, 64, 1)
         return carry
 
-    lax.fori_loop(0, blocks // 4, spread, 0)
+    lax.fori_loop(0, blocks // 8, spread, 0)
 
     def products(i, cross_ref):
-        for n in range(2 * kept):
-            slot = (2 * i + n // kept) * slots + half * kept + n % kept
+        for n in range(step * kept):
+            slot = (step * i + n // kept) * slots + half * kept + n % kept
             a, b = pairs_ref[0, slot], pairs_ref[1, slot]
             for m in range(groups):
                 lo, mid, hi = 2 * RADIX * m, 2 * RADIX * m + RADIX, 2 * RADIX * (m + 1)
@@ -272,15 +311,15 @@
 
     def project(i, cross_ref):
         result = jnp.dot(basis_ref[part], cross_ref[...], preferred_element_type=F32)
-        for u in range(2):
+        for u in range(step):
             lanes = [128 * (kept * u + j) for j in range(kept)]
             stacked = jnp.concatenate([result[:, at : at + 128] for at in lanes], axis=0)
             if mine:
-                out_ref[2 * i + u] = stacked
+                out_ref[step * i + u] = stacked
             else:
-                out_ref[2 * i + u] = (stacked + before_ref[2 * i + u]).astype(BF16)
-
-    last = blocks // 2 - 1
+                out_ref[step * i + u] = (stacked + before_ref[step * i + u]).astype(BF16)
+
+    last = blocks // step - 1
     products(0, cross0_ref)
 
     def owners(i, carry):
@@ -290,7 +329,7 @@
         project(2 * i + 1, cross1_ref)
         return carry
 
-    lax.fori_loop(0, blocks // 4, owners, 0)
+    lax.fori_loop(0, blocks // (2 * step), owners, 0)
 
 
 def lag_kernel(slots, scale, valid_ref, parts_ref, table_ref, out_ref, wide_ref, stage_ref, sem_ref):
@@ -313,13 +352,21 @@
     copies = []
     for first in range(0, slots, 2):
         columns = wide_ref[:, 128 * first : 128 * first + 256].astype(BF16)
-        result = jnp.dot(table_ref[...], columns, preferred_element_type=F32)
-        for j in range(2):
-            weight = valid_ref[first + j].astype(F32) * scale
-            stage_ref[first + j] = result[:, 128 * j : 128 * j + 128].T * weight
-            copy = pltpu.make_async_copy(stage_ref.at[first + j], out_ref.at[first + j], sem_ref.at[first + j])
-            copy.start()
-            copies.append(copy)
+        for n in range(NLAG // 128):
+            result = jnp.dot(table_ref[128 * n : 128 * n + 128, :], columns, preferred_element_type=F32)
+            for j in range(2):
+                turned = result[:, 128 * j : 128 * j + 128].T * (valid_ref[first + j].astype(F32) * scale)
+                half = turned.shape[0] // 2
+                at = (first + j) * (NLAG // 128) + n
+                for high in range(2):
+                    for parity in range(2):
+                        row = half * high + half // 2 * parity
+                        rows = turned[row : row + half // 2]
+                        stage_ref[at, pl.ds(half * high + parity, half // 2, stride=2), :] = rows
+                lanes = pl.ds(128 * n, 128)
+                copy = pltpu.make_async_copy(stage_ref.at[at], out_ref.at[first + j, :, lanes], sem_ref.at[at])
+                copy.start()
+                copies.append(copy)
     for copy in copies:
         copy.wait()
 
@@ -358,7 +405,7 @@
     slots = pair_valid.shape[0]
     inner = length // RADIX
     lanes = bin_count // RADIX
-    chunk = 32
+    chunk = 64
 
     twiddle, table = forward_constants(length)
     basis, lag_table = band_constants(devices // 2, 2 * bins_device, length)
@@ -375,22 +422,23 @@
     left = lax.ppermute(x[width - HALF :], AXES, [(i, i + 1) for i in range(ends)])
     right = lax.ppermute(x[:HALF], AXES, [(i + 1, i) for i in range(ends)])
 
-    own, taps, small, table = pl.pallas_call(
+    own, taps, both, small, table = pl.pallas_call(
         own_kernel,
         out_shape=(
             pltpu.VMEM((RADIX, 2, width, lanes), F32),
             pltpu.VMEM((RADIX, 2 * HALF + 1, lanes), F32),
+            pltpu.VMEM((RADIX, HALF + 1, lanes), F32),
             pltpu.VMEM(small.shape, F32),
             pltpu.VMEM(table.shape, BF16),
         ),
         in_specs=[far()] * 4,
-        out_specs=(vmem(), vmem(), vmem(), vmem()),
+        out_specs=(vmem(),) * 5,
         scratch_shapes=[
             pltpu.VMEM((width, length), BF16),
             pltpu.VMEM(fan_taps.shape, F32),
             pltpu.VMEM((RADIX * chunk, 4 * inner), BF16),
             pltpu.VMEM((RADIX * chunk, 4 * inner), BF16),
-            pltpu.VMEM((bin_count, 128), F32),
+            pltpu.VMEM((bin_count + lanes, 128), F32),
             pltpu.SemaphoreType.DMA((width // chunk + 3,)),
         ],
         compiler_params=params(),
@@ -400,21 +448,24 @@
     rows = pl.pallas_call(
         functools.partial(whiten_kernel, length),
         out_shape=pltpu.VMEM((2 * bin_count, width), BF16),
-        in_specs=[smem()] + [vmem()] * 6,
+        in_specs=[smem()] + [vmem()] * 7,
         out_specs=vmem(),
         scratch_shapes=[
             pltpu.VMEM((2 * HALF, length), BF16),
             pltpu.VMEM((RADIX * 2 * HALF, 4 * inner), BF16),
-            pltpu.VMEM((RADIX * 2 * HALF, 2 * lanes), F32),
-            pltpu.VMEM((2, width + 2 * HALF, lanes), F32),
+            pltpu.VMEM((2, RADIX * 2 * HALF, lanes), F32),
+            pltpu.VMEM((2, width // 2 + HALF + 8, lanes), F32),
+            pltpu.VMEM((2, width // 2 + HALF, lanes), F32),
+            pltpu.VMEM((2, width // 2 + HALF, lanes), F32),
+            pltpu.VMEM((2, width // 2 + 8, lanes), F32),
             pltpu.VMEM((RADIX, 2, width, lanes), F32),
             pltpu.VMEM((RADIX + 1, width, lanes), F32),
             pltpu.VMEM((width, lanes), F32),
-            pltpu.VMEM((2 * bin_count, width), F32),
+            pltpu.VMEM((2 * bin_count + lanes, width), F32),
         ],
         compiler_params=params(),
         name="whiten",
-    )(coil_offsets, near(own), near(left), near(right), near(small), near(table), near(taps))
+    )(coil_offsets, near(own), near(left), near(right), near(small), near(table), near(taps), near(both))
 
     band = lax.all_to_all(
         rows.reshape(devices, 2 * bins_device, width), AXES, split_axis=0, concat_axis=0, tiled=True
@@ -434,8 +485,8 @@
             scratch_shapes=[
                 pltpu.VMEM((devices, 2 * bins_device, width), F32),
                 pltpu.VMEM((devices, 2 * bins_device, width), F32),
-                pltpu.VMEM((2 * bins_device, slots * width), BF16),
-                pltpu.VMEM((2 * bins_device, slots * width), BF16),
+                pltpu.VMEM((2 * bins_device, 4 * slots * width), BF16),
+                pltpu.VMEM((2 * bins_device, 4 * slots * width), BF16),
             ],
             compiler_params=params(),
             name="pairs_own_part" if mine else "pairs_other_part",
@@ -453,8 +504,8 @@
         out_specs=pl.BlockSpec(memory_space=pl.ANY),
         scratch_shapes=[
             pltpu.VMEM((devices // 2 * deep, slots * width), F32),
-            pltpu.VMEM((slots, width, NLAG), F32),
-            pltpu.SemaphoreType.DMA((slots,)),
+            pltpu.VMEM((slots * NLAG // 128, width, 128), F32),
+            pltpu.SemaphoreType.DMA((slots * NLAG // 128,)),
         ],
         compiler_params=params(),
         name="lags",

time: 94.6 us -> 89.5 us (0.946)
  Pallas kernels: 23.9 us -> 18.8 us
    pallas_call x2, Pallas kernels: 6.89 us -> 5.06 us  [products(): pl.pallas_call(functools.partial(pair_kernel, slots, mine), out_shape=plt...]
    pallas_call x1, Pallas kernels: 8.64 us -> 6.95 us  [body(): pl.pallas_call(functools.partial(whiten_kernel, length), out_shape=pltpu....]
    pallas_call x1, Pallas kernels: 5.86 us -> 4.52 us  [body(): pl.pallas_call(own_kernel, out_shape=(pltpu.VMEM((RADIX, 2, width, lanes)...]
  transfers between devices with their start and end apart: 3 -> 3, of which waited for: 0 -> 1; matrix products, arithmetic and copies ran while one was open for 0% -> 0% of each run, Pallas kernels for 10% -> 8%
where the time goes in v4:
time: 89.5 us; the launch traced here: 89.3 us
  blocking collectives  64.8 us (72%)
  Pallas kernels  18.8 us (21%)
  starting transfers between devices  4.33 us (5%)
  local copies, waits for them, and re-layouts  1.03 us (1%)
    all_to_all x1, blocking collectives, body(): lax.all_to_all(rows.reshape(devices, 2 * bins_device, width), AXES, split...  38 us
    all_to_all x1, blocking collectives, body(): owned = lax.all_to_all(parts, AXES, split_axis=0, concat_axis=0, tiled=True)  26.8 us
    pallas_call x1, Pallas kernels, body(): pl.pallas_call(functools.partial(whiten_kernel, length), out_shape=pltpu....  6.95 us
    pallas_call x2, Pallas kernels, products(): pl.pallas_call(functools.partial(pair_kernel, slots, mine), out_shape=plt...  5.06 us
    pallas_call x1, Pallas kernels, body(): pl.pallas_call(own_kernel, out_shape=(pltpu.VMEM((RADIX, 2, width, lanes)...  4.52 us
    ppermute x1, starting transfers between devices, body(): lax.ppermute(x[width - HALF:], AXES, [(i, i + 1) for i in range(ends)])  3.04 us
    pallas_call x1, Pallas kernels, body(): pl.pallas_call(functools.partial(lag_kernel, slots, float(1.0 / np.sqrt(b...  2.31 us
  transfers between devices with their start and end apart: 3, of which 1 were waited for; matrix products, arithmetic and copies ran while one was open for 0% of the time, Pallas kernels for 8%

profile of v4, /device:TPU:0, one launch (start us, length us, event | category | flops | bytes accessed | tf_op | source)
XLA Modules:
  0.0 89.3 jit_solution(12056749461934863805)
XLA Ops:
  0.0 0.0 copy-start.3
  0.0 1.0 %slice_bitcast_fusion = (bf16[16,4096]{1,0:T(8,128)(2,1)S(1)}, bf16[16,4096]{1,0:T(8,128)(2,1)S(1)}) fusion(bf16[128,1,4096]{2,0,1:T(8,128)(2,1)} %param.9), kind=kLoop, calls=%fused_computation | loop fusion | bytes 524288 | tf_op jit(solution)/shard_map/slice | solution.py:423
  1.0 1.3 %collective-permute-start.1 = (bf16[16,4096]{1,0:T(8,128)(2,1)S(1)}, bf16[16,4096]{1,0:T(8,128)(2,1)S(1)}, u32[]{:S(2)}, u32[]{:S(2)}) collective-permute-start(bf16[16,4096]{1,0:T(8,128)(2,1)S(1)} %get-tuple-element.15), channel_id=1, source_target_pairs={{1,0},{2,1},{3,2},{4,3},{5,4},{6,5},{7,6},{8,7},{9,8},{10,9},{11,1... | collective-permute-start | bytes 393224 | tf_op jit(solution)/shard_map/ppermute | solution.py:423
  2.3 3.0 %collective-permute-start = (bf16[16,4096]{1,0:T(8,128)(2,1)S(1)}, bf16[16,4096]{1,0:T(8,128)(2,1)S(1)}, u32[]{:S(2)}, u32[]{:S(2)}) collective-permute-start(bf16[16,4096]{1,0:T(8,128)(2,1)S(1)} %get-tuple-element.16), channel_id=1, source_target_pairs={{0,1},{1,2},{2,3},{3,4},{4,5},{5,6},{6,7},{7,8},{8,9},{9,10},{10,1... | collective-permute-start | bytes 393224 | tf_op jit(solution)/shard_map/ppermute | solution.py:422
  5.3 4.5 %own_spectra.1 = (f32[16,2,128,128]{3,2,1,0:T(8,128)S(1)}, f32[16,33,128]{2,1,0:T(8,128)S(1)}, f32[16,17,128]{2,1,0:T(8,128)S(1)}, f32[48,256]{1,0:T(8,128)S(1)}, bf16[1024,256]{1,0:T(8,128)(2,1)S(1)}) custom-call(bf16[128,4096]{1,0:T(8,128)(2,1)} %bitcast.10, f32[33,2048]{1,0:T(8,128)} %taps_hbm.1, f32[48,256]{1,0:T(8,128)} %constant.8.clone.small_hbm, ...), custom_call_target="tpu_custom_call" | custom-call | tf_op jit(solution)/shard_map/own_spectra/pallas_call | solution.py:425
  9.9 0.0 collective-permute-done.1.right_ref
  9.9 0.0 collective-permute-done.left_ref
  9.9 0.0 copy-done.3
  9.9 7.0 %whiten.1 = bf16[4096,128]{1,0:T(8,128)(2,1)S(1)} custom-call(s32[32]{0:T(128)S(1)} %copy-done.3, f32[16,2,128,128]{3,2,1,0:T(8,128)S(1)} %get-tuple-element.10.own_ref, bf16[16,4096]{1,0:T(8,128)(2,1)S(1)} %collective-permute-done.left_ref, bf16[16,4096]{1,0:T(8,128)(2,1)S(1)} %collective-permute-done.1.right_ref, ...), custom_call_target="tpu_custom_call" | custom-call | tf_op jit(solution)/shard_map/whiten/pallas_call | solution.py:448
  16.9 0.0 copy-start.1
  16.9 0.0 copy-start.2
  16.9 38.0 %all_to_all.10.band_ref = bf16[32,128,128]{2,1,0:T(8,128)(2,1)S(1)} all-to-all(bf16[32,128,128]{2,1,0:T(8,128)(2,1)S(1)} %bitcast.7), channel_id=1, replica_groups=mesh['group'=4,'shard'=8] {'group','shard'}, dimensions={0} | all-to-all | bytes 2097152 | tf_op jit(solution)/shard_map/all_to_all | solution.py:470
  54.9 0.0 collective-permute-start.2
  54.9 0.0 copy-done.1
  54.9 0.0 copy-done.2
  54.9 2.5 %pairs_own_part.1.refs_0_ = f32[32,112,128]{2,1,0:T(8,128)S(1)} custom-call(s32[2,128]{1,0:T(2,128)S(1)} %bitcast.8, bf16[32,128,128]{2,1,0:T(8,128)(2,1)S(1)} %all_to_all.10.band_ref, bf16[2,56,128]{2,1,0:T(8,128)(2,1)S(1)} %copy-done.1), custom_call_target="tpu_custom_call" | custom-call | tf_op jit(solution)/shard_map/pairs_own_part/pallas_call | solution.py:480
  57.4 0.0 copy-start
  57.4 0.0 copy-start.4
  57.4 0.1 collective-permute-done.2.band_ref
  57.6 2.6 %pairs_other_part.1 = bf16[32,112,128]{2,1,0:T(8,128)(2,1)S(1)} custom-call(s32[2,128]{1,0:T(2,128)S(1)} %bitcast.9, bf16[32,128,128]{2,1,0:T(8,128)(2,1)S(1)} %collective-permute-done.2.band_ref, bf16[2,56,128]{2,1,0:T(8,128)(2,1)S(1)} %copy-done.1, f32[32,112,128]{2,1,0:T(8,128)S(1)} %pairs_own_part.1.refs_0_), custom_call_target="tpu_custom_call" | custom-call | tf_op jit(solution)/shard_map/pairs_other_part/pallas_call | solution.py:480
  60.1 26.8 %all_to_all.11.parts_ref = bf16[32,112,128]{2,1,0:T(8,128)(2,1)S(1)} all-to-all(bf16[32,112,128]{2,1,0:T(8,128)(2,1)S(1)} %pairs_other_part.1), channel_id=1, replica_groups=mesh['group'=4,'shard'=8] {'group','shard'}, dimensions={0} | all-to-all | bytes 1835008 | tf_op jit(solution)/shard_map/all_to_all | solution.py:498
  87.0 0.0 copy-done
  87.0 0.0 copy-done.4
  87.0 2.3 %lags.1 = f32[4,128,512]{2,1,0:T(8,128)} custom-call(s32[4]{0:T(128)S(1)} %copy-done.4, bf16[32,112,128]{2,1,0:T(8,128)(2,1)S(1)} %all_to_all.11.parts_ref, bf16[512,896]{1,0:T(8,128)(2,1)S(1)} %copy-done), custom_call_target="tpu_custom_call" | custom-call | tf_op jit(solution)/shard_map/lags/pallas_call | solution.py:500
Async XLA Ops:
  0.0 9.9 %copy-start.3 = (s32[32]{0:T(128)S(1)}, s32[32]{0:T(128)}, u32[]{:S(2)}) copy-start(s32[32]{0:T(128)} %offset_ref.1) | copy-start | bytes 388
  1.0 8.9 %collective-permute-start.1 = (bf16[16,4096]{1,0:T(8,128)(2,1)S(1)}, bf16[16,4096]{1,0:T(8,128)(2,1)S(1)}, u32[]{:S(2)}, u32[]{:S(2)}) collective-permute-start(bf16[16,4096]{1,0:T(8,128)(2,1)S(1)} %get-tuple-element.15), channel_id=1, source_target_pairs={{1,0},{2,1},{3,2},{4,3},{5,4},{6,5},{7,6},{8,7},{9,8},{10,9},{11,1... | collective-permute-start | bytes 393224 | tf_op jit(solution)/shard_map/ppermute | solution.py:423
  2.3 7.6 %collective-permute-start = (bf16[16,4096]{1,0:T(8,128)(2,1)S(1)}, bf16[16,4096]{1,0:T(8,128)(2,1)S(1)}, u32[]{:S(2)}, u32[]{:S(2)}) collective-permute-start(bf16[16,4096]{1,0:T(8,128)(2,1)S(1)} %get-tuple-element.16), channel_id=1, source_target_pairs={{0,1},{1,2},{2,3},{3,4},{4,5},{5,6},{6,7},{7,8},{8,9},{9,10},{10,1... | collective-permute-start | bytes 393224 | tf_op jit(solution)/shard_map/ppermute | solution.py:422
  16.9 38.0 %copy-start.1 = (bf16[2,56,128]{2,1,0:T(8,128)(2,1)S(1)}, bf16[2,56,128]{2,1,0:T(8,128)(2,1)}, u32[]{:S(2)}) copy-start(bf16[2,56,128]{2,1,0:T(8,128)(2,1)} %constant.10.clone.basis_ref) | copy-start | bytes 86020
  16.9 38.0 %copy-start.2 = (s32[128,2]{0,1:T(2,128)S(1)}, s32[128,2]{0,1:T(2,128)}, u32[]{:S(2)}) copy-start(s32[128,2]{0,1:T(2,128)} %param.11) | copy-start | bytes 3076
  54.9 2.7 %collective-permute-start.2 = (bf16[32,128,128]{2,1,0:T(8,128)(2,1)S(1)}, bf16[32,128,128]{2,1,0:T(8,128)(2,1)S(1)}, u32[]{:S(2)}, u32[]{:S(2)}) collective-permute-start(bf16[32,128,128]{2,1,0:T(8,128)(2,1)S(1)} %all_to_all.10.band_ref), channel_id=1, source_target_pairs={{0,1},{1,0},{2,3},{3,2},{4,5},{5,4},{6,7},{7,6},{8,9},{9,8},{10,11... | collective-permute-start | bytes 3145736 | tf_op jit(solution)/shard_map/ppermute | solution.py:473
  57.4 29.6 %copy-start = (bf16[512,896]{1,0:T(8,128)(2,1)S(1)}, bf16[512,896]{1,0:T(8,128)(2,1)}, u32[]{:S(2)}) copy-start(bf16[512,896]{1,0:T(8,128)(2,1)} %constant.11.clone.table_ref) | copy-start | bytes 2752516
  57.4 29.5 %copy-start.4 = (s32[4]{0:T(128)S(1)}, s32[4]{0:T(128)}, u32[]{:S(2)}) copy-start(s32[4]{0:T(128)} %valid_ref.1) | copy-start | bytes 52

commit v5 on v4

--- a/solution.py
+++ b/solution.py
@@ -145,12 +145,14 @@
     slots = (z0_ref, z1_ref)
     copies = [pltpu.make_async_copy(taps_hbm, taps_ref, sem_ref.at[0])]
     copies.append(pltpu.make_async_copy(small_hbm, small_ref, sem_ref.at[1]))
-    copies.append(pltpu.make_async_copy(table_hbm, table_ref, sem_ref.at[2]))
     for i in range(steps):
-        part = pl.ds(i * chunk, chunk)
-        copies.append(pltpu.make_async_copy(x_hbm.at[part], x_ref.at[part], sem_ref.at[3 + i]))
-    for copy in copies:
+        rows = pl.ds(i * chunk, chunk)
+        copies.append(pltpu.make_async_copy(x_hbm.at[rows], x_ref.at[rows], sem_ref.at[3 + i]))
+    table_copy = pltpu.make_async_copy(table_hbm, table_ref, sem_ref.at[2])
+    for i, copy in enumerate(copies):
         copy.start()
+        if i == 2:
+            table_copy.start()
 
     copies[0].wait()
     count = taps_ref.shape[0]
@@ -169,12 +171,13 @@
         both_ref[q, HALF : HALF + 1, :] = taps[count - 1 :]
 
     copies[1].wait()
-    copies[3].wait()
+
+    copies[2].wait()
     transform_rows(x_ref, 0, chunk, small_ref, z0_ref)
-    copies[2].wait()
+    table_copy.wait()
     for i in range(steps):
         if i + 1 < steps:
-            copies[4 + i].wait()
+            copies[3 + i].wait()
             transform_rows(x_ref, (i + 1) * chunk, chunk, small_ref, slots[(i + 1) % 2])
         values = transform_inner(slots[i % 2][...], table_ref)
         for q in range(RADIX):
@@ -255,7 +258,9 @@
     bins = lax.broadcasted_iota(jnp.int32, (RADIX, 128), 1) * RADIX + lax.broadcasted_iota(
         jnp.int32, (RADIX, 128), 0
     )
-    phases = lax.rem(bins * offset_ref[lax.axis_index(AXES)], length).astype(F32) * (2.0 * np.pi / length)
+    place = lax.broadcasted_iota(jnp.int32, offset_ref.shape, 1)
+    offset = jnp.sum(jnp.where(place == lax.axis_index(AXES), offset_ref[...], 0), axis=1, keepdims=True)
+    phases = lax.rem(bins * offset, length).astype(F32) * (2.0 * np.pi / length)
     cosine, sine = jnp.cos(phases), jnp.sin(phases)
     pitch = 2 * RADIX + 1
     for q in range(RADIX):
@@ -276,11 +281,14 @@
         out_ref[2 * RADIX * m : 2 * RADIX * (m + 1), :] = rows.astype(BF16)
 
 
-def pair_kernel(slots, mine, pairs_ref, band_ref, basis_ref, *refs):
+def pair_kernel(slots, mine, pairs_hbm, band_ref, basis_ref, *refs):
     if mine:
-        before_ref, (out_ref, left_ref, right_ref, cross0_ref, cross1_ref) = None, refs
+        before_ref = None
     else:
-        before_ref, out_ref, left_ref, right_ref, cross0_ref, cross1_ref = refs
+        before_ref, refs = refs[0], refs[1:]
+    out_ref, left_ref, right_ref, cross0_ref, cross1_ref, pairs_ref, sem_ref = refs
+    copy = pltpu.make_async_copy(pairs_hbm, pairs_ref, sem_ref.at[0])
+    copy.start()
     blocks = band_ref.shape[0]
     groups = band_ref.shape[1] // (2 * RADIX)
     deep = basis_ref.shape[1]
@@ -297,6 +305,7 @@
         return carry
 
     lax.fori_loop(0, blocks // 8, spread, 0)
+    copy.wait()
 
     def products(i, cross_ref):
         for n in range(step * kept):
@@ -355,7 +364,8 @@
         for n in range(NLAG // 128):
             result = jnp.dot(table_ref[128 * n : 128 * n + 128, :], columns, preferred_element_type=F32)
             for j in range(2):
-                turned = result[:, 128 * j : 128 * j + 128].T * (valid_ref[first + j].astype(F32) * scale)
+                weight = valid_ref[:, first + j : first + j + 1].astype(F32) * scale
+                turned = result[:, 128 * j : 128 * j + 128].T * weight
                 half = turned.shape[0] // 2
                 at = (first + j) * (NLAG // 128) + n
                 for high in range(2):
@@ -373,10 +383,6 @@
 
 def vmem():
     return pl.BlockSpec(memory_space=pltpu.VMEM)
-
-
-def smem():
-    return pl.BlockSpec(memory_space=pltpu.SMEM)
 
 
 def params():
@@ -448,7 +454,7 @@
     rows = pl.pallas_call(
         functools.partial(whiten_kernel, length),
         out_shape=pltpu.VMEM((2 * bin_count, width), BF16),
-        in_specs=[smem()] + [vmem()] * 7,
+        in_specs=[vmem()] * 8,
         out_specs=vmem(),
         scratch_shapes=[
             pltpu.VMEM((2 * HALF, length), BF16),
@@ -465,14 +471,14 @@
         ],
         compiler_params=params(),
         name="whiten",
-    )(coil_offsets, near(own), near(left), near(right), near(small), near(table), near(taps), near(both))
+    )(near(coil_offsets.reshape(1, -1)), near(own), near(left), near(right), near(small), near(table), near(taps), near(both))
 
     band = lax.all_to_all(
         rows.reshape(devices, 2 * bins_device, width), AXES, split_axis=0, concat_axis=0, tiled=True
     )
     other = lax.ppermute(band, "shard", [(i, i ^ 1) for i in range(shards)])
 
-    pairs = pair_blocks.T
+    pairs = distant(pair_blocks.T)
     project = near(jnp.asarray(project))
     sums = (devices, slots // 2 * deep, width)
 
@@ -480,13 +486,15 @@
         return pl.pallas_call(
             functools.partial(pair_kernel, slots, mine),
             out_shape=pltpu.VMEM(sums, F32 if mine else BF16),
-            in_specs=[smem()] + [vmem()] * (2 + len(before)),
+            in_specs=[far()] + [vmem()] * (2 + len(before)),
             out_specs=vmem(),
             scratch_shapes=[
                 pltpu.VMEM((devices, 2 * bins_device, width), F32),
                 pltpu.VMEM((devices, 2 * bins_device, width), F32),
                 pltpu.VMEM((2 * bins_device, 4 * slots * width), BF16),
                 pltpu.VMEM((2 * bins_device, 4 * slots * width), BF16),
+                pltpu.SMEM(pairs.shape, jnp.int32),
+                pltpu.SemaphoreType.DMA((1,)),
             ],
             compiler_params=params(),
             name="pairs_own_part" if mine else "pairs_other_part",
@@ -500,7 +508,7 @@
     return pl.pallas_call(
         functools.partial(lag_kernel, slots, float(1.0 / np.sqrt(bin_count * samples.shape[1]))),
         out_shape=jax.ShapeDtypeStruct((slots, width, NLAG), F32),
-        in_specs=[smem(), vmem(), vmem()],
+        in_specs=[vmem()] * 3,
         out_specs=pl.BlockSpec(memory_space=pl.ANY),
         scratch_shapes=[
             pltpu.VMEM((devices // 2 * deep, slots * width), F32),
@@ -509,7 +517,7 @@
         ],
         compiler_params=params(),
         name="lags",
-    )(pair_valid, near(owned), near(jnp.asarray(lag_table)))
+    )(near(pair_valid.reshape(1, -1)), near(owned), near(jnp.asarray(lag_table)))
 
 
 def solution(mesh):

time: 89.5 us -> 88 us (0.983)
  Pallas kernels: 18.8 us -> 16.9 us
where the time goes in v5:
time: 88 us; the launch traced here: 87.7 us
  blocking collectives  64.8 us (74%)
  Pallas kernels  16.9 us (19%)
  starting transfers between devices  4.33 us (5%)
  local copies, waits for them, and re-layouts  1.02 us (1%)
    all_to_all x1, blocking collectives, body(): lax.all_to_all(rows.reshape(devices, 2 * bins_device, width), AXES, split...  38 us
    all_to_all x1, blocking collectives, body(): owned = lax.all_to_all(parts, AXES, split_axis=0, concat_axis=0, tiled=True)  26.8 us
    pallas_call x1, Pallas kernels, body(): pl.pallas_call(functools.partial(whiten_kernel, length), out_shape=pltpu....  6.36 us
    pallas_call x1, Pallas kernels, body(): pl.pallas_call(own_kernel, out_shape=(pltpu.VMEM((RADIX, 2, width, lanes)...  4.52 us
    pallas_call x2, Pallas kernels, products(): pl.pallas_call(functools.partial(pair_kernel, slots, mine), out_shape=plt...  4.25 us
    ppermute x1, starting transfers between devices, body(): lax.ppermute(x[width - HALF:], AXES, [(i, i + 1) for i in range(ends)])  3.04 us
    pallas_call x1, Pallas kernels, body(): pl.pallas_call(functools.partial(lag_kernel, slots, float(1.0 / np.sqrt(b...  1.78 us
  transfers between devices with their start and end apart: 3, of which 1 were waited for; matrix products, arithmetic and copies ran while one was open for 0% of the time, Pallas kernels for 8%

profile of v5, /device:TPU:0, one launch (start us, length us, event | category | flops | bytes accessed | tf_op | source)
XLA Modules:
  0.0 87.7 jit_solution(2603716473308630014)
XLA Ops:
  0.0 0.0 copy-start.2
  0.0 1.0 %slice_bitcast_fusion = (bf16[16,4096]{1,0:T(8,128)(2,1)S(1)}, bf16[16,4096]{1,0:T(8,128)(2,1)S(1)}) fusion(bf16[128,1,4096]{2,0,1:T(8,128)(2,1)} %param.9), kind=kLoop, calls=%fused_computation | loop fusion | bytes 524288 | tf_op jit(solution)/shard_map/slice | solution.py:429
  1.0 1.3 %collective-permute-start.1 = (bf16[16,4096]{1,0:T(8,128)(2,1)S(1)}, bf16[16,4096]{1,0:T(8,128)(2,1)S(1)}, u32[]{:S(2)}, u32[]{:S(2)}) collective-permute-start(bf16[16,4096]{1,0:T(8,128)(2,1)S(1)} %get-tuple-element.15), channel_id=1, source_target_pairs={{1,0},{2,1},{3,2},{4,3},{5,4},{6,5},{7,6},{8,7},{9,8},{10,9},{11,1... | collective-permute-start | bytes 393224 | tf_op jit(solution)/shard_map/ppermute | solution.py:429
  2.3 3.0 %collective-permute-start = (bf16[16,4096]{1,0:T(8,128)(2,1)S(1)}, bf16[16,4096]{1,0:T(8,128)(2,1)S(1)}, u32[]{:S(2)}, u32[]{:S(2)}) collective-permute-start(bf16[16,4096]{1,0:T(8,128)(2,1)S(1)} %get-tuple-element.16), channel_id=1, source_target_pairs={{0,1},{1,2},{2,3},{3,4},{4,5},{5,6},{6,7},{7,8},{8,9},{9,10},{10,1... | collective-permute-start | bytes 393224 | tf_op jit(solution)/shard_map/ppermute | solution.py:428
  5.3 4.5 %own_spectra.1 = (f32[16,2,128,128]{3,2,1,0:T(8,128)S(1)}, f32[16,33,128]{2,1,0:T(8,128)S(1)}, f32[16,17,128]{2,1,0:T(8,128)S(1)}, f32[48,256]{1,0:T(8,128)S(1)}, bf16[1024,256]{1,0:T(8,128)(2,1)S(1)}) custom-call(bf16[128,4096]{1,0:T(8,128)(2,1)} %bitcast.12, f32[33,2048]{1,0:T(8,128)} %taps_hbm.1, f32[48,256]{1,0:T(8,128)} %constant.8.clone.small_hbm, ...), custom_call_target="tpu_custom_call" | custom-call | tf_op jit(solution)/shard_map/own_spectra/pallas_call | solution.py:431
  9.9 0.0 collective-permute-done.1.right_ref
  9.9 0.0 collective-permute-done.left_ref
  9.9 0.0 copy-done.2
  9.9 6.4 %whiten.1 = bf16[4096,128]{1,0:T(8,128)(2,1)S(1)} custom-call(s32[1,32]{1,0:T(1,128)S(1)} %bitcast.10, f32[16,2,128,128]{3,2,1,0:T(8,128)S(1)} %get-tuple-element.10.own_ref, bf16[16,4096]{1,0:T(8,128)(2,1)S(1)} %collective-permute-done.left_ref, bf16[16,4096]{1,0:T(8,128)(2,1)S(1)} %collective-permute-done.1.right_ref, ...), custom_call_target="tpu_custom_call" | custom-call | tf_op jit(solution)/shard_map/whiten/pallas_call | solution.py:454
  16.3 0.0 copy-start.1
  16.3 38.0 %all_to_all.10.band_ref = bf16[32,128,128]{2,1,0:T(8,128)(2,1)S(1)} all-to-all(bf16[32,128,128]{2,1,0:T(8,128)(2,1)S(1)} %bitcast.9), channel_id=1, replica_groups=mesh['group'=4,'shard'=8] {'group','shard'}, dimensions={0} | all-to-all | bytes 2097152 | tf_op jit(solution)/shard_map/all_to_all | solution.py:476
  54.3 0.0 collective-permute-start.2
  54.3 0.0 copy-done.1
  54.3 2.1 %pairs_own_part.1.refs_0_ = f32[32,112,128]{2,1,0:T(8,128)S(1)} custom-call(s32[2,128]{1,0:T(2,128)} %bitcast.13, bf16[32,128,128]{2,1,0:T(8,128)(2,1)S(1)} %all_to_all.10.band_ref, bf16[2,56,128]{2,1,0:T(8,128)(2,1)S(1)} %copy-done.1), custom_call_target="tpu_custom_call" | custom-call | tf_op jit(solution)/shard_map/pairs_own_part/pallas_call | solution.py:486
  56.4 0.0 copy-start
  56.4 0.0 copy-start.3
  56.4 0.6 collective-permute-done.2.band_ref
  57.0 2.2 %pairs_other_part.1 = bf16[32,112,128]{2,1,0:T(8,128)(2,1)S(1)} custom-call(s32[2,128]{1,0:T(2,128)} %bitcast.14, bf16[32,128,128]{2,1,0:T(8,128)(2,1)S(1)} %collective-permute-done.2.band_ref, bf16[2,56,128]{2,1,0:T(8,128)(2,1)S(1)} %copy-done.1, f32[32,112,128]{2,1,0:T(8,128)S(1)} %pairs_own_part.1.refs_0_), custom_call_target="tpu_custom_call" | custom-call | tf_op jit(solution)/shard_map/pairs_other_part/pallas_call | solution.py:486
  59.1 26.8 %all_to_all.11.parts_ref = bf16[32,112,128]{2,1,0:T(8,128)(2,1)S(1)} all-to-all(bf16[32,112,128]{2,1,0:T(8,128)(2,1)S(1)} %pairs_other_part.1), channel_id=1, replica_groups=mesh['group'=4,'shard'=8] {'group','shard'}, dimensions={0} | all-to-all | bytes 1835008 | tf_op jit(solution)/shard_map/all_to_all | solution.py:506
  85.9 0.0 copy-done
  85.9 0.0 copy-done.3
  85.9 1.8 %lags.1 = f32[4,128,512]{2,1,0:T(8,128)} custom-call(s32[1,4]{1,0:T(1,128)S(1)} %bitcast.11, bf16[32,112,128]{2,1,0:T(8,128)(2,1)S(1)} %all_to_all.11.parts_ref, bf16[512,896]{1,0:T(8,128)(2,1)S(1)} %copy-done), custom_call_target="tpu_custom_call" | custom-call | tf_op jit(solution)/shard_map/lags/pallas_call | solution.py:508
Async XLA Ops:
  0.0 9.9 %copy-start.2 = (s32[32]{0:T(128)S(1)}, s32[32]{0:T(128)}, u32[]{:S(2)}) copy-start(s32[32]{0:T(128)} %param.13) | copy-start | bytes 388
  1.0 8.9 %collective-permute-start.1 = (bf16[16,4096]{1,0:T(8,128)(2,1)S(1)}, bf16[16,4096]{1,0:T(8,128)(2,1)S(1)}, u32[]{:S(2)}, u32[]{:S(2)}) collective-permute-start(bf16[16,4096]{1,0:T(8,128)(2,1)S(1)} %get-tuple-element.15), channel_id=1, source_target_pairs={{1,0},{2,1},{3,2},{4,3},{5,4},{6,5},{7,6},{8,7},{9,8},{10,9},{11,1... | collective-permute-start | bytes 393224 | tf_op jit(solution)/shard_map/ppermute | solution.py:429
  2.3 7.6 %collective-permute-start = (bf16[16,4096]{1,0:T(8,128)(2,1)S(1)}, bf16[16,4096]{1,0:T(8,128)(2,1)S(1)}, u32[]{:S(2)}, u32[]{:S(2)}) collective-permute-start(bf16[16,4096]{1,0:T(8,128)(2,1)S(1)} %get-tuple-element.16), channel_id=1, source_target_pairs={{0,1},{1,2},{2,3},{3,4},{4,5},{5,6},{6,7},{7,8},{8,9},{9,10},{10,1... | collective-permute-start | bytes 393224 | tf_op jit(solution)/shard_map/ppermute | solution.py:428
  16.3 38.0 %copy-start.1 = (bf16[2,56,128]{2,1,0:T(8,128)(2,1)S(1)}, bf16[2,56,128]{2,1,0:T(8,128)(2,1)}, u32[]{:S(2)}) copy-start(bf16[2,56,128]{2,1,0:T(8,128)(2,1)} %constant.10.clone.basis_ref) | copy-start | bytes 86020
  54.3 2.7 %collective-permute-start.2 = (bf16[32,128,128]{2,1,0:T(8,128)(2,1)S(1)}, bf16[32,128,128]{2,1,0:T(8,128)(2,1)S(1)}, u32[]{:S(2)}, u32[]{:S(2)}) collective-permute-start(bf16[32,128,128]{2,1,0:T(8,128)(2,1)S(1)} %all_to_all.10.band_ref), channel_id=1, source_target_pairs={{0,1},{1,0},{2,3},{3,2},{4,5},{5,4},{6,7},{7,6},{8,9},{9,8},{10,11... | collective-permute-start | bytes 3145736 | tf_op jit(solution)/shard_map/ppermute | solution.py:479
  56.4 29.6 %copy-start = (bf16[512,896]{1,0:T(8,128)(2,1)S(1)}, bf16[512,896]{1,0:T(8,128)(2,1)}, u32[]{:S(2)}) copy-start(bf16[512,896]{1,0:T(8,128)(2,1)} %constant.11.clone.table_ref) | copy-start | bytes 2752516
  56.4 29.6 %copy-start.3 = (s32[4]{0:T(128)S(1)}, s32[4]{0:T(128)}, u32[]{:S(2)}) copy-start(s32[4]{0:T(128)} %param.12) | copy-start | bytes 52

commit v6 on v5

--- a/solution.py
+++ b/solution.py
@@ -186,13 +186,14 @@
 
 
 def whiten_kernel(
-    length, offset_ref, own_ref, left_ref, right_ref, small_ref, table_ref, taps_ref, both_ref, out_ref,
-    x_ref, z_ref, halo_ref, even_ref, odd_ref, pair_ref, part_ref, filtered_ref, power_ref, base_ref, rows_ref,
+    length, offset_ref, own_ref, next_ref, small_ref, table_ref, taps_ref, both_ref, out_ref,
+    z_ref, halo_ref, even_ref, odd_ref, pair_ref, part_ref, filtered_ref, power_ref, base_ref, rows_ref,
 ):
     width = own_ref.shape[2]
-    x_ref[0:HALF, :] = left_ref[...]
-    x_ref[HALF:, :] = right_ref[...]
-    transform_rows(x_ref, 0, 2 * HALF, small_ref, z_ref)
+    device = lax.axis_index(AXES)
+    devices = offset_ref.shape[1]
+    inside = jnp.where(device == devices - 1, 0.0, 1.0)
+    transform_rows(next_ref, 0, 2 * HALF, small_ref, z_ref)
     values = transform_inner(z_ref[...], table_ref)
     halo_ref[0] = values[:, :128]
     halo_ref[1] = values[:, 128:]
@@ -200,9 +201,10 @@
     power_ref[0] = jnp.zeros(power_ref.shape[1:], F32)
 
     half = width // 2
-    count = half + HALF
     edge = HALF // 2
-    even_ref[:, count:, :] = jnp.zeros((2, even_ref.shape[1] - count, 128), F32)
+    main = half - edge
+    even_tail, odd_tail = main + 3 * edge, main + 2 * edge
+    zeros = jnp.zeros((edge, 128), F32)
 
     def placed(values, parity):
         quarter = half // 2
@@ -214,22 +216,33 @@
         at = pl.multiple_of(q * 2 * HALF, 2 * HALF)
         total = [None, None]
         for r in range(2):
-            for first, ref in ((0, even_ref), (1, odd_ref)):
-                ref[r, 0:edge, :] = halo_ref[r, pl.ds(at + first, edge, stride=2), :]
-                ref[r, edge : edge + half, :] = own_ref[q, r, pl.ds(first, half, stride=2), :]
-                ref[r, edge + half : count, :] = halo_ref[r, pl.ds(at + HALF + first, edge, stride=2), :]
-            pair_ref[r] = odd_ref[r] + even_ref[r, 1 : count + 1, :]
-            evens = jnp.zeros((half + 8, 128), F32)
-            odds = jnp.zeros((half, 128), F32)
-            pairs = jnp.zeros((half, 128), F32)
-            for u in range(HALF + 1):
-                evens = evens + taps_ref[q, 2 * u : 2 * u + 1, :] * even_ref[r, u : u + half + 8, :]
-            part_ref[r] = evens
-            for u in range(HALF):
-                odds = odds + taps_ref[q, 2 * u + 1 : 2 * u + 2, :] * odd_ref[r, u : u + half, :]
-            for u in range(HALF + 1):
-                pairs = pairs + both_ref[q, u : u + 1, :] * pair_ref[r, u : u + half, :]
-            result = (evens[:half] + odds, pairs - (part_ref[r, 1 : half + 1, :] + odds))
+            for first, ref, tail in ((0, even_ref, even_tail), (1, odd_ref, odd_tail)):
+                last = own_ref[q, r, pl.ds(2 * main + first, edge, stride=2), :]
+                after = halo_ref[r, pl.ds(at + first, 2 * edge, stride=2), :]
+                ref[r, 0:main, :] = own_ref[q, r, pl.ds(first, main, stride=2), :]
+                ref[r, main : main + edge, :] = last
+                ref[r, main + edge : main + 2 * edge, :] = after[:edge] * inside
+                ref[r, tail : tail + edge, :] = last * inside
+                ref[r, tail + edge : tail + 3 * edge, :] = after
+            even_ref[r, main + 2 * edge : even_tail, :] = zeros
+            even_ref[r, even_tail + 3 * edge :, :] = zeros
+            pair_ref[r, 0:odd_tail, :] = odd_ref[r, 0:odd_tail, :] + even_ref[r, 1 : odd_tail + 1, :]
+            pair_ref[r, odd_tail:, :] = odd_ref[r, odd_tail:, :] + even_ref[r, even_tail + 1 : even_tail + 3 * edge + 1, :]
+            result = ([], [])
+            for rows, even, odd in ((main, 0, 0), (edge, even_tail, odd_tail)):
+                evens = jnp.zeros((rows + 8, 128), F32)
+                odds = jnp.zeros((rows, 128), F32)
+                pairs = jnp.zeros((rows, 128), F32)
+                for u in range(HALF + 1):
+                    evens = evens + taps_ref[q, 2 * u : 2 * u + 1, :] * even_ref[r, even + u : even + u + rows + 8, :]
+                part_ref[r, 0 : rows + 8, :] = evens
+                for u in range(HALF):
+                    odds = odds + taps_ref[q, 2 * u + 1 : 2 * u + 2, :] * odd_ref[r, odd + u : odd + u + rows, :]
+                for u in range(HALF + 1):
+                    pairs = pairs + both_ref[q, u : u + 1, :] * pair_ref[r, odd + u : odd + u + rows, :]
+                result[0].append(evens[:rows] + odds)
+                result[1].append(pairs - (part_ref[r, 1 : rows + 1, :] + odds))
+            result = [jnp.concatenate(parts, axis=0) for parts in result]
             for n in range(2):
                 for rows, values in placed(result[n], n):
                     filtered_ref[q, r, rows, :] = values
@@ -259,9 +272,19 @@
         jnp.int32, (RADIX, 128), 0
     )
     place = lax.broadcasted_iota(jnp.int32, offset_ref.shape, 1)
-    offset = jnp.sum(jnp.where(place == lax.axis_index(AXES), offset_ref[...], 0), axis=1, keepdims=True)
-    phases = lax.rem(bins * offset, length).astype(F32) * (2.0 * np.pi / length)
-    cosine, sine = jnp.cos(phases), jnp.sin(phases)
+    turns = []
+    for block in (device, lax.rem(device + 1, devices)):
+        offset = jnp.sum(jnp.where(place == block, offset_ref[...], 0), axis=1, keepdims=True)
+        phases = lax.rem(bins * offset, length).astype(F32) * (2.0 * np.pi / length)
+        turns.append((jnp.cos(phases), jnp.sin(phases)))
+
+    def by_row(part, q):
+        mine, its = turns[0][part][q : q + 1, :], turns[1][part][q : q + 1, :]
+        sizes = (half + half // 2 - edge, edge, half // 2 - edge, edge)
+        return jnp.concatenate(
+            [jnp.broadcast_to(its if n % 2 else mine, (size, 128)) for n, size in enumerate(sizes)], axis=0
+        )
+
     pitch = 2 * RADIX + 1
     for q in range(RADIX):
         window = (
@@ -271,7 +294,7 @@
         )
         scale = lax.rsqrt(window * small_ref[2 * RADIX + q : 2 * RADIX + q + 1, 0:128] + EPSILON)
         fr, fi = filtered_ref[q, 0], filtered_ref[q, 1]
-        c, s = cosine[q : q + 1, :], sine[q : q + 1, :]
+        c, s = by_row(0, q), by_row(1, q)
         wr = (fr * c + fi * s) * scale
         wi = (fi * c - fr * s) * scale
         rows_ref[pl.ds(q, 128, stride=pitch), :] = wr.T
@@ -297,11 +320,17 @@
     kept = slots // 2
     step = cross0_ref.shape[1] // (128 * kept)
 
+    lane = lax.broadcasted_iota(jnp.int32, band_ref.shape[1:], 1)
+    from_before = (lane >= 64) & (lax.rem(lane, 32) >= 32 - HALF // 2)
+
     def spread(i, carry):
+        before = band_ref[lax.rem(8 * i + blocks - 1, blocks)].astype(F32)
         for n in range(8):
             values = band_ref[8 * i + n].astype(F32)
-            left_ref[8 * i + n] = values
-            right_ref[8 * i + n] = pltpu.roll(values, 64, 1)
+            whole = jnp.where(from_before, before, values)
+            left_ref[8 * i + n] = whole
+            right_ref[8 * i + n] = pltpu.roll(whole, 64, 1)
+            before = values
         return carry
 
     lax.fori_loop(0, blocks // 8, spread, 0)
@@ -368,11 +397,15 @@
                 turned = result[:, 128 * j : 128 * j + 128].T * weight
                 half = turned.shape[0] // 2
                 at = (first + j) * (NLAG // 128) + n
-                for high in range(2):
-                    for parity in range(2):
-                        row = half * high + half // 2 * parity
-                        rows = turned[row : row + half // 2]
-                        stage_ref[at, pl.ds(half * high + parity, half // 2, stride=2), :] = rows
+                quarter = half // 2
+                for parity in range(2):
+                    pieces = (
+                        (quarter * parity, HALF, quarter),
+                        (half + quarter * parity, half + HALF, quarter - HALF // 2),
+                        (half + quarter * (parity + 1) - HALF // 2, 0, HALF // 2),
+                    )
+                    for row, channel, count in pieces:
+                        stage_ref[at, pl.ds(channel + parity, count, stride=2), :] = turned[row : row + count]
                 lanes = pl.ds(128 * n, 128)
                 copy = pltpu.make_async_copy(stage_ref.at[at], out_ref.at[first + j, :, lanes], sem_ref.at[at])
                 copy.start()
@@ -424,9 +457,7 @@
     small[2 * RADIX :, :lanes] = (1.0 / counts).reshape(lanes, RADIX).T
 
     x = samples.reshape(width, length)
-    ends = devices - 1
-    left = lax.ppermute(x[width - HALF :], AXES, [(i, i + 1) for i in range(ends)])
-    right = lax.ppermute(x[:HALF], AXES, [(i + 1, i) for i in range(ends)])
+    after = lax.ppermute(x[: 2 * HALF], AXES, [((i + 1) % devices, i) for i in range(devices)])
 
     own, taps, both, small, table = pl.pallas_call(
         own_kernel,
@@ -454,15 +485,14 @@
     rows = pl.pallas_call(
         functools.partial(whiten_kernel, length),
         out_shape=pltpu.VMEM((2 * bin_count, width), BF16),
-        in_specs=[vmem()] * 8,
+        in_specs=[vmem()] * 7,
         out_specs=vmem(),
         scratch_shapes=[
-            pltpu.VMEM((2 * HALF, length), BF16),
             pltpu.VMEM((RADIX * 2 * HALF, 4 * inner), BF16),
             pltpu.VMEM((2, RADIX * 2 * HALF, lanes), F32),
-            pltpu.VMEM((2, width // 2 + HALF + 8, lanes), F32),
-            pltpu.VMEM((2, width // 2 + HALF, lanes), F32),
-            pltpu.VMEM((2, width // 2 + HALF, lanes), F32),
+            pltpu.VMEM((2, width // 2 + 3 * HALF, lanes), F32),
+            pltpu.VMEM((2, width // 2 + 2 * HALF, lanes), F32),
+            pltpu.VMEM((2, width // 2 + 2 * HALF, lanes), F32),
             pltpu.VMEM((2, width // 2 + 8, lanes), F32),
             pltpu.VMEM((RADIX, 2, width, lanes), F32),
             pltpu.VMEM((RADIX + 1, width, lanes), F32),
@@ -471,7 +501,7 @@
         ],
         compiler_params=params(),
         name="whiten",
-    )(near(coil_offsets.reshape(1, -1)), near(own), near(left), near(right), near(small), near(table), near(taps), near(both))
+    )(near(coil_offsets.reshape(1, -1)), near(own), near(after), near(small), near(table), near(taps), near(both))
 
     band = lax.all_to_all(
         rows.reshape(devices, 2 * bins_device, width), AXES, split_axis=0, concat_axis=0, tiled=True

time: 88 us -> 85.4 us (0.970)
  blocking collectives: 64.8 us -> 59.4 us
  starting transfers between devices: 4.33 us -> 6.43 us
    all_to_all x1, blocking collectives: 38 us -> 32.6 us  [body(): lax.all_to_all(rows.reshape(devices, 2 * bins_device, width), AXES, split...]
    ppermute x2 -> x1, starting transfers between devices: 4.33 us -> 6.42 us  [body(): lax.ppermute(x[:2 * HALF], AXES, [((i + 1) % devices, i) for i in range(d...]
  transfers between devices with their start and end apart: 3 -> 2, of which waited for: 1 -> 1; matrix products, arithmetic and copies ran while one was open for 0% -> 0% of each run, Pallas kernels for 8% -> 8%
where the time goes in v6:
time: 85.4 us; the launch traced here: 85.2 us
  blocking collectives  59.4 us (70%)
  Pallas kernels  17.7 us (21%)
  starting transfers between devices  6.43 us (8%)
  local copies, waits for them, and re-layouts  1 us (1%)
    all_to_all x1, blocking collectives, body(): lax.all_to_all(rows.reshape(devices, 2 * bins_device, width), AXES, split...  32.6 us
    all_to_all x1, blocking collectives, body(): owned = lax.all_to_all(parts, AXES, split_axis=0, concat_axis=0, tiled=True)  26.8 us
    pallas_call x1, Pallas kernels, body(): pl.pallas_call(functools.partial(whiten_kernel, length), out_shape=pltpu....  7.16 us
    ppermute x1, starting transfers between devices, body(): lax.ppermute(x[:2 * HALF], AXES, [((i + 1) % devices, i) for i in range(d...  6.42 us
    pallas_call x1, Pallas kernels, body(): pl.pallas_call(own_kernel, out_shape=(pltpu.VMEM((RADIX, 2, width, lanes)...  4.51 us
    pallas_call x2, Pallas kernels, products(): pl.pallas_call(functools.partial(pair_kernel, slots, mine), out_shape=plt...  4.24 us
    pallas_call x1, Pallas kernels, body(): pl.pallas_call(functools.partial(lag_kernel, slots, float(1.0 / np.sqrt(b...  1.78 us
  transfers between devices with their start and end apart: 2, of which 1 were waited for; matrix products, arithmetic and copies ran while one was open for 0% of the time, Pallas kernels for 8%

profile of v6, /device:TPU:0, one launch (start us, length us, event | category | flops | bytes accessed | tf_op | source)
XLA Modules:
  0.0 85.2 jit_solution(3542237128674315487)
XLA Ops:
  0.0 0.0 copy-start.2
  0.0 1.0 %slice_bitcast_fusion = bf16[32,4096]{1,0:T(8,128)(2,1)S(1)} fusion(bf16[128,1,4096]{2,0,1:T(8,128)(2,1)} %param.9), kind=kLoop, calls=%fused_computation | loop fusion | bytes 524288 | tf_op jit(solution)/shard_map/slice | solution.py:460
  1.0 6.4 %collective-permute-start = (bf16[32,4096]{1,0:T(8,128)(2,1)S(1)}, bf16[32,4096]{1,0:T(8,128)(2,1)S(1)}, u32[]{:S(2)}, u32[]{:S(2)}) collective-permute-start(bf16[32,4096]{1,0:T(8,128)(2,1)S(1)} %slice_bitcast_fusion), channel_id=1, source_target_pairs={{1,0},{2,1},{3,2},{4,3},{5,4},{6,5},{7,6},{8,7},{9,8},{10,9},{11,1... | collective-permute-start | bytes 786440 | tf_op jit(solution)/shard_map/ppermute | solution.py:460
  7.4 4.5 %own_spectra.1 = (f32[16,2,128,128]{3,2,1,0:T(8,128)S(1)}, f32[16,33,128]{2,1,0:T(8,128)S(1)}, f32[16,17,128]{2,1,0:T(8,128)S(1)}, f32[48,256]{1,0:T(8,128)S(1)}, bf16[1024,256]{1,0:T(8,128)(2,1)S(1)}) custom-call(bf16[128,4096]{1,0:T(8,128)(2,1)} %bitcast.10, f32[33,2048]{1,0:T(8,128)} %taps_hbm.1, f32[48,256]{1,0:T(8,128)} %constant.8.clone.small_hbm, ...), custom_call_target="tpu_custom_call" | custom-call | tf_op jit(solution)/shard_map/own_spectra/pallas_call | solution.py:462
  11.9 0.0 collective-permute-done.next_ref
  11.9 0.0 copy-done.2
  12.0 7.2 %whiten.1 = bf16[4096,128]{1,0:T(8,128)(2,1)S(1)} custom-call(s32[1,32]{1,0:T(1,128)S(1)} %bitcast.8, f32[16,2,128,128]{3,2,1,0:T(8,128)S(1)} %get-tuple-element.10.own_ref, bf16[32,4096]{1,0:T(8,128)(2,1)S(1)} %collective-permute-done.next_ref, f32[48,256]{1,0:T(8,128)S(1)} %get-tuple-element.11.small_ref, ...), custom_call_target="tpu_custom_call" | custom-call | tf_op jit(solution)/shard_map/whiten/pallas_call | solution.py:485
  19.1 0.0 copy-start.1
  19.1 32.6 %all_to_all.10.band_ref = bf16[32,128,128]{2,1,0:T(8,128)(2,1)S(1)} all-to-all(bf16[32,128,128]{2,1,0:T(8,128)(2,1)S(1)} %bitcast.7), channel_id=1, replica_groups=mesh['group'=4,'shard'=8] {'group','shard'}, dimensions={0} | all-to-all | bytes 2097152 | tf_op jit(solution)/shard_map/all_to_all | solution.py:506
  51.7 0.0 collective-permute-start.1
  51.8 0.0 copy-done.1
  51.8 2.1 %pairs_own_part.1.refs_0_ = f32[32,112,128]{2,1,0:T(8,128)S(1)} custom-call(s32[2,128]{1,0:T(2,128)} %bitcast.11, bf16[32,128,128]{2,1,0:T(8,128)(2,1)S(1)} %all_to_all.10.band_ref, bf16[2,56,128]{2,1,0:T(8,128)(2,1)S(1)} %copy-done.1), custom_call_target="tpu_custom_call" | custom-call | tf_op jit(solution)/shard_map/pairs_own_part/pallas_call | solution.py:516
  53.8 0.0 copy-start
  53.8 0.0 copy-start.3
  53.9 0.6 collective-permute-done.1.band_ref
  54.4 2.2 %pairs_other_part.1 = bf16[32,112,128]{2,1,0:T(8,128)(2,1)S(1)} custom-call(s32[2,128]{1,0:T(2,128)} %bitcast.12, bf16[32,128,128]{2,1,0:T(8,128)(2,1)S(1)} %collective-permute-done.1.band_ref, bf16[2,56,128]{2,1,0:T(8,128)(2,1)S(1)} %copy-done.1, f32[32,112,128]{2,1,0:T(8,128)S(1)} %pairs_own_part.1.refs_0_), custom_call_target="tpu_custom_call" | custom-call | tf_op jit(solution)/shard_map/pairs_other_part/pallas_call | solution.py:516
  56.6 26.8 %all_to_all.11.parts_ref = bf16[32,112,128]{2,1,0:T(8,128)(2,1)S(1)} all-to-all(bf16[32,112,128]{2,1,0:T(8,128)(2,1)S(1)} %pairs_other_part.1), channel_id=1, replica_groups=mesh['group'=4,'shard'=8] {'group','shard'}, dimensions={0} | all-to-all | bytes 1835008 | tf_op jit(solution)/shard_map/all_to_all | solution.py:536
  83.4 0.0 copy-done
  83.4 0.0 copy-done.3
  83.4 1.8 %lags.1 = f32[4,128,512]{2,1,0:T(8,128)} custom-call(s32[1,4]{1,0:T(1,128)S(1)} %bitcast.9, bf16[32,112,128]{2,1,0:T(8,128)(2,1)S(1)} %all_to_all.11.parts_ref, bf16[512,896]{1,0:T(8,128)(2,1)S(1)} %copy-done), custom_call_target="tpu_custom_call" | custom-call | tf_op jit(solution)/shard_map/lags/pallas_call | solution.py:538
Async XLA Ops:
  0.0 11.9 %copy-start.2 = (s32[32]{0:T(128)S(1)}, s32[32]{0:T(128)}, u32[]{:S(2)}) copy-start(s32[32]{0:T(128)} %param.13) | copy-start | bytes 388
  1.0 10.9 %collective-permute-start = (bf16[32,4096]{1,0:T(8,128)(2,1)S(1)}, bf16[32,4096]{1,0:T(8,128)(2,1)S(1)}, u32[]{:S(2)}, u32[]{:S(2)}) collective-permute-start(bf16[32,4096]{1,0:T(8,128)(2,1)S(1)} %slice_bitcast_fusion), channel_id=1, source_target_pairs={{1,0},{2,1},{3,2},{4,3},{5,4},{6,5},{7,6},{8,7},{9,8},{10,9},{11,1... | collective-permute-start | bytes 786440 | tf_op jit(solution)/shard_map/ppermute | solution.py:460
  19.1 32.6 %copy-start.1 = (bf16[2,56,128]{2,1,0:T(8,128)(2,1)S(1)}, bf16[2,56,128]{2,1,0:T(8,128)(2,1)}, u32[]{:S(2)}) copy-start(bf16[2,56,128]{2,1,0:T(8,128)(2,1)} %constant.10.clone.basis_ref) | copy-start | bytes 86020
  51.7 2.7 %collective-permute-start.1 = (bf16[32,128,128]{2,1,0:T(8,128)(2,1)S(1)}, bf16[32,128,128]{2,1,0:T(8,128)(2,1)S(1)}, u32[]{:S(2)}, u32[]{:S(2)}) collective-permute-start(bf16[32,128,128]{2,1,0:T(8,128)(2,1)S(1)} %all_to_all.10.band_ref), channel_id=1, source_target_pairs={{0,1},{1,0},{2,3},{3,2},{4,5},{5,4},{6,7},{7,6},{8,9},{9,8},{10,11... | collective-permute-start | bytes 3145736 | tf_op jit(solution)/shard_map/ppermute | solution.py:509
  53.8 29.6 %copy-start = (bf16[512,896]{1,0:T(8,128)(2,1)S(1)}, bf16[512,896]{1,0:T(8,128)(2,1)}, u32[]{:S(2)}) copy-start(bf16[512,896]{1,0:T(8,128)(2,1)} %constant.11.clone.table_ref) | copy-start | bytes 2752516
  53.8 29.6 %copy-start.3 = (s32[4]{0:T(128)S(1)}, s32[4]{0:T(128)}, u32[]{:S(2)}) copy-start(s32[4]{0:T(128)} %param.12) | copy-start | bytes 52

commit v7 on v6

--- a/solution.py
+++ b/solution.py
@@ -136,9 +136,23 @@
     return out + jnp.dot(z[:, :depth], low, preferred_element_type=F32)
 
 
+def short_filters(taps_ref, both_ref, q, even_ref, odd_ref, pair_ref, part_ref, r, even, odd, rows):
+    evens = jnp.zeros((rows + 8, 128), F32)
+    odds = jnp.zeros((rows, 128), F32)
+    pairs = jnp.zeros((rows, 128), F32)
+    for u in range(HALF + 1):
+        evens = evens + taps_ref[q, 2 * u : 2 * u + 1, :] * even_ref[r, even + u : even + u + rows + 8, :]
+    part_ref[r, 0 : rows + 8, :] = evens
+    for u in range(HALF):
+        odds = odds + taps_ref[q, 2 * u + 1 : 2 * u + 2, :] * odd_ref[r, odd + u : odd + u + rows, :]
+    for u in range(HALF + 1):
+        pairs = pairs + both_ref[q, u : u + 1, :] * pair_ref[r, odd + u : odd + u + rows, :]
+    return evens[:rows] + odds, pairs - (part_ref[r, 1 : rows + 1, :] + odds)
+
+
 def own_kernel(
-    x_hbm, taps_hbm, small_hbm, table_hbm, out_ref, split_ref, both_ref, small_ref, table_ref,
-    x_ref, taps_ref, z0_ref, z1_ref, turned_ref, sem_ref,
+    x_hbm, taps_hbm, small_hbm, table_hbm, out_ref, first_ref, split_ref, both_ref, small_ref, table_ref,
+    x_ref, taps_ref, z0_ref, z1_ref, turned_ref, even_ref, odd_ref, pair_ref, part_ref, sem_ref,
 ):
     chunk = z0_ref.shape[0] // RADIX
     steps = x_ref.shape[0] // chunk
@@ -184,10 +198,29 @@
             out_ref[q, 0, i * chunk : (i + 1) * chunk, :] = values[q * chunk : (q + 1) * chunk, :128]
             out_ref[q, 1, i * chunk : (i + 1) * chunk, :] = values[q * chunk : (q + 1) * chunk, 128:]
 
+    half = x_ref.shape[0] // 2
+    rows = half - HALF
+    quarter = half // 2
+    even_ref[:, half:, :] = jnp.zeros((2, 8, 128), F32)
+
+    def filter_step(q, carry):
+        for r in range(2):
+            even_ref[r, 0:half, :] = out_ref[q, r, pl.ds(0, half, stride=2), :]
+            odd_ref[r] = out_ref[q, r, pl.ds(1, half, stride=2), :]
+            pair_ref[r] = odd_ref[r] + even_ref[r, 1 : half + 1, :]
+            result = short_filters(split_ref, both_ref, q, even_ref, odd_ref, pair_ref, part_ref, r, 0, 0, rows)
+            for parity in range(2):
+                first_ref[q, r, quarter * parity : quarter * (parity + 1), :] = result[parity][:quarter]
+                at = half + quarter * parity
+                first_ref[q, r, at : at + rows - quarter, :] = result[parity][quarter:]
+        return carry
+
+    lax.fori_loop(0, RADIX, filter_step, 0)
+
 
 def whiten_kernel(
-    length, offset_ref, own_ref, next_ref, small_ref, table_ref, taps_ref, both_ref, out_ref,
-    z_ref, halo_ref, even_ref, odd_ref, pair_ref, part_ref, filtered_ref, power_ref, base_ref, rows_ref,
+    length, offset_ref, own_ref, first_ref, next_ref, small_ref, table_ref, taps_ref, both_ref, out_ref,
+    z_ref, halo_ref, even_ref, odd_ref, pair_ref, part_ref, late_ref, power_ref, base_ref, rows_ref,
 ):
     width = own_ref.shape[2]
     device = lax.axis_index(AXES)
@@ -202,55 +235,40 @@
 
     half = width // 2
     edge = HALF // 2
-    main = half - edge
-    even_tail, odd_tail = main + 3 * edge, main + 2 * edge
+    main = half - HALF
     zeros = jnp.zeros((edge, 128), F32)
 
-    def placed(values, parity):
-        quarter = half // 2
-        for high in range(2):
-            first = half * high + quarter * parity
-            yield slice(first, first + quarter), values[quarter * high : quarter * (high + 1)]
+    def joined(q, r):
+        count = half // 2 - HALF
+        parts = [first_ref[q, r, 0 : half + count, :], late_ref[q, r, 0:HALF, :]]
+        parts += [first_ref[q, r, half + half // 2 : half + half // 2 + count, :], late_ref[q, r, HALF:, :]]
+        return jnp.concatenate(parts, axis=0)
 
     def filter_step(q, carry):
         at = pl.multiple_of(q * 2 * HALF, 2 * HALF)
-        total = [None, None]
         for r in range(2):
-            for first, ref, tail in ((0, even_ref, even_tail), (1, odd_ref, odd_tail)):
-                last = own_ref[q, r, pl.ds(2 * main + first, edge, stride=2), :]
-                after = halo_ref[r, pl.ds(at + first, 2 * edge, stride=2), :]
-                ref[r, 0:main, :] = own_ref[q, r, pl.ds(first, main, stride=2), :]
-                ref[r, main : main + edge, :] = last
-                ref[r, main + edge : main + 2 * edge, :] = after[:edge] * inside
-                ref[r, tail : tail + edge, :] = last * inside
-                ref[r, tail + edge : tail + 3 * edge, :] = after
-            even_ref[r, main + 2 * edge : even_tail, :] = zeros
-            even_ref[r, even_tail + 3 * edge :, :] = zeros
-            pair_ref[r, 0:odd_tail, :] = odd_ref[r, 0:odd_tail, :] + even_ref[r, 1 : odd_tail + 1, :]
-            pair_ref[r, odd_tail:, :] = odd_ref[r, odd_tail:, :] + even_ref[r, even_tail + 1 : even_tail + 3 * edge + 1, :]
-            result = ([], [])
-            for rows, even, odd in ((main, 0, 0), (edge, even_tail, odd_tail)):
-                evens = jnp.zeros((rows + 8, 128), F32)
-                odds = jnp.zeros((rows, 128), F32)
-                pairs = jnp.zeros((rows, 128), F32)
-                for u in range(HALF + 1):
-                    evens = evens + taps_ref[q, 2 * u : 2 * u + 1, :] * even_ref[r, even + u : even + u + rows + 8, :]
-                part_ref[r, 0 : rows + 8, :] = evens
-                for u in range(HALF):
-                    odds = odds + taps_ref[q, 2 * u + 1 : 2 * u + 2, :] * odd_ref[r, odd + u : odd + u + rows, :]
-                for u in range(HALF + 1):
-                    pairs = pairs + both_ref[q, u : u + 1, :] * pair_ref[r, odd + u : odd + u + rows, :]
-                result[0].append(evens[:rows] + odds)
-                result[1].append(pairs - (part_ref[r, 1 : rows + 1, :] + odds))
-            result = [jnp.concatenate(parts, axis=0) for parts in result]
-            for n in range(2):
-                for rows, values in placed(result[n], n):
-                    filtered_ref[q, r, rows, :] = values
-                square = result[n] * result[n]
-                total[n] = square if r == 0 else total[n] + square
-        for n in range(2):
-            for rows, values in placed(total[n], n):
-                power_ref[q + 1, rows, :] = power_ref[q, rows, :] + values
+            for parity, ref, pitch in ((0, even_ref, 4 * edge), (1, odd_ref, 3 * edge)):
+                last = own_ref[q, r, pl.ds(2 * main + parity, 2 * edge, stride=2), :]
+                after = halo_ref[r, pl.ds(at + parity, 2 * edge, stride=2), :]
+                ref[r, 0 : 2 * edge, :] = last
+                ref[r, 2 * edge : 3 * edge, :] = after[:edge] * inside
+                ref[r, pitch : pitch + edge, :] = last[edge:] * inside
+                ref[r, pitch + edge : pitch + 3 * edge, :] = after
+            for line in range(2):
+                even, odd = 4 * edge * line, 3 * edge * line
+                even_ref[r, even + 3 * edge : even + 4 * edge, :] = zeros
+                pair_ref[r, odd : odd + 3 * edge, :] = (
+                    odd_ref[r, odd : odd + 3 * edge, :] + even_ref[r, even + 1 : even + 3 * edge + 1, :]
+                )
+            for line in range(2):
+                result = short_filters(
+                    taps_ref, both_ref, q, even_ref, odd_ref, pair_ref, part_ref, r, 4 * edge * line, 3 * edge * line, edge
+                )
+                for parity in range(2):
+                    row = HALF * parity + edge * line
+                    late_ref[q, r, row : row + edge, :] = result[parity]
+        real, imaginary = joined(q, 0), joined(q, 1)
+        power_ref[q + 1] = power_ref[q] + (real * real + imaginary * imaginary)
         return carry
 
     lax.fori_loop(0, RADIX, filter_step, 0)
@@ -293,7 +311,7 @@
             + shifted(power_ref[q + 1], reach)
         )
         scale = lax.rsqrt(window * small_ref[2 * RADIX + q : 2 * RADIX + q + 1, 0:128] + EPSILON)
-        fr, fi = filtered_ref[q, 0], filtered_ref[q, 1]
+        fr, fi = joined(q, 0), joined(q, 1)
         c, s = by_row(0, q), by_row(1, q)
         wr = (fr * c + fi * s) * scale
         wi = (fi * c - fr * s) * scale
@@ -459,9 +477,10 @@
     x = samples.reshape(width, length)
     after = lax.ppermute(x[: 2 * HALF], AXES, [((i + 1) % devices, i) for i in range(devices)])
 
-    own, taps, both, small, table = pl.pallas_call(
+    own, ready, taps, both, small, table = pl.pallas_call(
         own_kernel,
         out_shape=(
+            pltpu.VMEM((RADIX, 2, width, lanes), F32),
             pltpu.VMEM((RADIX, 2, width, lanes), F32),
             pltpu.VMEM((RADIX, 2 * HALF + 1, lanes), F32),
             pltpu.VMEM((RADIX, HALF + 1, lanes), F32),
@@ -469,13 +488,17 @@
             pltpu.VMEM(table.shape, BF16),
         ),
         in_specs=[far()] * 4,
-        out_specs=(vmem(),) * 5,
+        out_specs=(vmem(),) * 6,
         scratch_shapes=[
             pltpu.VMEM((width, length), BF16),
             pltpu.VMEM(fan_taps.shape, F32),
             pltpu.VMEM((RADIX * chunk, 4 * inner), BF16),
             pltpu.VMEM((RADIX * chunk, 4 * inner), BF16),
             pltpu.VMEM((bin_count + lanes, 128), F32),
+            pltpu.VMEM((2, width // 2 + 8, lanes), F32),
+            pltpu.VMEM((2, width // 2, lanes), F32),
+            pltpu.VMEM((2, width // 2, lanes), F32),
+            pltpu.VMEM((2, width // 2, lanes), F32),
             pltpu.SemaphoreType.DMA((width // chunk + 3,)),
         ],
         compiler_params=params(),
@@ -485,23 +508,23 @@
     rows = pl.pallas_call(
         functools.partial(whiten_kernel, length),
         out_shape=pltpu.VMEM((2 * bin_count, width), BF16),
-        in_specs=[vmem()] * 7,
+        in_specs=[vmem()] * 8,
         out_specs=vmem(),
         scratch_shapes=[
             pltpu.VMEM((RADIX * 2 * HALF, 4 * inner), BF16),
             pltpu.VMEM((2, RADIX * 2 * HALF, lanes), F32),
-            pltpu.VMEM((2, width // 2 + 3 * HALF, lanes), F32),
-            pltpu.VMEM((2, width // 2 + 2 * HALF, lanes), F32),
-            pltpu.VMEM((2, width // 2 + 2 * HALF, lanes), F32),
-            pltpu.VMEM((2, width // 2 + 8, lanes), F32),
-            pltpu.VMEM((RADIX, 2, width, lanes), F32),
+            pltpu.VMEM((2, 4 * HALF, lanes), F32),
+            pltpu.VMEM((2, 3 * HALF, lanes), F32),
+            pltpu.VMEM((2, 3 * HALF, lanes), F32),
+            pltpu.VMEM((2, HALF, lanes), F32),
+            pltpu.VMEM((RADIX, 2, 2 * HALF, lanes), F32),
             pltpu.VMEM((RADIX + 1, width, lanes), F32),
             pltpu.VMEM((width, lanes), F32),
             pltpu.VMEM((2 * bin_count + lanes, width), F32),
         ],
         compiler_params=params(),
         name="whiten",
-    )(near(coil_offsets.reshape(1, -1)), near(own), near(after), near(small), near(table), near(taps), near(both))
+    )(near(coil_offsets.reshape(1, -1)), near(own), near(ready), near(after), near(small), near(table), near(taps), near(both))
 
     band = lax.all_to_all(
         rows.reshape(devices, 2 * bins_device, width), AXES, split_axis=0, concat_axis=0, tiled=True

time: 85.4 us -> 82.5 us (0.966)
  blocking collectives: 59.4 us -> 56.3 us
    pallas_call x1, Pallas kernels: 4.51 us -> 7.61 us  [body(): pl.pallas_call(own_kernel, out_shape=(pltpu.VMEM((RADIX, 2, width, lanes)...]
    all_to_all x1, blocking collectives: 32.6 us -> 29.5 us  [body(): lax.all_to_all(rows.reshape(devices, 2 * bins_device, width), AXES, split...]
    pallas_call x1, Pallas kernels: 7.16 us -> 4.18 us  [body(): pl.pallas_call(functools.partial(whiten_kernel, length), out_shape=pltpu....]
  transfers between devices with their start and end apart: 2 -> 2, of which waited for: 1 -> 1; matrix products, arithmetic and copies ran while one was open for 0% -> 0% of each run, Pallas kernels for 8% -> 12%
where the time goes in v7:
time: 82.5 us; the launch traced here: 82.2 us
  blocking collectives  56.3 us (68%)
  Pallas kernels  17.8 us (22%)
  starting transfers between devices  6.43 us (8%)
  local copies, waits for them, and re-layouts  1 us (1%)
    all_to_all x1, blocking collectives, body(): lax.all_to_all(rows.reshape(devices, 2 * bins_device, width), AXES, split...  29.5 us
    all_to_all x1, blocking collectives, body(): owned = lax.all_to_all(parts, AXES, split_axis=0, concat_axis=0, tiled=True)  26.8 us
    pallas_call x1, Pallas kernels, body(): pl.pallas_call(own_kernel, out_shape=(pltpu.VMEM((RADIX, 2, width, lanes)...  7.61 us
    ppermute x1, starting transfers between devices, body(): lax.ppermute(x[:2 * HALF], AXES, [((i + 1) % devices, i) for i in range(d...  6.42 us
    pallas_call x2, Pallas kernels, products(): pl.pallas_call(functools.partial(pair_kernel, slots, mine), out_shape=plt...  4.24 us
    pallas_call x1, Pallas kernels, body(): pl.pallas_call(functools.partial(whiten_kernel, length), out_shape=pltpu....  4.18 us
    pallas_call x1, Pallas kernels, body(): pl.pallas_call(functools.partial(lag_kernel, slots, float(1.0 / np.sqrt(b...  1.78 us
  transfers between devices with their start and end apart: 2, of which 1 were waited for; matrix products, arithmetic and copies ran while one was open for 0% of the time, Pallas kernels for 12%

profile of v7, /device:TPU:0, one launch (start us, length us, event | category | flops | bytes accessed | tf_op | source)
XLA Modules:
  0.0 82.2 jit_solution(5860619868065766020)
XLA Ops:
  0.0 0.0 copy-start.3
  0.0 1.0 %slice_bitcast_fusion = bf16[32,4096]{1,0:T(8,128)(2,1)S(1)} fusion(bf16[128,1,4096]{2,0,1:T(8,128)(2,1)} %param.9), kind=kLoop, calls=%fused_computation | loop fusion | bytes 524288 | tf_op jit(solution)/shard_map/slice | solution.py:478
  1.0 6.4 %collective-permute-start = (bf16[32,4096]{1,0:T(8,128)(2,1)S(1)}, bf16[32,4096]{1,0:T(8,128)(2,1)S(1)}, u32[]{:S(2)}, u32[]{:S(2)}) collective-permute-start(bf16[32,4096]{1,0:T(8,128)(2,1)S(1)} %slice_bitcast_fusion), channel_id=1, source_target_pairs={{1,0},{2,1},{3,2},{4,3},{5,4},{6,5},{7,6},{8,7},{9,8},{10,9},{11,1... | collective-permute-start | bytes 786440 | tf_op jit(solution)/shard_map/ppermute | solution.py:478
  7.4 7.6 %own_spectra.1 = (f32[16,2,128,128]{3,2,1,0:T(8,128)S(1)}, f32[16,2,128,128]{3,2,1,0:T(8,128)S(1)}, f32[16,33,128]{2,1,0:T(8,128)S(1)}, f32[16,17,128]{2,1,0:T(8...) custom-call(bf16[128,4096]{1,0:T(8,128)(2,1)} %bitcast.10, f32[33,2048]{1,0:T(8,128)} %taps_hbm.1, ...), custom_call_target="tpu_custom_call" | custom-call | tf_op jit(solution)/shard_map/own_spectra/pallas_call | solution.py:480
  15.0 0.0 collective-permute-done.next_ref
  15.0 0.0 copy-done.3
  15.0 4.2 %whiten.1 = bf16[4096,128]{1,0:T(8,128)(2,1)S(1)} custom-call(s32[1,32]{1,0:T(1,128)S(1)} %bitcast.9, f32[16,2,128,128]{3,2,1,0:T(8,128)S(1)} %get-tuple-element.11.own_ref, f32[16,2,128,128]{3,2,1,0:T(8,128)S(1)} %get-tuple-element.12.first_ref, bf16[32,4096]{1,0:T(8,128)(2,1)S(1)} %collective-permute-done.next_ref, ...), custom_call_target="tpu_custom_call" | custom-call | tf_op jit(solution)/shard_map/whiten/pallas_call | solution.py:508
  19.2 0.0 copy-start.1
  19.3 29.5 %all_to_all.10.band_ref = bf16[32,128,128]{2,1,0:T(8,128)(2,1)S(1)} all-to-all(bf16[32,128,128]{2,1,0:T(8,128)(2,1)S(1)} %bitcast.7), channel_id=1, replica_groups=mesh['group'=4,'shard'=8] {'group','shard'}, dimensions={0} | all-to-all | bytes 2097152 | tf_op jit(solution)/shard_map/all_to_all | solution.py:529
  48.8 0.0 collective-permute-start.1
  48.8 0.0 copy-done.1
  48.8 2.1 %pairs_own_part.1.refs_0_ = f32[32,112,128]{2,1,0:T(8,128)S(1)} custom-call(s32[2,128]{1,0:T(2,128)} %bitcast.11, bf16[32,128,128]{2,1,0:T(8,128)(2,1)S(1)} %all_to_all.10.band_ref, bf16[2,56,128]{2,1,0:T(8,128)(2,1)S(1)} %copy-done.1), custom_call_target="tpu_custom_call" | custom-call | tf_op jit(solution)/shard_map/pairs_own_part/pallas_call | solution.py:539
  50.8 0.0 copy-start
  50.9 0.0 copy-start.2
  50.9 0.6 collective-permute-done.1.band_ref
  51.4 2.2 %pairs_other_part.1 = bf16[32,112,128]{2,1,0:T(8,128)(2,1)S(1)} custom-call(s32[2,128]{1,0:T(2,128)} %bitcast.12, bf16[32,128,128]{2,1,0:T(8,128)(2,1)S(1)} %collective-permute-done.1.band_ref, bf16[2,56,128]{2,1,0:T(8,128)(2,1)S(1)} %copy-done.1, f32[32,112,128]{2,1,0:T(8,128)S(1)} %pairs_own_part.1.refs_0_), custom_call_target="tpu_custom_call" | custom-call | tf_op jit(solution)/shard_map/pairs_other_part/pallas_call | solution.py:539
  53.6 26.8 %all_to_all.11.parts_ref = bf16[32,112,128]{2,1,0:T(8,128)(2,1)S(1)} all-to-all(bf16[32,112,128]{2,1,0:T(8,128)(2,1)S(1)} %pairs_other_part.1), channel_id=1, replica_groups=mesh['group'=4,'shard'=8] {'group','shard'}, dimensions={0} | all-to-all | bytes 1835008 | tf_op jit(solution)/shard_map/all_to_all | solution.py:559
  80.4 0.0 copy-done
  80.4 0.0 copy-done.2
  80.4 1.8 %lags.1 = f32[4,128,512]{2,1,0:T(8,128)} custom-call(s32[1,4]{1,0:T(1,128)S(1)} %bitcast.8, bf16[32,112,128]{2,1,0:T(8,128)(2,1)S(1)} %all_to_all.11.parts_ref, bf16[512,896]{1,0:T(8,128)(2,1)S(1)} %copy-done), custom_call_target="tpu_custom_call" | custom-call | tf_op jit(solution)/shard_map/lags/pallas_call | solution.py:561
Async XLA Ops:
  0.0 15.0 %copy-start.3 = (s32[32]{0:T(128)S(1)}, s32[32]{0:T(128)}, u32[]{:S(2)}) copy-start(s32[32]{0:T(128)} %param.13) | copy-start | bytes 388
  1.0 14.0 %collective-permute-start = (bf16[32,4096]{1,0:T(8,128)(2,1)S(1)}, bf16[32,4096]{1,0:T(8,128)(2,1)S(1)}, u32[]{:S(2)}, u32[]{:S(2)}) collective-permute-start(bf16[32,4096]{1,0:T(8,128)(2,1)S(1)} %slice_bitcast_fusion), channel_id=1, source_target_pairs={{1,0},{2,1},{3,2},{4,3},{5,4},{6,5},{7,6},{8,7},{9,8},{10,9},{11,1... | collective-permute-start | bytes 786440 | tf_op jit(solution)/shard_map/ppermute | solution.py:478
  19.2 29.5 %copy-start.1 = (bf16[2,56,128]{2,1,0:T(8,128)(2,1)S(1)}, bf16[2,56,128]{2,1,0:T(8,128)(2,1)}, u32[]{:S(2)}) copy-start(bf16[2,56,128]{2,1,0:T(8,128)(2,1)} %constant.10.clone.basis_ref) | copy-start | bytes 86020
  48.8 2.7 %collective-permute-start.1 = (bf16[32,128,128]{2,1,0:T(8,128)(2,1)S(1)}, bf16[32,128,128]{2,1,0:T(8,128)(2,1)S(1)}, u32[]{:S(2)}, u32[]{:S(2)}) collective-permute-start(bf16[32,128,128]{2,1,0:T(8,128)(2,1)S(1)} %all_to_all.10.band_ref), channel_id=1, source_target_pairs={{0,1},{1,0},{2,3},{3,2},{4,5},{5,4},{6,7},{7,6},{8,9},{9,8},{10,11... | collective-permute-start | bytes 3145736 | tf_op jit(solution)/shard_map/ppermute | solution.py:532
  50.8 29.6 %copy-start = (bf16[512,896]{1,0:T(8,128)(2,1)S(1)}, bf16[512,896]{1,0:T(8,128)(2,1)}, u32[]{:S(2)}) copy-start(bf16[512,896]{1,0:T(8,128)(2,1)} %constant.11.clone.table_ref) | copy-start | bytes 2752516
  50.9 29.6 %copy-start.2 = (s32[4]{0:T(128)S(1)}, s32[4]{0:T(128)}, u32[]{:S(2)}) copy-start(s32[4]{0:T(128)} %param.12) | copy-start | bytes 52

commit v8 on v7

--- a/solution.py
+++ b/solution.py
@@ -150,25 +150,33 @@
     return evens[:rows] + odds, pairs - (part_ref[r, 1 : rows + 1, :] + odds)
 
 
+def head_kernel(x_hbm, taps_hbm, small_hbm, head_ref, taps_ref, small_ref, sem_ref):
+    sources = (x_hbm.at[pl.ds(0, head_ref.shape[0])], taps_hbm, small_hbm)
+    targets = (head_ref, taps_ref, small_ref)
+    copies = [pltpu.make_async_copy(sources[i], targets[i], sem_ref.at[i]) for i in range(3)]
+    for copy in copies:
+        copy.start()
+    for copy in copies:
+        copy.wait()
+
+
 def own_kernel(
-    x_hbm, taps_hbm, small_hbm, table_hbm, out_ref, first_ref, split_ref, both_ref, small_ref, table_ref,
-    x_ref, taps_ref, z0_ref, z1_ref, turned_ref, even_ref, odd_ref, pair_ref, part_ref, sem_ref,
+    x_hbm, taps_ref, small_ref, table_hbm, out_ref, first_ref, split_ref, both_ref, table_ref,
+    x_ref, z0_ref, z1_ref, turned_ref, even_ref, odd_ref, pair_ref, part_ref, sem_ref,
 ):
     chunk = z0_ref.shape[0] // RADIX
     steps = x_ref.shape[0] // chunk
     slots = (z0_ref, z1_ref)
-    copies = [pltpu.make_async_copy(taps_hbm, taps_ref, sem_ref.at[0])]
-    copies.append(pltpu.make_async_copy(small_hbm, small_ref, sem_ref.at[1]))
+    copies = []
     for i in range(steps):
         rows = pl.ds(i * chunk, chunk)
-        copies.append(pltpu.make_async_copy(x_hbm.at[rows], x_ref.at[rows], sem_ref.at[3 + i]))
-    table_copy = pltpu.make_async_copy(table_hbm, table_ref, sem_ref.at[2])
+        copies.append(pltpu.make_async_copy(x_hbm.at[rows], x_ref.at[rows], sem_ref.at[i]))
+    table_copy = pltpu.make_async_copy(table_hbm, table_ref, sem_ref.at[steps])
     for i, copy in enumerate(copies):
         copy.start()
-        if i == 2:
+        if i == 0:
             table_copy.start()
 
-    copies[0].wait()
     count = taps_ref.shape[0]
     pitch = RADIX + 1
     for at in range(0, taps_ref.shape[1], 128):
@@ -184,14 +192,12 @@
         both_ref[q, 0:HALF, :] = even + odd
         both_ref[q, HALF : HALF + 1, :] = taps[count - 1 :]
 
-    copies[1].wait()
-
-    copies[2].wait()
+    copies[0].wait()
     transform_rows(x_ref, 0, chunk, small_ref, z0_ref)
     table_copy.wait()
     for i in range(steps):
         if i + 1 < steps:
-            copies[3 + i].wait()
+            copies[1 + i].wait()
             transform_rows(x_ref, (i + 1) * chunk, chunk, small_ref, slots[(i + 1) % 2])
         values = transform_inner(slots[i % 2][...], table_ref)
         for q in range(RADIX):
@@ -244,34 +250,42 @@
         parts += [first_ref[q, r, half + half // 2 : half + half // 2 + count, :], late_ref[q, r, HALF:, :]]
         return jnp.concatenate(parts, axis=0)
 
-    def filter_step(q, carry):
+    def filter_step(q, n):
         at = pl.multiple_of(q * 2 * HALF, 2 * HALF)
         for r in range(2):
+            b = 2 * n + r
             for parity, ref, pitch in ((0, even_ref, 4 * edge), (1, odd_ref, 3 * edge)):
                 last = own_ref[q, r, pl.ds(2 * main + parity, 2 * edge, stride=2), :]
                 after = halo_ref[r, pl.ds(at + parity, 2 * edge, stride=2), :]
-                ref[r, 0 : 2 * edge, :] = last
-                ref[r, 2 * edge : 3 * edge, :] = after[:edge] * inside
-                ref[r, pitch : pitch + edge, :] = last[edge:] * inside
-                ref[r, pitch + edge : pitch + 3 * edge, :] = after
+                ref[b, 0 : 2 * edge, :] = last
+                ref[b, 2 * edge : 3 * edge, :] = after[:edge] * inside
+                ref[b, pitch : pitch + edge, :] = last[edge:] * inside
+                ref[b, pitch + edge : pitch + 3 * edge, :] = after
             for line in range(2):
                 even, odd = 4 * edge * line, 3 * edge * line
-                even_ref[r, even + 3 * edge : even + 4 * edge, :] = zeros
-                pair_ref[r, odd : odd + 3 * edge, :] = (
-                    odd_ref[r, odd : odd + 3 * edge, :] + even_ref[r, even + 1 : even + 3 * edge + 1, :]
+                even_ref[b, even + 3 * edge : even + 4 * edge, :] = zeros
+                pair_ref[b, odd : odd + 3 * edge, :] = (
+                    odd_ref[b, odd : odd + 3 * edge, :] + even_ref[b, even + 1 : even + 3 * edge + 1, :]
                 )
             for line in range(2):
                 result = short_filters(
-                    taps_ref, both_ref, q, even_ref, odd_ref, pair_ref, part_ref, r, 4 * edge * line, 3 * edge * line, edge
+                    taps_ref, both_ref, q, even_ref, odd_ref, pair_ref, part_ref, b, 4 * edge * line, 3 * edge * line, edge
                 )
                 for parity in range(2):
                     row = HALF * parity + edge * line
                     late_ref[q, r, row : row + edge, :] = result[parity]
-        real, imaginary = joined(q, 0), joined(q, 1)
-        power_ref[q + 1] = power_ref[q] + (real * real + imaginary * imaginary)
+
+    def filter_steps(i, carry):
+        for n in range(together):
+            filter_step(together * i + n, n)
+        for n in range(together):
+            q = together * i + n
+            real, imaginary = joined(q, 0), joined(q, 1)
+            power_ref[q + 1] = power_ref[q] + (real * real + imaginary * imaginary)
         return carry
 
-    lax.fori_loop(0, RADIX, filter_step, 0)
+    together = 4
+    lax.fori_loop(0, RADIX // together, filter_steps, 0)
 
     reach = SMOOTH // RADIX
     lane = lax.broadcasted_iota(jnp.int32, (1, 128), 1)
@@ -475,23 +489,35 @@
     small[2 * RADIX :, :lanes] = (1.0 / counts).reshape(lanes, RADIX).T
 
     x = samples.reshape(width, length)
-    after = lax.ppermute(x[: 2 * HALF], AXES, [((i + 1) % devices, i) for i in range(devices)])
-
-    own, ready, taps, both, small, table = pl.pallas_call(
+    x, fan_taps, small = distant(x), distant(fan_taps), distant(jnp.asarray(small))
+    head, fan_taps, small = pl.pallas_call(
+        head_kernel,
+        out_shape=(
+            pltpu.VMEM((2 * HALF, length), BF16),
+            pltpu.VMEM(fan_taps.shape, F32),
+            pltpu.VMEM(small.shape, F32),
+        ),
+        in_specs=[far()] * 3,
+        out_specs=(vmem(),) * 3,
+        scratch_shapes=[pltpu.SemaphoreType.DMA((3,))],
+        compiler_params=params(),
+        name="head",
+    )(x, fan_taps, small)
+    after = lax.ppermute(head, AXES, [((i + 1) % devices, i) for i in range(devices)])
+
+    own, ready, taps, both, table = pl.pallas_call(
         own_kernel,
         out_shape=(
             pltpu.VMEM((RADIX, 2, width, lanes), F32),
             pltpu.VMEM((RADIX, 2, width, lanes), F32),
             pltpu.VMEM((RADIX, 2 * HALF + 1, lanes), F32),
             pltpu.VMEM((RADIX, HALF + 1, lanes), F32),
-            pltpu.VMEM(small.shape, F32),
             pltpu.VMEM(table.shape, BF16),
         ),
-        in_specs=[far()] * 4,
-        out_specs=(vmem(),) * 6,
+        in_specs=[far(), vmem(), vmem(), far()],
+        out_specs=(vmem(),) * 5,
         scratch_shapes=[
             pltpu.VMEM((width, length), BF16),
-            pltpu.VMEM(fan_taps.shape, F32),
             pltpu.VMEM((RADIX * chunk, 4 * inner), BF16),
             pltpu.VMEM((RADIX * chunk, 4 * inner), BF16),
             pltpu.VMEM((bin_count + lanes, 128), F32),
@@ -499,11 +525,11 @@
             pltpu.VMEM((2, width // 2, lanes), F32),
             pltpu.VMEM((2, width // 2, lanes), F32),
             pltpu.VMEM((2, width // 2, lanes), F32),
-            pltpu.SemaphoreType.DMA((width // chunk + 3,)),
+            pltpu.SemaphoreType.DMA((width // chunk + 1,)),
         ],
         compiler_params=params(),
         name="own_spectra",
-    )(distant(x), distant(fan_taps), distant(jnp.asarray(small)), distant(jnp.asarray(table)))
+    )(x, near(fan_taps), near(small), distant(jnp.asarray(table)))
 
     rows = pl.pallas_call(
         functools.partial(whiten_kernel, length),
@@ -513,10 +539,10 @@
         scratch_shapes=[
             pltpu.VMEM((RADIX * 2 * HALF, 4 * inner), BF16),
             pltpu.VMEM((2, RADIX * 2 * HALF, lanes), F32),
-            pltpu.VMEM((2, 4 * HALF, lanes), F32),
-            pltpu.VMEM((2, 3 * HALF, lanes), F32),
-            pltpu.VMEM((2, 3 * HALF, lanes), F32),
-            pltpu.VMEM((2, HALF, lanes), F32),
+            pltpu.VMEM((8, 4 * HALF, lanes), F32),
+            pltpu.VMEM((8, 3 * HALF, lanes), F32),
+            pltpu.VMEM((8, 3 * HALF, lanes), F32),
+            pltpu.VMEM((8, HALF, lanes), F32),
             pltpu.VMEM((RADIX, 2, 2 * HALF, lanes), F32),
             pltpu.VMEM((RADIX + 1, width, lanes), F32),
             pltpu.VMEM((width, lanes), F32),

time: 82.5 us -> 82.3 us (level)
  local copies, waits for them, and re-layouts: 1 us -> 0.02 us
    pallas_call x0 -> x1, Pallas kernels: none -> 1.09 us  [body(): pl.pallas_call(head_kernel, out_shape=(pltpu.VMEM((2 * HALF, length), BF1...]
    slice x1 -> x0, local copies, waits for them, and re-layouts: 0.98 us -> none  [body(): x[:2 * HALF]]
  transfers between devices with their start and end apart: 2 -> 2, of which waited for: 1 -> 1; matrix products, arithmetic and copies ran while one was open for 0% -> 0% of each run, Pallas kernels for 12% -> 11%
where the time goes in v8:
time: 82.3 us; the launch traced here: 82.1 us
  blocking collectives  56.9 us (69%)
  Pallas kernels  18.1 us (22%)
  starting transfers between devices  6.43 us (8%)
    all_to_all x1, blocking collectives, body(): lax.all_to_all(rows.reshape(devices, 2 * bins_device, width), AXES, split...  30.1 us
    all_to_all x1, blocking collectives, body(): owned = lax.all_to_all(parts, AXES, split_axis=0, concat_axis=0, tiled=True)  26.8 us
    pallas_call x1, Pallas kernels, body(): pl.pallas_call(own_kernel, out_shape=(pltpu.VMEM((RADIX, 2, width, lanes)...  7.01 us
    ppermute x1, starting transfers between devices, body(): lax.ppermute(head, AXES, [((i + 1) % devices, i) for i in range(devices)])  6.42 us
    pallas_call x2, Pallas kernels, products(): pl.pallas_call(functools.partial(pair_kernel, slots, mine), out_shape=plt...  4.24 us
    pallas_call x1, Pallas kernels, body(): pl.pallas_call(functools.partial(whiten_kernel, length), out_shape=pltpu....  3.93 us
    pallas_call x1, Pallas kernels, body(): pl.pallas_call(functools.partial(lag_kernel, slots, float(1.0 / np.sqrt(b...  1.78 us
  transfers between devices with their start and end apart: 2, of which 1 were waited for; matrix products, arithmetic and copies ran while one was open for 0% of the time, Pallas kernels for 11%

profile of v8, /device:TPU:0, one launch (start us, length us, event | category | flops | bytes accessed | tf_op | source)
XLA Modules:
  0.0 82.1 jit_solution(6214131888378064001)
XLA Ops:
  0.0 0.0 copy-start.3
  0.0 1.1 %head.1 = (bf16[32,4096]{1,0:T(8,128)(2,1)S(1)}, f32[33,2048]{1,0:T(8,128)S(1)}, f32[48,256]{1,0:T(8,128)S(1)}) custom-call(bf16[128,4096]{1,0:T(8,128)(2,1)} %bitcast.8, f32[33,2048]{1,0:T(8,128)} %taps_hbm.1, f32[48,256]{1,0:T(8,128)} %constant.8.clone.small_hbm), custom_call_target="tpu_custom_call" | custom-call | tf_op jit(solution)/shard_map/head/pallas_call | solution.py:493
  1.1 6.4 %collective-permute-start = (bf16[32,4096]{1,0:T(8,128)(2,1)S(1)}, bf16[32,4096]{1,0:T(8,128)(2,1)S(1)}, u32[]{:S(2)}, u32[]{:S(2)}) collective-permute-start(bf16[32,4096]{1,0:T(8,128)(2,1)S(1)} %get-tuple-element.17), channel_id=1, source_target_pairs={{1,0},{2,1},{3,2},{4,3},{5,4},{6,5},{7,6},{8,7},{9,8},{10,9},{11,1... | collective-permute-start | bytes 786440 | tf_op jit(solution)/shard_map/ppermute | solution.py:506
  7.5 7.0 %own_spectra.1 = (f32[16,2,128,128]{3,2,1,0:T(8,128)S(1)}, f32[16,2,128,128]{3,2,1,0:T(8,128)S(1)}, f32[16,33,128]{2,1,0:T(8,128)S(1)}, f32[16,17,128]{2,1,0:T(8,128)S(1)}, bf16[1024,256]{1,0:T(8,128)(2,1)S(1)}) custom-call(bf16[128,4096]{1,0:T(8,128)(2,1)} %bitcast.9, f32[33,2048]{1,0:T(8,128)S(1)} %get-tuple-element.13.taps_ref, ...), custom_call_target="tpu_custom_call" | custom-call | tf_op jit(solution)/shard_map/own_spectra/pallas_call | solution.py:508
  14.5 0.0 collective-permute-done.next_ref
  14.6 0.0 copy-done.3
  14.6 3.9 %whiten.1 = bf16[4096,128]{1,0:T(8,128)(2,1)S(1)} custom-call(s32[1,32]{1,0:T(1,128)S(1)} %bitcast.7, f32[16,2,128,128]{3,2,1,0:T(8,128)S(1)} %get-tuple-element.15.own_ref, f32[16,2,128,128]{3,2,1,0:T(8,128)S(1)} %get-tuple-element.16.first_ref, bf16[32,4096]{1,0:T(8,128)(2,1)S(1)} %collective-permute-done.next_ref, ...), custom_call_target="tpu_custom_call" | custom-call | tf_op jit(solution)/shard_map/whiten/pallas_call | solution.py:534
  18.5 0.0 copy-start.1
  18.5 30.1 %all_to_all.10.band_ref = bf16[32,128,128]{2,1,0:T(8,128)(2,1)S(1)} all-to-all(bf16[32,128,128]{2,1,0:T(8,128)(2,1)S(1)} %bitcast.5), channel_id=1, replica_groups=mesh['group'=4,'shard'=8] {'group','shard'}, dimensions={0} | all-to-all | bytes 2097152 | tf_op jit(solution)/shard_map/all_to_all | solution.py:555
  48.6 0.0 collective-permute-start.1
  48.6 0.0 copy-done.1
  48.6 2.1 %pairs_own_part.1.refs_0_ = f32[32,112,128]{2,1,0:T(8,128)S(1)} custom-call(s32[2,128]{1,0:T(2,128)} %bitcast.10, bf16[32,128,128]{2,1,0:T(8,128)(2,1)S(1)} %all_to_all.10.band_ref, bf16[2,56,128]{2,1,0:T(8,128)(2,1)S(1)} %copy-done.1), custom_call_target="tpu_custom_call" | custom-call | tf_op jit(solution)/shard_map/pairs_own_part/pallas_call | solution.py:565
  50.7 0.0 copy-start
  50.7 0.0 copy-start.2
  50.7 0.6 collective-permute-done.1.band_ref
  51.3 2.2 %pairs_other_part.1 = bf16[32,112,128]{2,1,0:T(8,128)(2,1)S(1)} custom-call(s32[2,128]{1,0:T(2,128)} %bitcast.11, bf16[32,128,128]{2,1,0:T(8,128)(2,1)S(1)} %collective-permute-done.1.band_ref, bf16[2,56,128]{2,1,0:T(8,128)(2,1)S(1)} %copy-done.1, f32[32,112,128]{2,1,0:T(8,128)S(1)} %pairs_own_part.1.refs_0_), custom_call_target="tpu_custom_call" | custom-call | tf_op jit(solution)/shard_map/pairs_other_part/pallas_call | solution.py:565
  53.5 26.8 %all_to_all.11.parts_ref = bf16[32,112,128]{2,1,0:T(8,128)(2,1)S(1)} all-to-all(bf16[32,112,128]{2,1,0:T(8,128)(2,1)S(1)} %pairs_other_part.1), channel_id=1, replica_groups=mesh['group'=4,'shard'=8] {'group','shard'}, dimensions={0} | all-to-all | bytes 1835008 | tf_op jit(solution)/shard_map/all_to_all | solution.py:585
  80.3 0.0 copy-done
  80.3 0.0 copy-done.2
  80.3 1.8 %lags.1 = f32[4,128,512]{2,1,0:T(8,128)} custom-call(s32[1,4]{1,0:T(1,128)S(1)} %bitcast.6, bf16[32,112,128]{2,1,0:T(8,128)(2,1)S(1)} %all_to_all.11.parts_ref, bf16[512,896]{1,0:T(8,128)(2,1)S(1)} %copy-done), custom_call_target="tpu_custom_call" | custom-call | tf_op jit(solution)/shard_map/lags/pallas_call | solution.py:587
Async XLA Ops:
  0.0 14.6 %copy-start.3 = (s32[32]{0:T(128)S(1)}, s32[32]{0:T(128)}, u32[]{:S(2)}) copy-start(s32[32]{0:T(128)} %param.13) | copy-start | bytes 388
  1.1 13.4 %collective-permute-start = (bf16[32,4096]{1,0:T(8,128)(2,1)S(1)}, bf16[32,4096]{1,0:T(8,128)(2,1)S(1)}, u32[]{:S(2)}, u32[]{:S(2)}) collective-permute-start(bf16[32,4096]{1,0:T(8,128)(2,1)S(1)} %get-tuple-element.17), channel_id=1, source_target_pairs={{1,0},{2,1},{3,2},{4,3},{5,4},{6,5},{7,6},{8,7},{9,8},{10,9},{11,1... | collective-permute-start | bytes 786440 | tf_op jit(solution)/shard_map/ppermute | solution.py:506
  18.5 30.1 %copy-start.1 = (bf16[2,56,128]{2,1,0:T(8,128)(2,1)S(1)}, bf16[2,56,128]{2,1,0:T(8,128)(2,1)}, u32[]{:S(2)}) copy-start(bf16[2,56,128]{2,1,0:T(8,128)(2,1)} %constant.10.clone.basis_ref) | copy-start | bytes 86020
  48.6 2.7 %collective-permute-start.1 = (bf16[32,128,128]{2,1,0:T(8,128)(2,1)S(1)}, bf16[32,128,128]{2,1,0:T(8,128)(2,1)S(1)}, u32[]{:S(2)}, u32[]{:S(2)}) collective-permute-start(bf16[32,128,128]{2,1,0:T(8,128)(2,1)S(1)} %all_to_all.10.band_ref), channel_id=1, source_target_pairs={{0,1},{1,0},{2,3},{3,2},{4,5},{5,4},{6,7},{7,6},{8,9},{9,8},{10,11... | collective-permute-start | bytes 3145736 | tf_op jit(solution)/shard_map/ppermute | solution.py:558
  50.7 29.6 %copy-start = (bf16[512,896]{1,0:T(8,128)(2,1)S(1)}, bf16[512,896]{1,0:T(8,128)(2,1)}, u32[]{:S(2)}) copy-start(bf16[512,896]{1,0:T(8,128)(2,1)} %constant.11.clone.table_ref) | copy-start | bytes 2752516
  50.7 29.6 %copy-start.2 = (s32[4]{0:T(128)S(1)}, s32[4]{0:T(128)}, u32[]{:S(2)}) copy-start(s32[4]{0:T(128)} %param.12) | copy-start | bytes 52

commit v9 on v8

--- a/solution.py
+++ b/solution.py
@@ -150,23 +150,23 @@
     return evens[:rows] + odds, pairs - (part_ref[r, 1 : rows + 1, :] + odds)
 
 
-def head_kernel(x_hbm, taps_hbm, small_hbm, head_ref, taps_ref, small_ref, sem_ref):
-    sources = (x_hbm.at[pl.ds(0, head_ref.shape[0])], taps_hbm, small_hbm)
-    targets = (head_ref, taps_ref, small_ref)
-    copies = [pltpu.make_async_copy(sources[i], targets[i], sem_ref.at[i]) for i in range(3)]
-    for copy in copies:
-        copy.start()
-    for copy in copies:
-        copy.wait()
+def head_kernel(x_hbm, head_ref, sem_ref):
+    copy = pltpu.make_async_copy(x_hbm.at[pl.ds(0, head_ref.shape[0])], head_ref, sem_ref.at[0])
+    copy.start()
+    copy.wait()
 
 
 def own_kernel(
-    x_hbm, taps_ref, small_ref, table_hbm, out_ref, first_ref, split_ref, both_ref, table_ref,
-    x_ref, z0_ref, z1_ref, turned_ref, even_ref, odd_ref, pair_ref, part_ref, sem_ref,
+    x_hbm, taps_hbm, small_hbm, table_hbm, out_ref, first_ref, split_ref, both_ref, small_ref, table_ref,
+    x_ref, taps_ref, z0_ref, z1_ref, turned_ref, even_ref, odd_ref, pair_ref, part_ref, sem_ref,
 ):
     chunk = z0_ref.shape[0] // RADIX
     steps = x_ref.shape[0] // chunk
     slots = (z0_ref, z1_ref)
+    taps_copy = pltpu.make_async_copy(taps_hbm, taps_ref, sem_ref.at[steps + 1])
+    small_copy = pltpu.make_async_copy(small_hbm, small_ref, sem_ref.at[steps + 2])
+    taps_copy.start()
+    small_copy.start()
     copies = []
     for i in range(steps):
         rows = pl.ds(i * chunk, chunk)
@@ -177,6 +177,7 @@
         if i == 0:
             table_copy.start()
 
+    taps_copy.wait()
     count = taps_ref.shape[0]
     pitch = RADIX + 1
     for at in range(0, taps_ref.shape[1], 128):
@@ -192,6 +193,7 @@
         both_ref[q, 0:HALF, :] = even + odd
         both_ref[q, HALF : HALF + 1, :] = taps[count - 1 :]
 
+    small_copy.wait()
     copies[0].wait()
     transform_rows(x_ref, 0, chunk, small_ref, z0_ref)
     table_copy.wait()
@@ -490,34 +492,32 @@
 
     x = samples.reshape(width, length)
     x, fan_taps, small = distant(x), distant(fan_taps), distant(jnp.asarray(small))
-    head, fan_taps, small = pl.pallas_call(
+    head = pl.pallas_call(
         head_kernel,
-        out_shape=(
-            pltpu.VMEM((2 * HALF, length), BF16),
-            pltpu.VMEM(fan_taps.shape, F32),
-            pltpu.VMEM(small.shape, F32),
-        ),
-        in_specs=[far()] * 3,
-        out_specs=(vmem(),) * 3,
-        scratch_shapes=[pltpu.SemaphoreType.DMA((3,))],
+        out_shape=pltpu.VMEM((2 * HALF, length), BF16),
+        in_specs=[far()],
+        out_specs=vmem(),
+        scratch_shapes=[pltpu.SemaphoreType.DMA((1,))],
         compiler_params=params(),
         name="head",
-    )(x, fan_taps, small)
+    )(x)
     after = lax.ppermute(head, AXES, [((i + 1) % devices, i) for i in range(devices)])
 
-    own, ready, taps, both, table = pl.pallas_call(
+    own, ready, taps, both, small, table = pl.pallas_call(
         own_kernel,
         out_shape=(
             pltpu.VMEM((RADIX, 2, width, lanes), F32),
             pltpu.VMEM((RADIX, 2, width, lanes), F32),
             pltpu.VMEM((RADIX, 2 * HALF + 1, lanes), F32),
             pltpu.VMEM((RADIX, HALF + 1, lanes), F32),
+            pltpu.VMEM(small.shape, F32),
             pltpu.VMEM(table.shape, BF16),
         ),
-        in_specs=[far(), vmem(), vmem(), far()],
-        out_specs=(vmem(),) * 5,
+        in_specs=[far()] * 4,
+        out_specs=(vmem(),) * 6,
         scratch_shapes=[
             pltpu.VMEM((width, length), BF16),
+            pltpu.VMEM(fan_taps.shape, F32),
             pltpu.VMEM((RADIX * chunk, 4 * inner), BF16),
             pltpu.VMEM((RADIX * chunk, 4 * inner), BF16),
             pltpu.VMEM((bin_count + lanes, 128), F32),
@@ -525,11 +525,11 @@
             pltpu.VMEM((2, width // 2, lanes), F32),
             pltpu.VMEM((2, width // 2, lanes), F32),
             pltpu.VMEM((2, width // 2, lanes), F32),
-            pltpu.SemaphoreType.DMA((width // chunk + 1,)),
+            pltpu.SemaphoreType.DMA((width // chunk + 3,)),
         ],
         compiler_params=params(),
         name="own_spectra",
-    )(x, near(fan_taps), near(small), distant(jnp.asarray(table)))
+    )(x, fan_taps, small, distant(jnp.asarray(table)))
 
     rows = pl.pallas_call(
         functools.partial(whiten_kernel, length),

time: 82.3 us -> 82.2 us (level)
  transfers between devices with their start and end apart: 2 -> 2, of which waited for: 1 -> 1; matrix products, arithmetic and copies ran while one was open for 0% -> 0% of each run, Pallas kernels for 11% -> 12%
where the time goes in v9:
time: 82.2 us; the launch traced here: 81.9 us
  blocking collectives  56.3 us (68%)
  Pallas kernels  18.5 us (23%)
  starting transfers between devices  6.43 us (8%)
    all_to_all x1, blocking collectives, body(): lax.all_to_all(rows.reshape(devices, 2 * bins_device, width), AXES, split...  29.5 us
    all_to_all x1, blocking collectives, body(): owned = lax.all_to_all(parts, AXES, split_axis=0, concat_axis=0, tiled=True)  26.8 us
    pallas_call x1, Pallas kernels, body(): pl.pallas_call(own_kernel, out_shape=(pltpu.VMEM((RADIX, 2, width, lanes)...  7.61 us
    ppermute x1, starting transfers between devices, body(): lax.ppermute(head, AXES, [((i + 1) % devices, i) for i in range(devices)])  6.42 us
    pallas_call x2, Pallas kernels, products(): pl.pallas_call(functools.partial(pair_kernel, slots, mine), out_shape=plt...  4.24 us
    pallas_call x1, Pallas kernels, body(): pl.pallas_call(functools.partial(whiten_kernel, length), out_shape=pltpu....  3.9 us
    pallas_call x1, Pallas kernels, body(): pl.pallas_call(functools.partial(lag_kernel, slots, float(1.0 / np.sqrt(b...  1.78 us
  transfers between devices with their start and end apart: 2, of which 1 were waited for; matrix products, arithmetic and copies ran while one was open for 0% of the time, Pallas kernels for 12%

profile of v9, /device:TPU:0, one launch (start us, length us, event | category | flops | bytes accessed | tf_op | source)
XLA Modules:
  0.0 81.9 jit_solution(5124725789874688719)
XLA Ops:
  0.0 0.0 copy-start.3
  0.0 1.0 %head.1 = bf16[32,4096]{1,0:T(8,128)(2,1)S(1)} custom-call(bf16[128,4096]{1,0:T(8,128)(2,1)} %bitcast.8), custom_call_target="tpu_custom_call" | custom-call | tf_op jit(solution)/shard_map/head/pallas_call | solution.py:495
  1.0 6.4 %collective-permute-start = (bf16[32,4096]{1,0:T(8,128)(2,1)S(1)}, bf16[32,4096]{1,0:T(8,128)(2,1)S(1)}, u32[]{:S(2)}, u32[]{:S(2)}) collective-permute-start(bf16[32,4096]{1,0:T(8,128)(2,1)S(1)} %head.1), channel_id=1, source_target_pairs={{1,0},{2,1},{3,2},{4,3},{5,4},{6,5},{7,6},{8,7},{9,8},{10,9},{11,1... | collective-permute-start | bytes 786440 | tf_op jit(solution)/shard_map/ppermute | solution.py:504
  7.4 7.6 %own_spectra.1 = (f32[16,2,128,128]{3,2,1,0:T(8,128)S(1)}, f32[16,2,128,128]{3,2,1,0:T(8,128)S(1)}, f32[16,33,128]{2,1,0:T(8,128)S(1)}, f32[16,17,128]{2,1,0:T(8...) custom-call(bf16[128,4096]{1,0:T(8,128)(2,1)} %bitcast.9, f32[33,2048]{1,0:T(8,128)} %taps_hbm.1, ...), custom_call_target="tpu_custom_call" | custom-call | tf_op jit(solution)/shard_map/own_spectra/pallas_call | solution.py:506
  15.0 0.0 collective-permute-done.next_ref
  15.0 0.0 copy-done.3
  15.0 3.9 %whiten.1 = bf16[4096,128]{1,0:T(8,128)(2,1)S(1)} custom-call(s32[1,32]{1,0:T(1,128)S(1)} %bitcast.7, f32[16,2,128,128]{3,2,1,0:T(8,128)S(1)} %get-tuple-element.11.own_ref, f32[16,2,128,128]{3,2,1,0:T(8,128)S(1)} %get-tuple-element.12.first_ref, bf16[32,4096]{1,0:T(8,128)(2,1)S(1)} %collective-permute-done.next_ref, ...), custom_call_target="tpu_custom_call" | custom-call | tf_op jit(solution)/shard_map/whiten/pallas_call | solution.py:534
  19.0 0.0 copy-start.1
  19.0 29.5 %all_to_all.10.band_ref = bf16[32,128,128]{2,1,0:T(8,128)(2,1)S(1)} all-to-all(bf16[32,128,128]{2,1,0:T(8,128)(2,1)S(1)} %bitcast.5), channel_id=1, replica_groups=mesh['group'=4,'shard'=8] {'group','shard'}, dimensions={0} | all-to-all | bytes 2097152 | tf_op jit(solution)/shard_map/all_to_all | solution.py:555
  48.5 0.0 collective-permute-start.1
  48.5 0.0 copy-done.1
  48.5 2.1 %pairs_own_part.1.refs_0_ = f32[32,112,128]{2,1,0:T(8,128)S(1)} custom-call(s32[2,128]{1,0:T(2,128)} %bitcast.10, bf16[32,128,128]{2,1,0:T(8,128)(2,1)S(1)} %all_to_all.10.band_ref, bf16[2,56,128]{2,1,0:T(8,128)(2,1)S(1)} %copy-done.1), custom_call_target="tpu_custom_call" | custom-call | tf_op jit(solution)/shard_map/pairs_own_part/pallas_call | solution.py:565
  50.6 0.0 copy-start
  50.6 0.0 copy-start.2
  50.6 0.6 collective-permute-done.1.band_ref
  51.1 2.2 %pairs_other_part.1 = bf16[32,112,128]{2,1,0:T(8,128)(2,1)S(1)} custom-call(s32[2,128]{1,0:T(2,128)} %bitcast.11, bf16[32,128,128]{2,1,0:T(8,128)(2,1)S(1)} %collective-permute-done.1.band_ref, bf16[2,56,128]{2,1,0:T(8,128)(2,1)S(1)} %copy-done.1, f32[32,112,128]{2,1,0:T(8,128)S(1)} %pairs_own_part.1.refs_0_), custom_call_target="tpu_custom_call" | custom-call | tf_op jit(solution)/shard_map/pairs_other_part/pallas_call | solution.py:565
  53.3 26.8 %all_to_all.11.parts_ref = bf16[32,112,128]{2,1,0:T(8,128)(2,1)S(1)} all-to-all(bf16[32,112,128]{2,1,0:T(8,128)(2,1)S(1)} %pairs_other_part.1), channel_id=1, replica_groups=mesh['group'=4,'shard'=8] {'group','shard'}, dimensions={0} | all-to-all | bytes 1835008 | tf_op jit(solution)/shard_map/all_to_all | solution.py:585
  80.1 0.0 copy-done
  80.1 0.0 copy-done.2
  80.1 1.8 %lags.1 = f32[4,128,512]{2,1,0:T(8,128)} custom-call(s32[1,4]{1,0:T(1,128)S(1)} %bitcast.6, bf16[32,112,128]{2,1,0:T(8,128)(2,1)S(1)} %all_to_all.11.parts_ref, bf16[512,896]{1,0:T(8,128)(2,1)S(1)} %copy-done), custom_call_target="tpu_custom_call" | custom-call | tf_op jit(solution)/shard_map/lags/pallas_call | solution.py:587
Async XLA Ops:
  0.0 15.0 %copy-start.3 = (s32[32]{0:T(128)S(1)}, s32[32]{0:T(128)}, u32[]{:S(2)}) copy-start(s32[32]{0:T(128)} %param.13) | copy-start | bytes 388
  1.0 14.0 %collective-permute-start = (bf16[32,4096]{1,0:T(8,128)(2,1)S(1)}, bf16[32,4096]{1,0:T(8,128)(2,1)S(1)}, u32[]{:S(2)}, u32[]{:S(2)}) collective-permute-start(bf16[32,4096]{1,0:T(8,128)(2,1)S(1)} %head.1), channel_id=1, source_target_pairs={{1,0},{2,1},{3,2},{4,3},{5,4},{6,5},{7,6},{8,7},{9,8},{10,9},{11,1... | collective-permute-start | bytes 786440 | tf_op jit(solution)/shard_map/ppermute | solution.py:504
  19.0 29.5 %copy-start.1 = (bf16[2,56,128]{2,1,0:T(8,128)(2,1)S(1)}, bf16[2,56,128]{2,1,0:T(8,128)(2,1)}, u32[]{:S(2)}) copy-start(bf16[2,56,128]{2,1,0:T(8,128)(2,1)} %constant.10.clone.basis_ref) | copy-start | bytes 86020
  48.5 2.7 %collective-permute-start.1 = (bf16[32,128,128]{2,1,0:T(8,128)(2,1)S(1)}, bf16[32,128,128]{2,1,0:T(8,128)(2,1)S(1)}, u32[]{:S(2)}, u32[]{:S(2)}) collective-permute-start(bf16[32,128,128]{2,1,0:T(8,128)(2,1)S(1)} %all_to_all.10.band_ref), channel_id=1, source_target_pairs={{0,1},{1,0},{2,3},{3,2},{4,5},{5,4},{6,7},{7,6},{8,9},{9,8},{10,11... | collective-permute-start | bytes 3145736 | tf_op jit(solution)/shard_map/ppermute | solution.py:558
  50.6 29.6 %copy-start = (bf16[512,896]{1,0:T(8,128)(2,1)S(1)}, bf16[512,896]{1,0:T(8,128)(2,1)}, u32[]{:S(2)}) copy-start(bf16[512,896]{1,0:T(8,128)(2,1)} %constant.11.clone.table_ref) | copy-start | bytes 2752516
  50.6 29.6 %copy-start.2 = (s32[4]{0:T(128)S(1)}, s32[4]{0:T(128)}, u32[]{:S(2)}) copy-start(s32[4]{0:T(128)} %param.12) | copy-start | bytes 52
